TPU v7x, 32 devices: a whole 2x2x4 slice. The times are simulated.
32 devices in a mesh: fsdp: 4 (over y, x), expert: 4 (over z), tensor: 2 (over core).
Axes of the slice: x: 2, y: 2, z: 4, core: 2. Of those that a mesh axis runs over, the one named last changes fastest.
Arguments:
- tokens: bfloat16 [2, 256, 4096], P(None, 'expert'), may hold values from -6 to 6
- route: int32 [2, 256, 2], P(None, 'expert'), may hold values from 0 to 7, all different within a row; in each aligned block of 64 rows (0 to 63, 64 to 127, ..., all dimensions but the last counted through in order) at most 32 rows name the same one
- route_weight: float32 [2, 256, 2], P(None, 'expert'), may hold values from 0.1 to 1
- gate_up: bfloat16 [8, 2, 4096, 8192], P('expert', None, None, ('fsdp', 'tensor')), may hold values from -0.09375 to 0.09375
- down_weight: bfloat16 [8, 8192, 4096], P('expert', ('fsdp', 'tensor')), may hold values from -0.09375 to 0.09375
- adam_first: float32 [8, 2048, 4096], P(None, ('fsdp', 'tensor'), 'expert'), may hold values from -2.5 to 2.5
- adam_second: float32 [8, 2048, 4096], P(None, ('fsdp', 'tensor'), 'expert'), may hold values from 0.05 to 1
- gradient: bfloat16 [8, 2048, 4096], P(None, ('fsdp', 'tensor'), 'expert'), may hold values from -6 to 6
- block_list: int32 [8, 8, 4], P(None, ('fsdp', 'tensor')), may hold values from 0 to 31, as said below
- block_count: int32 [8, 8], P(None, ('fsdp', 'tensor')), may hold values from 1 to 4, as said below
Outputs:
- mixed: bfloat16 [2, 256, 4096], P(None, 'expert', ('fsdp', 'tensor'))
- first_new: float32 [8, 2048, 4096], P(None, ('fsdp', 'tensor'), 'expert')
- second_new: float32 [8, 2048, 4096], P(None, ('fsdp', 'tensor'), 'expert')
Inputs may be any that keep to these rules, and one draw needn't show every extreme that they name: `route`: the two experts of a token differ; in each aligned block of 64 tokens of one step no expert is named more than 32 times. `block_list`: the 4 entries of one list are distinct block numbers; only the first block_count entries are applied. `block_count`: 4 is reached in every draw.
All inputs are finite; a program needn't handle non-finite values.
Results may differ from a plain program's by a relative error of at most 0.023.
Values may be sent and summed in bfloat16 or wider, within the bound.
No kernel may reach another device: no remote copies, remote signals or barrier semaphores. Data moves between devices by JAX's collectives and lax.ppermute only.
A program may use at most 192 MiB of HBM per device.

v0:
```python
import jax
import jax.numpy as jnp
from jax import lax
from jax.sharding import PartitionSpec as P

E = 8
STRIDE = 4
BLOCK_ROWS = 8
MAXCH = 4
S = 2
CAP = 32


BETA_ONE = 0.9
BETA_TWO = 0.95
LEARN_RATE = 0.03
ADAM_EPS = 1e-08
FIRST_FIX = 1.0 - 0.9**10
SECOND_FIX = 1.0 - 0.95**10


def adam_moments(adam_first, adam_second, gradient):
    grad_wide = gradient.astype(jnp.float32)
    first_new = BETA_ONE * adam_first + (1.0 - BETA_ONE) * grad_wide
    second_new = BETA_TWO * adam_second + (1.0 - BETA_TWO) * grad_wide * grad_wide
    step_size = (
        LEARN_RATE * (first_new / FIRST_FIX) / (jnp.sqrt(second_new / SECOND_FIX) + ADAM_EPS)
    )
    return (first_new, second_new, (-step_size).astype(jnp.bfloat16))


def on_device(
    tokens,
    route,
    route_weight,
    gate_up,
    down_weight,
    adam_first,
    adam_second,
    gradient,
    block_list,
    block_count,
):
    first_new, second_new, delta = adam_moments(adam_first, adam_second, gradient)
    groups = lax.axis_size("expert")
    owned_experts = gate_up.shape[0]
    shard_rows = delta.shape[1]
    block_total = shard_rows // BLOCK_ROWS
    width = down_weight.shape[2]
    expert_start = lax.axis_index("expert") * owned_experts
    own_list = lax.dynamic_slice_in_dim(block_list[:, 0, :], expert_start, owned_experts, 0)
    own_count = lax.dynamic_slice_in_dim(block_count[:, 0], expert_start, owned_experts, 0)
    listed = jnp.arange(MAXCH)[None, :] < own_count[:, None]
    picked = (own_list[:, :, None] == jnp.arange(block_total)[None, None, :]) & listed[:, :, None]
    row_mask = jnp.repeat(jnp.any(picked, axis=1), BLOCK_ROWS, axis=1)
    incoming = lax.all_to_all(delta, "expert", split_axis=0, concat_axis=2, tiled=True)
    strided = down_weight.reshape(owned_experts, shard_rows, STRIDE, width)
    fresh_rows = (
        strided[:, :, 0, :].astype(jnp.float32)
        + jnp.where(row_mask[:, :, None], incoming.astype(jnp.float32), 0.0)
    ).astype(jnp.bfloat16)
    down_new = jnp.concatenate([fresh_rows[:, :, None, :], strided[:, :, 1:, :]], axis=2).reshape(
        owned_experts, shard_rows * STRIDE, width
    )
    slots_all = CAP * E
    shards = lax.axis_size(("fsdp", "tensor"))
    group_index = lax.axis_index(("fsdp", "tensor"))
    my_rows = slots_all // shards
    token_count = tokens.shape[1]
    outputs = []
    for decode_step in range(S):
        token_rows = tokens[decode_step]
        pair_expert = route[decode_step].reshape(-1)
        onehot = (pair_expert[:, None] == jnp.arange(E)[None, :]).astype(jnp.int32)
        position = jnp.sum((jnp.cumsum(onehot, axis=0) - onehot) * onehot, axis=1)
        slot_index = position * E + pair_expert
        placed = (slot_index[:, None] == jnp.arange(slots_all)[None, :]).reshape(
            token_count, 2, slots_all
        )
        selector = jnp.sum(placed.astype(jnp.int32), axis=1).astype(jnp.bfloat16)
        gathered = lax.dot_general(
            selector, token_rows, (((0,), (0,)), ((), ())), preferred_element_type=jnp.float32
        )
        outgoing = gathered.astype(jnp.bfloat16).reshape(CAP, E, 1, width)
        received = lax.all_to_all(outgoing, "expert", split_axis=1, concat_axis=2, tiled=True)
        flat_rows = received.reshape(slots_all, width)
        weights = route_weight[decode_step].reshape(-1)
        slot_block = flat_rows.reshape(slots_all // E, owned_experts, groups, width)
        projected = jnp.einsum(
            "cxed,xgdh->cxegh", slot_block, gate_up, preferred_element_type=jnp.float32
        )
        hidden = (jax.nn.silu(projected[:, :, :, 0, :]) * projected[:, :, :, 1, :]).astype(
            jnp.bfloat16
        )
        down_term = jnp.einsum(
            "cxeh,xhd->cxed", hidden, down_new, preferred_element_type=jnp.float32
        )
        rounded = lax.optimization_barrier(down_term.astype(jnp.bfloat16))
        summed_all = lax.psum(
            rounded.astype(jnp.float32).reshape(slots_all, width).astype(jnp.bfloat16),
            ("fsdp", "tensor"),
        ).astype(jnp.float32)
        own_rows = lax.dynamic_slice_in_dim(summed_all, group_index * my_rows, my_rows, 0)
        returned = lax.all_to_all(
            own_rows.reshape(my_rows // E, owned_experts, groups, width).astype(jnp.bfloat16),
            "expert",
            split_axis=2,
            concat_axis=1,
            tiled=True,
        ).astype(jnp.float32)
        back_rows = returned.reshape(my_rows, width)
        local_slot = slot_index - group_index * my_rows
        matches = (local_slot[:, None] == jnp.arange(my_rows)[None, :]).astype(
            jnp.float32
        ) * weights[:, None]
        mixing = jnp.sum(matches.reshape(token_count, 2, my_rows), axis=1)
        token_part = jnp.dot(
            mixing, back_rows, precision=lax.Precision.HIGHEST, preferred_element_type=jnp.float32
        )
        summed = lax.psum_scatter(
            token_part.astype(jnp.bfloat16), ("fsdp", "tensor"), scatter_dimension=1, tiled=True
        )
        outputs.append(summed)
    return (jnp.stack(outputs), first_new, second_new)


def solution(mesh):
    return jax.shard_map(
        on_device,
        mesh=mesh,
        in_specs=(
            P(None, "expert", None),
            P(None, "expert", None),
            P(None, "expert", None),
            P("expert", None, None, ("fsdp", "tensor")),
            P("expert", ("fsdp", "tensor"), None),
            P(None, ("fsdp", "tensor"), "expert"),
            P(None, ("fsdp", "tensor"), "expert"),
            P(None, ("fsdp", "tensor"), "expert"),
            P(None, ("fsdp", "tensor"), None),
            P(None, ("fsdp", "tensor")),
        ),
        out_specs=(
            P(None, "expert", ("fsdp", "tensor")),
            P(None, ("fsdp", "tensor"), "expert"),
            P(None, ("fsdp", "tensor"), "expert"),
        ),
        check_vma=False,
    )
```

profile of v0, /device:TPU:0, one launch (start us, length us, event | category | flops | bytes accessed | tf_op | source)
XLA Modules:
  0.0 507.8 jit_solution(17644777390238776356)
XLA Ops:
  14.9 6.3 %all-to-all-start.1 = ((bf16[32,8,1,4096]{3,0,2,1:T(8,128)(2,1)}), bf16[32,8,1,4096]{3,0,2,1:T(8,128)(2,1)S(1)}, u32[]{:S(2)}, u32[]{:S(2)}) async-start(bf16[32,8,1,4096]{3,0,2,1:T(8,128)(2,1)} %copy.87), calls=%async_computation.1 | async-start | bytes 4194304 | tf_op jit(solution)/shard_map/all_to_all | solution.py:85
  24.4 45.0 %all-to-all-done.1 = bf16[32,8,1,4096]{3,0,2,1:T(8,128)(2,1)S(1)} async-done(((bf16[32,8,1,4096]{3,0,2,1:T(8,128)(2,1)}), bf16[32,8,1,4096]{3,0,2,1:T(8,128)(2,1)S(1)}, u32[]{:S(2)}, u32[]{:S(2)}) %all-to-all-start.1) | async-done | bytes 2097184 | tf_op jit(solution)/shard_map/all_to_all | solution.py:85
  73.9 15.1 %negate_convert_fusion = (bf16[8,256,1024]{2,1,0:T(8,128)(2,1)}, f32[8,256,1024]{2,1,0:T(8,128)}, f32[8,256,1024]{2,1,0:T(8,128)}) fusion(bf16[8,256,1024]{2,1,0:T(8,128)(2,1)} %param.17, f32[8,256,1024]{2,1,0:T(8,128)} %param.15, f32[8,256,1024]{2,1,0:T(8,128)} %param.16), kind=kLoop, calls=%fused_computation.18 | loop fusion | flops 29360128 | bytes 41943040 | tf_op jit(solution)/shard_map/convert_element_type | solution.py:29
  89.0 32.6 %all-to-all-done.3 = bf16[32,8,1,4096]{3,0,2,1:T(8,128)(2,1)} async-done(((bf16[32,8,1,4096]{3,0,2,1:T(8,128)(2,1)}), bf16[32,8,1,4096]{3,0,2,1:T(8,128)(2,1)}, u32[]{:S(2)}, u32[]{:S(2)}) %all-to-all-start.3) | async-done | bytes 2097184 | tf_op jit(solution)/shard_map/all_to_all | solution.py:85
  121.6 4.8 all-to-all-start
  127.3 24.9 %reshape.165 = bf16[2,256,4,4096]{3,2,1,0:T(4,128)(2,1)} reshape(bf16[2,1024,4096]{2,1,0:T(8,128)(2,1)} %param.14) | data formatting | bytes 33554432 | tf_op jit(solution)/shard_map/reshape | solution.py:57
  152.2 15.5 %slice.49 = bf16[2,256,3,4096]{3,2,1,0:T(4,128)(2,1)} slice(bf16[2,256,4,4096]{3,2,1,0:T(4,128)(2,1)} %reshape.165), slice={[0:2], [0:256], [1:4], [0:4096]} | slice | bytes 25165824 | tf_op jit(solution)/shard_map/slice | solution.py:62
  167.7 15.0 %fusion.30 = f32[32,2,4,2,1024]{4,0,2,1,3:T(8,128)} fusion(bf16[32,4,2,1,4096]{4,0,2,1,3:T(8,128)(2,1)} %bitcast.27, bf16[2,2,4096,1024]{3,2,1,0:T(8,128)(2,1)} %param.13), kind=kOutput, calls=%fused_computation.33 | convolution fusion | flops 4294967296 | bytes 37748736 | tf_op jit(solution)/shard_map/cxed,xgdh->cxegh/dot_general | solution.py:89
  182.7 13.5 %fusion.35 = f32[32,2,4,2,1024]{4,0,3,2,1:T(8,128)S(1)} fusion(bf16[2,2,4096,1024]{3,2,1,0:T(8,128)(2,1)} %param.13, bf16[32,4,2,1,4096]{4,0,2,1,3:T(8,128)(2,1)} %bitcast.122), kind=kOutput, calls=%fused_computation.34 | convolution fusion | flops 4294967296 | bytes 37748736 | tf_op jit(solution)/shard_map/cxed,xgdh->cxegh/dot_general | solution.py:89
  196.2 23.0 %all-to-all-done = bf16[8,256,1024]{2,1,0:T(8,128)(2,1)} async-done(((bf16[8,256,1024]{2,1,0:T(8,128)(2,1)}), bf16[8,256,1024]{2,1,0:T(8,128)(2,1)}, u32[]{:S(2)}, u32[]{:S(2)}) %all-to-all-start) | async-done | bytes 4194336 | tf_op jit(solution)/shard_map/all_to_all | solution.py:56
  219.2 6.4 %convert_bitcast_fusion = f32[2,256,4,1024]{3,1,0,2:T(8,128)} fusion(bf16[4,2,256,1024]{3,2,1,0:T(8,128)(2,1)} %bitcast.38), kind=kLoop, calls=%fused_computation.17 | loop fusion | flops 2097152 | bytes 12582912 | tf_op jit(solution)/shard_map/convert_element_type | solution.py:60
  225.6 12.0 %copy.86 = f32[2,256,4,1024]{3,2,1,0:T(4,128)} copy(f32[2,256,4,1024]{3,1,0,2:T(8,128)} %convert_bitcast_fusion) | data formatting | bytes 16777216 | tf_op jit(solution)/shard_map/convert_element_type | solution.py:60
  237.6 14.3 %reshape.171 = f32[2,256,1,4096]{3,2,1,0:T(1,128)} reshape(f32[2,256,4,1024]{3,2,1,0:T(4,128)} %copy.86) | data formatting | bytes 16777216 | tf_op jit(solution)/shard_map/convert_element_type | solution.py:60
  251.9 14.3 %fusion.11 = bf16[2,256,1,4096]{3,2,1,0:T(2,128)(2,1)S(1)} fusion(f32[2,256,1,4096]{3,2,1,0:T(1,128)} %reshape.171, pred[2,256]{1,0:T(4,128)(4,1)S(1)} %broadcast_in_dim.17, bf16[2,256,4,4096]{3,2,1,0:T(4,128)(2,1)} %reshape.165), kind=kLoop, calls=%fused_computation.15 | loop fusion | flops 8388608 | bytes 16777728 | tf_op jit(solution)/shard_map/convert_element_type | solution.py:61
  266.2 20.0 %pad_maximum_fusion = bf16[2,256,4,4096]{3,2,1,0:T(4,128)(2,1)} fusion(bf16[2,256,3,4096]{3,2,1,0:T(4,128)(2,1)} %slice.49, bf16[2,256,1,4096]{3,2,1,0:T(2,128)(2,1)S(1)} %fusion.11), kind=kLoop, calls=%fused_computation.4 | loop fusion | flops 33554432 | bytes 33554432 | tf_op jit(solution)/shard_map/concatenate | solution.py:62
  286.2 23.7 %reshape.175 = bf16[2,1024,4096,1]{2,1,0,3:T(8,128)(2,1)} reshape(bf16[2,256,4,4096]{3,2,1,0:T(4,128)(2,1)} %pad_maximum_fusion) | data formatting | bytes 33554432 | tf_op jit(solution)/shard_map/reshape | solution.py:62
  309.9 7.1 %fusion.23 = bf16[32,2,4,4096]{3,0,2,1:T(8,128)(2,1)S(1)} fusion(bf16[2,1024,4096,1]{2,1,0,3:T(8,128)(2,1)} %reshape.175, f32[32,2,4,2,1024]{4,0,3,2,1:T(8,128)S(1)} %fusion.35), kind=kOutput, calls=%fused_computation.26 | convolution fusion | flops 2150105088 | bytes 20971520 | tf_op jit(solution)/shard_map/cxeh,xhd->cxed/dot_general | solution.py:95
  320.7 7.6 %fusion.20 = bf16[32,2,4,4096]{3,0,2,1:T(8,128)(2,1)S(1)} fusion(bf16[2,1024,4096,1]{2,1,0,3:T(8,128)(2,1)} %reshape.175, f32[32,2,4,2,1024]{4,0,2,1,3:T(8,128)} %fusion.30), kind=kOutput, calls=%fused_computation.25 | convolution fusion | flops 2150105088 | bytes 20971520 | tf_op jit(solution)/shard_map/cxeh,xhd->cxed/dot_general | solution.py:95
  332.1 80.5 %all-reduce.3.cloned.1.call-done = (bf16[256,4096]{1,0:T(8,128)(2,1)}, bf16[256,4096]{1,0:T(8,128)(2,1)}) async-done(((bf16[256,4096]{1,0:T(8,128)(2,1)}, bf16[256,4096]{1,0:T(8,128)(2,1)}), (bf16[256,4096]{1,0:T(8,128)(2,1)}, bf16[256,4096]{1,0:T(8,128)(2,1)})) %all-reduce.3.cloned.1.call-update) | async-done | bytes 4194320 | tf_op jit(solution)/shard_map/psum | solution.py:99
  414.6 4.6 all-to-all-start.2
  419.3 8.8 %all-to-all-done.2 = bf16[4,2,4,4096]{3,1,0,2:T(2,128)(2,1)S(1)} async-done(((bf16[4,2,4,4096]{3,1,0,2:T(2,128)(2,1)}), bf16[4,2,4,4096]{3,1,0,2:T(2,128)(2,1)S(1)}, u32[]{:S(2)}, u32[]{:S(2)}) %all-to-all-start.2) | async-done | bytes 262176 | tf_op jit(solution)/shard_map/all_to_all | solution.py:104
  435.4 6.9 %all-to-all-done.4 = bf16[4,2,4,4096]{3,1,0,2:T(2,128)(2,1)S(1)} async-done(((bf16[4,2,4,4096]{3,1,0,2:T(2,128)(2,1)}), bf16[4,2,4,4096]{3,1,0,2:T(2,128)(2,1)S(1)}, u32[]{:S(2)}, u32[]{:S(2)}) %all-to-all-start.4) | async-done | bytes 262176 | tf_op jit(solution)/shard_map/all_to_all | solution.py:104
  444.1 18.4 %reduce-scatter.3.cloned.1.call-done = bf16[64,512]{1,0:T(8,128)(2,1)} async-done(((bf16[64,4096]{1,0:T(8,128)(2,1)}), bf16[64,512]{1,0:T(8,128)(2,1)}) %reduce-scatter.3.cloned.1.call-update) | async-done | bytes 65552 | tf_op jit(solution)/shard_map/reduce_scatter | solution.py:120
  462.5 37.2 %reduce-scatter.5.cloned.1.call-done = bf16[64,512]{1,0:T(8,128)(2,1)} async-done(((bf16[64,4096]{1,0:T(8,128)(2,1)}), bf16[64,512]{1,0:T(8,128)(2,1)}) %reduce-scatter.5.cloned.1.call-update) | async-done | bytes 65552 | tf_op jit(solution)/shard_map/reduce_scatter | solution.py:120
  (70 shorter events, 36.2 us)
Async XLA Ops:
  7.2 119.6 %copy-start = (s32[8,1,4]{0,2,1:T(4,128)S(1)}, s32[8,1,4]{0,2,1:T(4,128)}, u32[]{:S(2)}) copy-start(s32[8,1,4]{0,2,1:T(4,128)} %param.18) | copy-start | bytes 388
  7.2 14.0 %copy-start.3 = (bf16[2,64,4096]{2,1,0:T(8,128)(2,1)S(1)}, bf16[2,64,4096]{2,1,0:T(8,128)(2,1)}, u32[]{:S(2)}) copy-start(bf16[2,64,4096]{2,1,0:T(8,128)(2,1)} %param.10) | copy-start | bytes 3145732
  14.9 54.5 %all-to-all-start.1 = ((bf16[32,8,1,4096]{3,0,2,1:T(8,128)(2,1)}), bf16[32,8,1,4096]{3,0,2,1:T(8,128)(2,1)S(1)}, u32[]{:S(2)}, u32[]{:S(2)}) async-start(bf16[32,8,1,4096]{3,0,2,1:T(8,128)(2,1)} %copy.87), calls=%async_computation.1 | async-start | bytes 4194304 | tf_op jit(solution)/shard_map/all_to_all | solution.py:85
  69.4 19.6 %copy-start.2 = (bf16[32,8,1,4096]{3,0,2,1:T(8,128)(2,1)}, bf16[32,8,1,4096]{3,0,2,1:T(8,128)(2,1)S(1)}, u32[]{:S(2)}) copy-start(bf16[32,8,1,4096]{3,0,2,1:T(8,128)(2,1)S(1)} %all-to-all-done.1) | copy-start | bytes 6291460
  69.4 52.2 %all-to-all-start.3 = ((bf16[32,8,1,4096]{3,0,2,1:T(8,128)(2,1)}), bf16[32,8,1,4096]{3,0,2,1:T(8,128)(2,1)}, u32[]{:S(2)}, u32[]{:S(2)}) async-start(bf16[32,8,1,4096]{3,0,2,1:T(8,128)(2,1)} %copy.95), calls=%async_computation.4 | async-start | bytes 4194304 | tf_op jit(solution)/shard_map/all_to_all | solution.py:85
  89.0 37.9 %copy-start.5 = (s32[8,1]{0,1:T(1,128)S(1)}, s32[8,1]{0,1:T(1,128)}, u32[]{:S(2)}) copy-start(s32[8,1]{0,1:T(1,128)} %param.19) | copy-start | bytes 100
  121.6 97.5 %all-to-all-start = ((bf16[8,256,1024]{2,1,0:T(8,128)(2,1)}), bf16[8,256,1024]{2,1,0:T(8,128)(2,1)}, u32[]{:S(2)}, u32[]{:S(2)}) async-start(bf16[8,256,1024]{2,1,0:T(8,128)(2,1)} %get-tuple-element.7), calls=%async_computation | async-start | bytes 8388608 | tf_op jit(solution)/shard_map/all_to_all | solution.py:56
  126.5 286.1 %all-reduce.3.cloned.1.call-start = ((), (), s32[]{:S(2)}) async-start(), calls=%async_computation.9 | async-start | bytes 8388608 | tf_op jit(solution)/shard_map/psum | solution.py:99
  328.3 90.9 %copy-start.4 = (f32[2,64,2]{1,2,0:T(2,128)S(1)}, f32[2,64,2]{1,2,0:T(2,128)}, u32[]{:S(2)}) copy-start(f32[2,64,2]{1,2,0:T(2,128)} %param.12) | copy-start | bytes 3076
  328.3 172.9 %copy-start.1 = (s32[8,1,4]{0,2,1:T(4,128)S(1)}, s32[8,1,4]{0,2,1:T(4,128)}, u32[]{:S(2)}) copy-start(s32[8,1,4]{0,2,1:T(4,128)} %param.18) | copy-start | bytes 388
  414.6 13.4 %all-to-all-start.2 = ((bf16[4,2,4,4096]{3,1,0,2:T(2,128)(2,1)}), bf16[4,2,4,4096]{3,1,0,2:T(2,128)(2,1)S(1)}, u32[]{:S(2)}, u32[]{:S(2)}) async-start(bf16[4,2,4,4096]{3,1,0,2:T(2,128)(2,1)} %copy.91), calls=%async_computation.2 | async-start | bytes 524288 | tf_op jit(solution)/shard_map/all_to_all | solution.py:104
  419.2 43.2 %reduce-scatter.3.cloned.1.call-start = ((), (), s32[]{:S(2)}) async-start(), calls=%async_computation.7 | async-start | bytes 589824 | tf_op jit(solution)/shard_map/reduce_scatter | solution.py:120
  431.9 10.4 %all-to-all-start.4 = ((bf16[4,2,4,4096]{3,1,0,2:T(2,128)(2,1)}), bf16[4,2,4,4096]{3,1,0,2:T(2,128)(2,1)S(1)}, u32[]{:S(2)}, u32[]{:S(2)}) async-start(bf16[4,2,4,4096]{3,1,0,2:T(2,128)(2,1)} %copy.99), calls=%async_computation.5 | async-start | bytes 524288 | tf_op jit(solution)/shard_map/all_to_all | solution.py:104
  435.3 64.4 %reduce-scatter.5.cloned.1.call-start = ((), (), s32[]{:S(2)}) async-start(), calls=%async_computation.8 | async-start | bytes 589824 | tf_op jit(solution)/shard_map/reduce_scatter | solution.py:120
Sparse Core Ops, SparseCore 0:
  332.2 80.3 all-reduce.2
  430.0 32.4 reduce-scatter.2
  465.5 34.1 reduce-scatter.4
where the time goes:
time: 510 us; the launch traced here: 508 us
  waiting for transfers between devices  252 us (49%)
  local copies, waits for them, and re-layouts  108 us (21%)
  other arithmetic  61.2 us (12%)
  matrix products  48.5 us (10%)
  starting transfers between devices  23.9 us (5%)
  between operations  14 us (3%)
    psum x1, waiting for transfers between devices, on_device(): lax.psum(rounded.astype(jnp.float32).reshape(slots_all, width).astype(jnp...  80.5 us
    all_to_all x2, waiting for transfers between devices, on_device(): lax.all_to_all(outgoing, 'expert', split_axis=1, concat_axis=2, tiled=True)  77.6 us
    reduce_scatter x2, waiting for transfers between devices, on_device(): lax.psum_scatter(token_part.astype(jnp.bfloat16), ('fsdp', 'tensor'), sca...  55.6 us
    dot_general x2, matrix products, on_device(): jnp.einsum('cxed,xgdh->cxegh', slot_block, gate_up, preferred_element_typ...  28.5 us
    convert_element_type x2, local copies, waits for them, and re-layouts, on_device(): incoming.astype(jnp.float32)  26.3 us
    reshape x1, local copies, waits for them, and re-layouts, on_device(): strided = down_weight.reshape(owned_experts, shard_rows, STRIDE, width)  24.9 us
    reshape x1, local copies, waits for them, and re-layouts, on_device(): jnp.concatenate([fresh_rows[:, :, None, :], strided[:, :, 1:, :]], axis=2)  23.7 us
    all_to_all x1, waiting for transfers between devices, on_device(): lax.all_to_all(delta, 'expert', split_axis=0, concat_axis=2, tiled=True)  23 us
  transfers between devices with their start and end apart: 8, of which 8 were waited for; matrix products, arithmetic and copies ran while one was open for 18% of the time, Pallas kernels for 0%

commit v1 on v0

v1 whole, which is shorter than its diff:
```python
import functools

import jax
import jax.numpy as jnp
from jax import lax
from jax.experimental import pallas as pl
from jax.experimental.pallas import tpu as pltpu
from jax.sharding import PartitionSpec as P

STRIDE = 4
BLOCK_ROWS = 8
MAXCH = 4
CAP = 32
HALF = 256
UNIT_TILE = 512

BETA_ONE = 0.9
BETA_TWO = 0.95
LEARN_RATE = 0.03
ADAM_EPS = 1e-08
FIRST_FIX = 1.0 - 0.9**10
SECOND_FIX = 1.0 - 0.95**10

F32 = jnp.float32
BF16 = jnp.bfloat16
SMALL_VMEM = 16 * 2**20
STAGE_VMEM = 24 * 2**20


def adam_kernel(list_ref, count_ref, first_ref, second_ref, grad_ref, first_out, second_out, delta_out):
    expert = pl.program_id(0)
    grad = grad_ref[...].astype(F32)
    first_out[...] = BETA_ONE * first_ref[...] + (1.0 - BETA_ONE) * grad
    second_out[...] = BETA_TWO * second_ref[...] + (1.0 - BETA_TWO) * grad * grad
    parts = []
    for entry in range(MAXCH):
        start = pl.multiple_of(list_ref[expert * MAXCH + entry] * BLOCK_ROWS, BLOCK_ROWS)
        first = first_out[0, pl.ds(start, BLOCK_ROWS), :]
        second = second_out[0, pl.ds(start, BLOCK_ROWS), :]
        step = LEARN_RATE * (first / FIRST_FIX) / (jnp.sqrt(second / SECOND_FIX) + ADAM_EPS)
        parts.append(jnp.where(entry < count_ref[expert], -step, 0.0))
    delta_out[0] = jnp.concatenate(parts, axis=0).astype(BF16)


def adam_update(adam_first, adam_second, gradient, block_list, block_count):
    experts, rows, cols = adam_first.shape
    block = pl.BlockSpec((1, rows, cols), lambda e, *_: (e, 0, 0))
    size = experts * rows * cols
    return pl.pallas_call(
        adam_kernel,
        grid_spec=pltpu.PrefetchScalarGridSpec(
            num_scalar_prefetch=2,
            grid=(experts,),
            in_specs=[block, block, block],
            out_specs=[block, block, pl.BlockSpec((1, MAXCH * BLOCK_ROWS, cols), lambda e, *_: (e, 0, 0))],
        ),
        out_shape=[
            jax.ShapeDtypeStruct(adam_first.shape, F32),
            jax.ShapeDtypeStruct(adam_first.shape, F32),
            jax.ShapeDtypeStruct((experts, MAXCH * BLOCK_ROWS, cols), BF16),
        ],
        compiler_params=pltpu.CompilerParams(vmem_limit_bytes=SMALL_VMEM),
        cost_estimate=pl.CostEstimate(flops=8 * size, bytes_accessed=18 * size, transcendentals=0),
        name="adam_listed",
    )(block_list, block_count, adam_first, adam_second, gradient)


def route_kernel(groups, owned, tok_block, meta_ref, *refs):
    infos = refs[:groups]
    select_ref, scatter_ref, weight_ref = refs[groups:]
    halves = scatter_ref.shape[0]
    per_half = groups // halves
    half_slots = (HALF // tok_block) * CAP
    first_expert = (meta_ref[0] * owned).astype(F32)
    row = lax.broadcasted_iota(jnp.int32, (HALF, HALF), 0)
    col = lax.broadcasted_iota(jnp.int32, (HALF, HALF), 1)
    before = ((row < col) & (row // tok_block == col // tok_block)).astype(F32).astype(BF16)
    slot = lax.broadcasted_iota(jnp.int32, (half_slots, HALF), 0)
    token = lax.broadcasted_iota(jnp.int32, (half_slots, HALF), 1)
    same_block = slot // CAP == token // tok_block
    slot_pos = (slot % CAP).astype(F32)
    for half in range(halves):
        info = jnp.concatenate([infos[k][...] for k in range(half * per_half, (half + 1) * per_half)], axis=1)
        selectors = []
        for e in range(owned):
            named = first_expert + e
            hit_a, hit_b = info[0:1] == named, info[1:2] == named
            member = jnp.where(hit_a | hit_b, 1.0, 0.0)
            weight = jnp.where(hit_a, info[2:3], 0.0) + jnp.where(hit_b, info[3:4], 0.0)
            position = jnp.dot(
                jnp.broadcast_to(member, (16, HALF)).astype(BF16), before, preferred_element_type=F32
            )[0:1]
            chosen = same_block & (position == slot_pos) & (member > 0.5)
            selectors.append(jnp.where(chosen, 1.0, 0.0))
            slot_weight = jnp.sum(jnp.where(chosen, weight, 0.0), axis=1, keepdims=True)
            weight_ref[e, half * half_slots : (half + 1) * half_slots, :] = jnp.broadcast_to(
                slot_weight, (half_slots, 128)
            )
        selector = jnp.concatenate(selectors, axis=0)
        select_ref[half] = selector.astype(BF16)
        scatter_ref[half] = jnp.transpose(selector).astype(BF16)


def route_tables(meta, infos, owned, tok_block):
    groups = len(infos)
    halves = groups * infos[0].shape[1] // HALF
    half_slots = (HALF // tok_block) * CAP
    vmem = pl.BlockSpec(memory_space=pltpu.VMEM)
    return pl.pallas_call(
        functools.partial(route_kernel, groups, owned, tok_block),
        grid_spec=pltpu.PrefetchScalarGridSpec(
            num_scalar_prefetch=1, grid=(), in_specs=[vmem] * groups, out_specs=[vmem] * 3
        ),
        out_shape=[
            jax.ShapeDtypeStruct((halves, owned * half_slots, HALF), BF16),
            jax.ShapeDtypeStruct((halves, HALF, owned * half_slots), BF16),
            jax.ShapeDtypeStruct((owned, halves * half_slots, 128), F32),
        ],
        compiler_params=pltpu.CompilerParams(vmem_limit_bytes=SMALL_VMEM),
        cost_estimate=pl.CostEstimate(flops=10**7, bytes_accessed=10**6, transcendentals=0),
        name="route_tables",
    )(meta, *infos)


def gate_up_kernel(shares, within, first, last, meta_ref, select_ref, weight_ref, tokens_ref, *refs):
    recv = [refs[i * within : (i + 1) * within] for i in range(shares)]
    refs = refs[shares * within :]
    if first:
        gate_up_ref, refs = refs[0], refs[1:]
    else:
        gate_up_ref, sums_ref, refs = refs[0], refs[1], refs[2:]
    out_ref, rows_ref, total_ref = refs
    expert, share = pl.program_id(0), pl.program_id(2)
    steps, tok_block, width = tokens_ref.shape
    cols = recv[0][0].shape[2]
    halves = select_ref.shape[0]
    per_half = HALF // (steps * tok_block)
    owned = rows_ref.shape[1]
    half_slots = select_ref.shape[1] // owned

    @pl.when((expert == 0) & (pl.program_id(1) == 0) & (share == 0))
    def _():
        for i in range(shares):
            for q in range(within):
                place = meta_ref[shares + q]
                start = (meta_ref[i] * within + place) * cols
                lanes = pl.ds(pl.multiple_of(start, cols), cols)
                into = pl.ds(pl.multiple_of(place * cols, cols), cols)
                for half in range(halves):
                    blocks = []
                    for k in range(half * per_half, (half + 1) * per_half):
                        if k == 0:
                            blocks += [tokens_ref[s, :, lanes] for s in range(steps)]
                        else:
                            blocks.append(recv[i][q][k - 1])
                    picked = jnp.dot(
                        select_ref[half], jnp.concatenate(blocks, axis=0), preferred_element_type=F32
                    ).astype(BF16)
                    for e in range(owned):
                        rows_ref[i, e, half * half_slots : (half + 1) * half_slots, into] = picked[
                            e * half_slots : (e + 1) * half_slots
                        ]

    rows = rows_ref[share, expert]
    gate = jnp.dot(rows, gate_up_ref[0, 0], preferred_element_type=F32)
    up = jnp.dot(rows, gate_up_ref[0, 1], preferred_element_type=F32)

    def finish(gate, up):
        if last:
            out_ref[0] = (gate * jax.nn.sigmoid(gate) * up * weight_ref[expert, :, 0:1]).astype(BF16)
        else:
            out_ref[0, 0], out_ref[0, 1] = gate, up

    if shares == 1:
        if not first:
            gate, up = gate + sums_ref[0, 0], up + sums_ref[0, 1]
        finish(gate, up)
    else:

        @pl.when(share == 0)
        def _():
            total_ref[0] = gate if first else gate + sums_ref[0, 0]
            total_ref[1] = up if first else up + sums_ref[0, 1]

        @pl.when((share > 0) & (share < shares - 1))
        def _():
            total_ref[0] += gate
            total_ref[1] += up

        @pl.when(share == shares - 1)
        def _():
            finish(total_ref[0] + gate, total_ref[1] + up)


def gate_up_stage(places, select, weight, tokens, received, gate_up, sums, last):
    owned, _, width, units = gate_up.shape
    shares, within = len(received), len(received[0])
    depth = within * received[0][0].shape[2]
    slots = weight.shape[1]
    tile = min(UNIT_TILE, units)
    vmem = pl.BlockSpec(memory_space=pltpu.VMEM)
    sums_spec = pl.BlockSpec((1, 2, slots, tile), lambda e, j, i, *_: (e, 0, 0, j))
    if last:
        out_spec = pl.BlockSpec((1, slots, tile), lambda e, j, i, *_: (e, 0, j))
        out_shape = jax.ShapeDtypeStruct((owned, slots, units), BF16)
    else:
        out_spec = sums_spec
        out_shape = jax.ShapeDtypeStruct((owned, 2, slots, units), F32)
    first = sums is None
    return pl.pallas_call(
        functools.partial(gate_up_kernel, shares, within, first, last),
        grid_spec=pltpu.PrefetchScalarGridSpec(
            num_scalar_prefetch=1,
            grid=(owned, units // tile, shares),
            in_specs=[vmem] * (3 + shares * within)
            + [pl.BlockSpec((1, 2, depth, tile), lambda e, j, i, meta: (e, 0, meta[i], j))]
            + ([] if first else [sums_spec]),
            out_specs=out_spec,
            scratch_shapes=[
                pltpu.VMEM((shares, owned, slots, depth), BF16),
                pltpu.VMEM((2, slots, tile), F32),
            ],
        ),
        out_shape=out_shape,
        compiler_params=pltpu.CompilerParams(vmem_limit_bytes=STAGE_VMEM),
        cost_estimate=pl.CostEstimate(
            flops=4 * owned * slots * depth * units * shares,
            bytes_accessed=4 * owned * depth * units * shares + 16 * owned * slots * units,
            transcendentals=0,
        ),
        name="gate_up_stage",
    )(places, select, weight, tokens, *sum([list(r) for r in received], []), gate_up, *([] if first else [sums]))


def down_kernel(owned, within, meta_ref, list_ref, hidden_ref, scatter_ref, delta_ref, down_ref, *refs):
    outs, (buf, sem) = refs[:within], refs[within:]
    cols = buf.shape[3]
    src_cols = delta_ref.shape[3]
    halves = scatter_ref.shape[0]
    half_slots = hidden_ref.shape[1] // halves
    order = list(range(1, within)) + [0]

    def fetch(q, e):
        lanes = pl.ds(pl.multiple_of(meta_ref[1 + q] * cols, cols), cols)
        return pltpu.make_async_copy(down_ref.at[e, :, lanes], buf.at[q, e], sem.at[q, e])

    for q in order:
        for e in range(owned):
            fetch(q, e).start()
    listed = MAXCH * BLOCK_ROWS
    span = BLOCK_ROWS * STRIDE
    row = lax.broadcasted_iota(jnp.int32, (MAXCH * span, listed), 0)
    col = lax.broadcasted_iota(jnp.int32, (MAXCH * span, listed), 1)
    spread = ((row // STRIDE == col) & (row % STRIDE == 0)).astype(F32).astype(BF16)
    for q in order:
        first_col = meta_ref[1 + q] * cols
        source = first_col // src_cols
        lanes = pl.ds(pl.multiple_of(first_col - source * src_cols, cols), cols)
        parts = []
        for e in range(owned):
            added = jnp.dot(spread, delta_ref[source, e, :, lanes], preferred_element_type=F32)
            fetch(q, e).wait()
            for entry in range(MAXCH):
                block = list_ref[(meta_ref[0] * owned + e) * MAXCH + entry]
                where = pl.ds(pl.multiple_of(block * span, span), span)
                fresh = buf[q, e, where, :].astype(F32) + added[entry * span : (entry + 1) * span]
                buf[q, e, where, :] = fresh.astype(BF16)
            parts.append(jnp.dot(hidden_ref[e], buf[q, e], preferred_element_type=F32).astype(BF16))
        for half in range(halves):
            mine = jnp.concatenate([p[half * half_slots : (half + 1) * half_slots] for p in parts], axis=0)
            outs[q][half * HALF : (half + 1) * HALF, :] = jnp.dot(
                scatter_ref[half], mine, preferred_element_type=F32
            ).astype(BF16)


def down_pieces(meta, block_list, hidden, scatter, delta, down_weight, cols):
    owned, units, _ = down_weight.shape
    within = meta.shape[0] - 1
    rows = scatter.shape[0] * HALF
    slots = hidden.shape[1]
    vmem = pl.BlockSpec(memory_space=pltpu.VMEM)
    return pl.pallas_call(
        functools.partial(down_kernel, owned, within),
        grid_spec=pltpu.PrefetchScalarGridSpec(
            num_scalar_prefetch=2,
            grid=(),
            in_specs=[vmem, vmem, vmem, pl.BlockSpec(memory_space=pl.ANY)],
            out_specs=[vmem] * within,
            scratch_shapes=[
                pltpu.VMEM((within, owned, units, cols), BF16),
                pltpu.SemaphoreType.DMA((within, owned)),
            ],
        ),
        out_shape=[jax.ShapeDtypeStruct((rows, cols), BF16)] * within,
        compiler_params=pltpu.CompilerParams(vmem_limit_bytes=STAGE_VMEM),
        cost_estimate=pl.CostEstimate(
            flops=2 * owned * slots * units * cols * within,
            bytes_accessed=2 * owned * units * cols * within,
            transcendentals=0,
        ),
        name="down_mixed",
    )(meta, block_list, hidden, scatter, delta, down_weight)


def swap(value, axis, distance):
    return lax.ppermute(value, axis, [(i, i ^ distance) for i in range(lax.axis_size(axis))])


def shift(value, axis, distance):
    size = lax.axis_size(axis)
    return lax.ppermute(value, axis, [(i, (i + distance) % size) for i in range(size)])


def on_device(
    tokens,
    route,
    route_weight,
    gate_up,
    down_weight,
    adam_first,
    adam_second,
    gradient,
    block_list,
    block_count,
):
    groups = lax.axis_size("expert")
    across, within = lax.axis_size("fsdp"), lax.axis_size("tensor")
    at_z, at_f, at_t = lax.axis_index("expert"), lax.axis_index("fsdp"), lax.axis_index("tensor")
    owned = gate_up.shape[0]
    steps, block, width = tokens.shape
    own_rows = steps * block
    cols = width // (across * within)
    lists = block_list.reshape(-1)
    counts = block_count.reshape(-1)

    share = lax.dynamic_slice_in_dim(tokens, (at_f * within + at_t) * cols, cols, 2).reshape(own_rows, cols)
    info = jnp.concatenate(
        [route.astype(F32).reshape(own_rows, 2).T, route_weight.reshape(own_rows, 2).T, jnp.zeros((4, own_rows), F32)]
    )
    infos = [info] + [shift(info, "expert", k) for k in range(1, groups)]
    away = [shift(share, "expert", k) for k in range(1, groups)]
    first_new, second_new, delta = adam_update(adam_first, adam_second, gradient, lists, counts)
    away, first_new, second_new, delta = lax.optimization_barrier((away, first_new, second_new, delta))
    away = jnp.stack(away)

    here = jnp.stack([at_z]).astype(jnp.int32)
    select, scatter, weight = route_tables(here, infos, owned, block)
    columns = [away] + [swap(away, "fsdp", r) for r in range(1, across)]

    def stage(shares, sums, last):
        places = jnp.stack([at_f ^ r for r in shares] + [at_t ^ q for q in range(within)]).astype(jnp.int32)
        received = [[columns[r]] + [swap(columns[r], "tensor", q) for q in range(1, within)] for r in shares]
        return gate_up_stage(places, select, weight, tokens, received, gate_up, sums, last)

    sums = stage([0], None, False)
    delta, sums = lax.optimization_barrier((delta, sums))
    by_owner = delta.reshape(groups, owned, *delta.shape[1:])
    incoming = lax.all_to_all(by_owner, "expert", split_axis=0, concat_axis=0, tiled=True)
    sums = stage(list(range(1, across - 1)), sums, False)
    hidden = stage([across - 1], sums, True)

    def place(r):
        return jnp.stack([at_z] + [(at_f ^ r) * within + (at_t ^ q) for q in range(within)]).astype(jnp.int32)

    def down(where):
        pieces = down_pieces(where, lists, hidden, scatter, incoming, down_weight, cols)
        return pieces[0], [swap(pieces[q], "tensor", q) for q in range(1, within)]

    def add(*terms):
        total = terms[0].astype(F32)
        for term in terms[1:]:
            total = total + term.astype(F32)
        return total.astype(BF16)

    rows = groups * own_rows
    upper, lower = slice(0, rows // 2), slice(rows // 2, rows)

    def summed(pair, at):
        return add(pair[0][at], *[other[at] for other in pair[1]])

    if across == 4:
        far = down(place(3))
        one = down(place(1))
        far_up, far_low = summed(far, upper), summed(far, lower)
        next_place, far_up, far_low = lax.optimization_barrier((place(2), far_up, far_low))
        by_one, by_two = swap(far_up, "fsdp", 1), swap(far_low, "fsdp", 2)
        two = down(next_place)
        one_sum = summed(one, upper)
        next_place, one_sum, one = lax.optimization_barrier((place(0), one_sum, one))
        one_up = swap(one_sum, "fsdp", 1)
        own = down(next_place)
        one_low = swap(add(one[0][lower], *[o[lower] for o in one[1]], by_two), "fsdp", 1)
        two_low = swap(summed(two, lower), "fsdp", 2)
        two_up = swap(add(two[0][upper], *[o[upper] for o in two[1]], by_one), "fsdp", 2)
        total_up = add(own[0][upper], *[o[upper] for o in own[1]], one_up, two_up)
        total_low = add(own[0][lower], *[o[lower] for o in own[1]], one_low, two_low)
        parts = list(total_up.reshape(groups // 2, own_rows, cols)) + list(
            total_low.reshape(groups // 2, own_rows, cols)
        )
    else:
        others = [swap(summed(down(place(r)), slice(0, rows)), "fsdp", r) for r in range(1, across)]
        parts = list(add(summed(down(place(0)), slice(0, rows)), *others).reshape(groups, own_rows, cols))
    mixed = add(parts[0], *[shift(parts[k], "expert", -k) for k in range(1, groups)])
    return (mixed.reshape(steps, block, cols), first_new, second_new)


def solution(mesh):
    return jax.shard_map(
        on_device,
        mesh=mesh,
        in_specs=(
            P(None, "expert", None),
            P(None, "expert", None),
            P(None, "expert", None),
            P("expert", None, None, ("fsdp", "tensor")),
            P("expert", ("fsdp", "tensor"), None),
            P(None, ("fsdp", "tensor"), "expert"),
            P(None, ("fsdp", "tensor"), "expert"),
            P(None, ("fsdp", "tensor"), "expert"),
            P(None, ("fsdp", "tensor"), None),
            P(None, ("fsdp", "tensor")),
        ),
        out_specs=(
            P(None, "expert", ("fsdp", "tensor")),
            P(None, ("fsdp", "tensor"), "expert"),
            P(None, ("fsdp", "tensor"), "expert"),
        ),
        check_vma=False,
    )
```

time: 510 us -> 140 us (0.27)
  waiting for transfers between devices: 252 us -> 25.6 us
  local copies, waits for them, and re-layouts: 108 us -> 28 us
  other arithmetic: 61.2 us -> 3.76 us
  Pallas kernels: 0 us -> 50.5 us
  matrix products: 48.5 us -> 0 us
  between operations: 14 us -> 0.85 us
  starting transfers between devices: 23.9 us -> 30.9 us
    all_to_all x5 -> x1, waiting for transfers between devices: 116 us -> 0.01 us  [on_device(): lax.all_to_all(by_owner, 'expert', split_axis=0, concat_axis=0, tiled=True)]
    psum x1 -> x0, waiting for transfers between devices: 80.5 us -> none  [on_device(): lax.psum(rounded.astype(jnp.float32).reshape(slots_all, width).astype(jnp...]
    reduce_scatter x2 -> x0, waiting for transfers between devices: 55.6 us -> none  [on_device(): lax.psum_scatter(token_part.astype(jnp.bfloat16), ('fsdp', 'tensor'), sca...]
    reshape x6 -> x3, local copies, waits for them, and re-layouts: 53.7 us -> 0.25 us  [the longest x1 0.08 us: on_device(): route.astype(F32).reshape(own_rows, 2)]
    pallas_call x0 -> x9, Pallas kernels: none -> 50.5 us  [the longest x3 26.6 us: gate_up_stage(): pl.pallas_call(functools.partial(gate_up_kernel, shares, within, first, l...]
    dot_general x8 -> x0, matrix products: 48.5 us -> none  [the longest x2 28.5 us: on_device(): jnp.einsum('cxed,xgdh->cxegh', slot_block, gate_up, preferred_element_typ...]
    convert_element_type x7, other arithmetic: 38 us -> 3.18 us  [the longest x6 2.5 us: add(): return total.astype(BF16)]
    convert_element_type x8 -> x1, local copies, waits for them, and re-layouts: 32.6 us -> 0.01 us  [on_device(): route.astype(F32).reshape(own_rows, 2)]
  transfers between devices with their start and end apart: 8 -> 27, of which waited for: 8 -> 8; matrix products, arithmetic and copies ran while one was open for 18% -> 3% of each run, Pallas kernels for 0% -> 33%
where the time goes in v1:
time: 140 us
  Pallas kernels  50.5 us (36%)
  starting transfers between devices  30.9 us (22%)
  local copies, waits for them, and re-layouts  28 us (20%)
  waiting for transfers between devices  25.6 us (18%)
  other arithmetic  3.76 us (3%)
    unnamed x20, local copies, waits for them, and re-layouts  26.7 us
    pallas_call x3, Pallas kernels, gate_up_stage(): pl.pallas_call(functools.partial(gate_up_kernel, shares, within, first, l...  26.6 us
    pallas_call x4, Pallas kernels, down_pieces(): pl.pallas_call(functools.partial(down_kernel, owned, within), grid_spec=p...  15.6 us
    ppermute x9, starting transfers between devices, shift(): lax.ppermute(value, axis, [(i, (i + distance) % size) for i in range(size)])  14.6 us
    ppermute x9, waiting for transfers between devices, shift(): lax.ppermute(value, axis, [(i, (i + distance) % size) for i in range(size)])  13.3 us
    ppermute x17, starting transfers between devices, swap(): lax.ppermute(value, axis, [(i, i ^ distance) for i in range(lax.axis_size...  12.6 us
    ppermute x17, waiting for transfers between devices, swap(): lax.ppermute(value, axis, [(i, i ^ distance) for i in range(lax.axis_size...  12.3 us
    pallas_call x1, Pallas kernels, adam_update(): pl.pallas_call(adam_kernel, grid_spec=pltpu.PrefetchScalarGridSpec(num_sc...  7.89 us
  transfers between devices with their start and end apart: 27, of which 8 were waited for; matrix products, arithmetic and copies ran while one was open for 3% of the time, Pallas kernels for 33%

profile of v1, /device:TPU:0, one launch (start us, length us, event | category | flops | bytes accessed | tf_op | source)
XLA Modules:
  0.0 139.6 jit_solution(8923338115337123712)
XLA Ops:
  1.6 3.1 %collective-permute-start.3 = (bf16[128,512]{1,0:T(8,128)(2,1)S(1)}, bf16[128,512]{1,0:T(8,128)(2,1)S(1)}, u32[]{:S(2)}, u32[]{:S(2)}) collective-permute-start(bf16[128,512]{1,0:T(8,128)(2,1)S(1)} %bitcast.32), channel_id=1, source_target_pairs={{0,2},{2,4},{4,6},{6,0},{1,3},{3,5},{5,7},{7,1},{8,10},{10,12},{12... | collective-permute-start | bytes 393224 | tf_op jit(solution)/shard_map/ppermute | solution.py:311
  4.6 2.6 %collective-permute-start.4 = (bf16[128,512]{1,0:T(8,128)(2,1)S(1)}, bf16[128,512]{1,0:T(8,128)(2,1)S(1)}, u32[]{:S(2)}, u32[]{:S(2)}) collective-permute-start(bf16[128,512]{1,0:T(8,128)(2,1)S(1)} %bitcast.33), channel_id=1, source_target_pairs={{0,4},{2,6},{4,0},{6,2},{1,5},{3,7},{5,1},{7,3},{8,12},{10,14},{12... | collective-permute-start | bytes 393224 | tf_op jit(solution)/shard_map/ppermute | solution.py:311
  11.0 3.4 %copy-done.5 = f32[8,256,1024]{2,1,0:T(8,128)S(1)} copy-done((f32[8,256,1024]{2,1,0:T(8,128)S(1)}, f32[8,256,1024]{2,1,0:T(8,128)}, u32[]{:S(2)}) %copy-start.5) | copy-done | bytes 8388632
  14.4 3.4 %copy-done.6 = f32[8,256,1024]{2,1,0:T(8,128)S(1)} copy-done((f32[8,256,1024]{2,1,0:T(8,128)S(1)}, f32[8,256,1024]{2,1,0:T(8,128)}, u32[]{:S(2)}) %copy-start.6) | copy-done | bytes 8388632
  17.8 2.2 %copy-done.7 = bf16[8,256,1024]{2,1,0:T(8,128)(2,1)S(1)} copy-done((bf16[8,256,1024]{2,1,0:T(8,128)(2,1)S(1)}, bf16[8,256,1024]{2,1,0:T(8,128)(2,1)}, u32[]{:S(2)}) %copy-start.7) | copy-done | bytes 4194328
  20.6 7.9 %adam_listed.1 = (f32[8,256,1024]{2,1,0:T(8,128)}, f32[8,256,1024]{2,1,0:T(8,128)}, bf16[8,32,1024]{2,1,0:T(8,128)(2,1)}) custom-call(s32[32]{0:T(128)S(1)} %reshape.37.list_ref, s32[8]{0:T(128)S(1)} %bitcast.30, f32[8,256,1024]{2,1,0:T(8,128)S(1)} %copy-done.5, f32[8,256,1024]{2,1,0:T(8,128)S(1)} %copy-done.6, bf16[8,256,1024]{2,1,0:T(8,128)(2,1)S(1)} %copy-done.7), custom_call_target="tpu_custom_call" | custom-call | flops 16777216 | bytes 37748736 | tf_op jit(solution)/shard_map/adam_listed/pallas_call | solution.py:49
  32.9 4.3 %collective-permute-done.refs_1_ = f32[8,128]{1,0:T(8,128)S(1)} collective-permute-done((f32[8,128]{1,0:T(8,128)S(1)}, f32[8,128]{1,0:T(8,128)S(1)}, u32[]{:S(2)}, u32[]{:S(2)}) %collective-permute-start) | collective-permute-done | bytes 4128 | tf_op jit(solution)/shard_map/ppermute | solution.py:311
  37.3 3.5 %collective-permute-done.2.refs_3_ = f32[8,128]{1,0:T(8,128)S(1)} collective-permute-done((f32[8,128]{1,0:T(8,128)S(1)}, f32[8,128]{1,0:T(8,128)S(1)}, u32[]{:S(2)}, u32[]{:S(2)}) %collective-permute-start.2) | collective-permute-done | bytes 4128 | tf_op jit(solution)/shard_map/ppermute | solution.py:311
  42.4 6.8 %gate_up_stage.3.refs_5_ = f32[2,2,256,1024]{3,2,1,0:T(8,128)S(1)} custom-call(s32[3]{0:T(128)S(1)} %add_add_fusion.1.meta_ref, bf16[2,256,256]{2,1,0:T(8,128)(2,1)S(1)} %get-tuple-element.32.select_ref, f32[2,256,128]{2,1,0:T(8,128)S(1)} %get-tuple-element.33.weight_ref, bf16[2,64,4096]{2,1,0:T(8,128)(2,1)S(1)} %copy-done.4, ...), custom_call_target="tpu_custom_call" | custom-call | flops 2147483648 | bytes 16777216 | tf_op jit(solution)/shard_map/gate_up_stage/pallas_call | solution.py:210
  51.1 3.6 %all-to-all-start = ((bf16[4,2,32,1024]{3,2,1,0:T(8,128)(2,1)}), bf16[4,2,32,1024]{3,2,1,0:T(8,128)(2,1)S(1)}, u32[]{:S(2)}, u32[]{:S(2)}) async-start(bf16[4,2,32,1024]{3,2,1,0:T(8,128)(2,1)} %bitcast.18), calls=%async_computation | async-start | bytes 1048576 | tf_op jit(solution)/shard_map/all_to_all | solution.py:358
  57.2 13.0 %gate_up_stage.4.refs_3_ = f32[2,2,256,1024]{3,2,1,0:T(8,128)S(1)} custom-call(s32[4]{0:T(128)S(1)} %pad_add_fusion.2.meta_ref, bf16[2,256,256]{2,1,0:T(8,128)(2,1)S(1)} %get-tuple-element.32.select_ref, f32[2,256,128]{2,1,0:T(8,128)S(1)} %get-tuple-element.33.weight_ref, bf16[2,64,4096]{2,1,0:T(8,128)(2,1)S(1)} %copy-done.4, ...), custom_call_target="tpu_custom_call" | custom-call | flops 4294967296 | bytes 25165824 | tf_op jit(solution)/shard_map/gate_up_stage/pallas_call | solution.py:210
  70.3 6.8 %gate_up_stage.5.hidden_ref = bf16[2,256,1024]{2,1,0:T(8,128)(2,1)S(1)} custom-call(s32[3]{0:T(128)S(1)} %add_add_fusion.meta_ref, bf16[2,256,256]{2,1,0:T(8,128)(2,1)S(1)} %get-tuple-element.32.select_ref, f32[2,256,128]{2,1,0:T(8,128)S(1)} %get-tuple-element.33.weight_ref, bf16[2,64,4096]{2,1,0:T(8,128)(2,1)S(1)} %copy-done.4, ...), custom_call_target="tpu_custom_call" | custom-call | flops 2147483648 | bytes 16777216 | tf_op jit(solution)/shard_map/gate_up_stage/pallas_call | solution.py:210
  77.1 5.8 %copy-done = bf16[2,1024,4096]{2,1,0:T(8,128)(2,1)S(1)} copy-done((bf16[2,1024,4096]{2,1,0:T(8,128)(2,1)S(1)}, bf16[2,1024,4096]{2,1,0:T(8,128)(2,1)}, u32[]{:S(2)}) %copy-start) | copy-done | bytes 16777240
  82.9 4.3 %down_mixed.6 = (bf16[512,512]{1,0:T(8,128)(2,1)S(1)}, bf16[512,512]{1,0:T(8,128)(2,1)}) custom-call(s32[3]{0:T(128)S(1)} %get-tuple-element.70.meta_ref, s32[32]{0:T(128)S(1)} %reshape.37.list_ref, bf16[2,256,1024]{2,1,0:T(8,128)(2,1)S(1)} %gate_up_stage.5.hidden_ref, bf16[2,256,256]{2,1,0:T(8,128)(2,1)S(1)} %get-tuple-element.42.scatter_ref, ...), custom_call_target="tpu_custom_call" | custom-call | flops 1073741824 | bytes 4194304 | tf_op jit(solution)/shard_map/down_mixed/pallas_call | solution.py:282
  87.6 5.8 %copy-done.1 = bf16[2,1024,4096]{2,1,0:T(8,128)(2,1)S(1)} copy-done((bf16[2,1024,4096]{2,1,0:T(8,128)(2,1)S(1)}, bf16[2,1024,4096]{2,1,0:T(8,128)(2,1)}, u32[]{:S(2)}) %copy-start.1) | copy-done | bytes 16777240
  93.4 3.8 %down_mixed.4 = (bf16[512,512]{1,0:T(8,128)(2,1)S(1)}, bf16[512,512]{1,0:T(8,128)(2,1)S(1)}) custom-call(s32[3]{0:T(128)S(1)} %get-tuple-element.69.meta_ref, s32[32]{0:T(128)S(1)} %reshape.37.list_ref, bf16[2,256,1024]{2,1,0:T(8,128)(2,1)S(1)} %gate_up_stage.5.hidden_ref, bf16[2,256,256]{2,1,0:T(8,128)(2,1)S(1)} %get-tuple-element.42.scatter_ref, ...), custom_call_target="tpu_custom_call" | custom-call | flops 1073741824 | bytes 4194304 | tf_op jit(solution)/shard_map/down_mixed/pallas_call | solution.py:282
  100.2 3.8 %down_mixed.7 = (bf16[512,512]{1,0:T(8,128)(2,1)S(1)}, bf16[512,512]{1,0:T(8,128)(2,1)S(1)}) custom-call(s32[3]{0:T(128)S(1)} %pad_add_fusion.3.meta_ref, s32[32]{0:T(128)S(1)} %reshape.37.list_ref, bf16[2,256,1024]{2,1,0:T(8,128)(2,1)S(1)} %gate_up_stage.5.hidden_ref, bf16[2,256,256]{2,1,0:T(8,128)(2,1)S(1)} %get-tuple-element.42.scatter_ref, ...), custom_call_target="tpu_custom_call" | custom-call | flops 1073741824 | bytes 4194304 | tf_op jit(solution)/shard_map/down_mixed/pallas_call | solution.py:282
  105.9 3.8 %down_mixed.5 = (bf16[512,512]{1,0:T(8,128)(2,1)S(1)}, bf16[512,512]{1,0:T(8,128)(2,1)S(1)}) custom-call(s32[3]{0:T(128)S(1)} %pad_add_fusion.meta_ref, s32[32]{0:T(128)S(1)} %reshape.37.list_ref, bf16[2,256,1024]{2,1,0:T(8,128)(2,1)S(1)} %gate_up_stage.5.hidden_ref, bf16[2,256,256]{2,1,0:T(8,128)(2,1)S(1)} %get-tuple-element.42.scatter_ref, ...), custom_call_target="tpu_custom_call" | custom-call | flops 1073741824 | bytes 4194304 | tf_op jit(solution)/shard_map/down_mixed/pallas_call | solution.py:282
  115.3 3.7 %collective-permute-done.15 = bf16[256,512]{1,0:T(8,128)(2,1)S(1)} collective-permute-done((bf16[256,512]{1,0:T(8,128)(2,1)S(1)}, bf16[256,512]{1,0:T(8,128)(2,1)S(1)}, u32[]{:S(2)}, u32[]{:S(2)}) %collective-permute-start.15) | collective-permute-done | bytes 262176 | tf_op jit(solution)/shard_map/ppermute | solution.py:306
  118.9 5.3 %collective-permute-done.22 = bf16[256,512]{1,0:T(8,128)(2,1)S(1)} collective-permute-done((bf16[256,512]{1,0:T(8,128)(2,1)S(1)}, bf16[256,512]{1,0:T(8,128)(2,1)S(1)}, u32[]{:S(2)}, u32[]{:S(2)}) %collective-permute-start.22) | collective-permute-done | bytes 262176 | tf_op jit(solution)/shard_map/ppermute | solution.py:306
  124.2 2.4 %collective-permute-done.23 = bf16[256,512]{1,0:T(8,128)(2,1)S(1)} collective-permute-done((bf16[256,512]{1,0:T(8,128)(2,1)S(1)}, bf16[256,512]{1,0:T(8,128)(2,1)S(1)}, u32[]{:S(2)}, u32[]{:S(2)}) %collective-permute-start.23) | collective-permute-done | bytes 262176 | tf_op jit(solution)/shard_map/ppermute | solution.py:306
  126.9 2.7 %collective-permute-start.24 = (bf16[128,512]{1,0:T(8,128)(2,1)S(1)}, bf16[128,512]{1,0:T(8,128)(2,1)S(1)}, u32[]{:S(2)}, u32[]{:S(2)}) collective-permute-start(bf16[128,512]{1,0:T(8,128)(2,1)S(1)} %get-tuple-element.67), channel_id=1, source_target_pairs={{0,4},{2,6},{4,0},{6,2},{1,5},{3,7},{5,1},{7,3},{8,12},{10,14},{12... | collective-permute-start | bytes 393224 | tf_op jit(solution)/shard_map/ppermute | solution.py:311
  131.0 2.4 %collective-permute-start.20 = (bf16[128,512]{1,0:T(8,128)(2,1)S(1)}, bf16[128,512]{1,0:T(8,128)(2,1)S(1)}, u32[]{:S(2)}, u32[]{:S(2)}) collective-permute-start(bf16[128,512]{1,0:T(8,128)(2,1)S(1)} %unstack.21), channel_id=1, source_target_pairs={{0,6},{2,0},{4,2},{6,4},{1,7},{3,1},{5,3},{7,5},{8,14},{10,8},{12,... | collective-permute-start | bytes 393224 | tf_op jit(solution)/shard_map/ppermute | solution.py:311
  133.4 5.3 %collective-permute-done.24 = bf16[128,512]{1,0:T(8,128)(2,1)S(1)} collective-permute-done((bf16[128,512]{1,0:T(8,128)(2,1)S(1)}, bf16[128,512]{1,0:T(8,128)(2,1)S(1)}, u32[]{:S(2)}, u32[]{:S(2)}) %collective-permute-start.24) | collective-permute-done | bytes 131104 | tf_op jit(solution)/shard_map/ppermute | solution.py:311
  (83 shorter events, 29.3 us)
Async XLA Ops:
  1.6 27.0 %collective-permute-start.3 = (bf16[128,512]{1,0:T(8,128)(2,1)S(1)}, bf16[128,512]{1,0:T(8,128)(2,1)S(1)}, u32[]{:S(2)}, u32[]{:S(2)}) collective-permute-start(bf16[128,512]{1,0:T(8,128)(2,1)S(1)} %bitcast.32), channel_id=1, source_target_pairs={{0,2},{2,4},{4,6},{6,0},{1,3},{3,5},{5,7},{7,1},{8,10},{10,12},{12... | collective-permute-start | bytes 393224 | tf_op jit(solution)/shard_map/ppermute | solution.py:311
  4.6 23.9 %collective-permute-start.4 = (bf16[128,512]{1,0:T(8,128)(2,1)S(1)}, bf16[128,512]{1,0:T(8,128)(2,1)S(1)}, u32[]{:S(2)}, u32[]{:S(2)}) collective-permute-start(bf16[128,512]{1,0:T(8,128)(2,1)S(1)} %bitcast.33), channel_id=1, source_target_pairs={{0,4},{2,6},{4,0},{6,2},{1,5},{3,7},{5,1},{7,3},{8,12},{10,14},{12... | collective-permute-start | bytes 393224 | tf_op jit(solution)/shard_map/ppermute | solution.py:311
  7.2 21.3 %collective-permute-start.5 = (bf16[128,512]{1,0:T(8,128)(2,1)S(1)}, bf16[128,512]{1,0:T(8,128)(2,1)S(1)}, u32[]{:S(2)}, u32[]{:S(2)}) collective-permute-start(bf16[128,512]{1,0:T(8,128)(2,1)S(1)} %bitcast.34), channel_id=1, source_target_pairs={{0,6},{2,0},{4,2},{6,4},{1,7},{3,1},{5,3},{7,5},{8,14},{10,8},{12,... | collective-permute-start | bytes 393224 | tf_op jit(solution)/shard_map/ppermute | solution.py:311
  28.6 13.8 %collective-permute-start.12 = (bf16[3,128,512]{2,1,0:T(8,128)(2,1)S(1)}, bf16[3,128,512]{2,1,0:T(8,128)(2,1)S(1)}, u32[]{:S(2)}, u32[]{:S(2)}) collective-permute-start(bf16[3,128,512]{2,1,0:T(8,128)(2,1)S(1)} %pad_maximum_fusion.refs_0_), channel_id=1, source_target_pairs={{0,1},{1,0},{2,3},{3,2},{4,5},{5,4},{6,7},{7,6},{8,9},{9,8},{10,11... | collective-permute-start | bytes 1179656 | tf_op jit(solution)/shard_map/ppermute | solution.py:306
  28.7 13.2 %collective-permute-start.10 = (bf16[3,128,512]{2,1,0:T(8,128)(2,1)S(1)}, bf16[3,128,512]{2,1,0:T(8,128)(2,1)S(1)}, u32[]{:S(2)}, u32[]{:S(2)}) collective-permute-start(bf16[3,128,512]{2,1,0:T(8,128)(2,1)S(1)} %pad_maximum_fusion.refs_0_), channel_id=1, source_target_pairs={{0,16},{8,24},{16,0},{24,8},{1,17},{9,25},{17,1},{25,9},{2,18},{10... | collective-permute-start | bytes 1179656 | tf_op jit(solution)/shard_map/ppermute | solution.py:306
  30.3 11.6 %collective-permute-start.8 = (bf16[3,128,512]{2,1,0:T(8,128)(2,1)S(1)}, bf16[3,128,512]{2,1,0:T(8,128)(2,1)}, u32[]{:S(2)}, u32[]{:S(2)}) collective-permute-start(bf16[3,128,512]{2,1,0:T(8,128)(2,1)S(1)} %pad_maximum_fusion.refs_0_), channel_id=1, source_target_pairs={{0,8},{8,0},{16,24},{24,16},{1,9},{9,1},{17,25},{25,17},{2,10},{10... | collective-permute-start | bytes 1179656 | tf_op jit(solution)/shard_map/ppermute | solution.py:306
  41.3 13.6 %collective-permute-start.6 = (bf16[3,128,512]{2,1,0:T(8,128)(2,1)S(1)}, bf16[3,128,512]{2,1,0:T(8,128)(2,1)}, u32[]{:S(2)}, u32[]{:S(2)}) collective-permute-start(bf16[3,128,512]{2,1,0:T(8,128)(2,1)S(1)} %pad_maximum_fusion.refs_0_), channel_id=1, source_target_pairs={{0,24},{8,16},{16,8},{24,0},{1,25},{9,17},{17,9},{25,1},{2,26},{10... | collective-permute-start | bytes 1179656 | tf_op jit(solution)/shard_map/ppermute | solution.py:306
  41.9 13.2 %collective-permute-start.11 = (bf16[3,128,512]{2,1,0:T(8,128)(2,1)S(1)}, bf16[3,128,512]{2,1,0:T(8,128)(2,1)}, u32[]{:S(2)}, u32[]{:S(2)}) collective-permute-start(bf16[3,128,512]{2,1,0:T(8,128)(2,1)S(1)} %collective-permute-done.10.refs_2_), channel_id=1, source_target_pairs={{0,1},{1,0},{2,3},{3,2},{4,5},{5,4},{6,7},{7,6},{8,9},{9,8},{10,11... | collective-permute-start | bytes 1179656 | tf_op jit(solution)/shard_map/ppermute | solution.py:306
  41.9 13.2 %collective-permute-start.9 = (bf16[3,128,512]{2,1,0:T(8,128)(2,1)}, bf16[3,128,512]{2,1,0:T(8,128)(2,1)}, u32[]{:S(2)}, u32[]{:S(2)}) collective-permute-start(bf16[3,128,512]{2,1,0:T(8,128)(2,1)} %collective-permute-done.8.refs_0_), channel_id=1, source_target_pairs={{0,1},{1,0},{2,3},{3,2},{4,5},{5,4},{6,7},{7,6},{8,9},{9,8},{10,11... | collective-permute-start | bytes 1179656 | tf_op jit(solution)/shard_map/ppermute | solution.py:306
  51.1 25.9 %all-to-all-start = ((bf16[4,2,32,1024]{3,2,1,0:T(8,128)(2,1)}), bf16[4,2,32,1024]{3,2,1,0:T(8,128)(2,1)S(1)}, u32[]{:S(2)}, u32[]{:S(2)}) async-start(bf16[4,2,32,1024]{3,2,1,0:T(8,128)(2,1)} %bitcast.18), calls=%async_computation | async-start | bytes 1048576 | tf_op jit(solution)/shard_map/all_to_all | solution.py:358
  54.9 15.3 %collective-permute-start.7 = (bf16[3,128,512]{2,1,0:T(8,128)(2,1)}, bf16[3,128,512]{2,1,0:T(8,128)(2,1)S(1)}, u32[]{:S(2)}, u32[]{:S(2)}) collective-permute-start(bf16[3,128,512]{2,1,0:T(8,128)(2,1)} %collective-permute-done.6.refs_0_), channel_id=1, source_target_pairs={{0,1},{1,0},{2,3},{3,2},{4,5},{5,4},{6,7},{7,6},{8,9},{9,8},{10,11... | collective-permute-start | bytes 1179656 | tf_op jit(solution)/shard_map/ppermute | solution.py:306
  87.1 10.3 %collective-permute-start.16 = (bf16[512,512]{1,0:T(8,128)(2,1)}, bf16[512,512]{1,0:T(8,128)(2,1)}, u32[]{:S(2)}, u32[]{:S(2)}) collective-permute-start(bf16[512,512]{1,0:T(8,128)(2,1)} %get-tuple-element.51), channel_id=1, source_target_pairs={{0,1},{1,0},{2,3},{3,2},{4,5},{5,4},{6,7},{7,6},{8,9},{9,8},{10,11... | collective-permute-start | bytes 1572872 | tf_op jit(solution)/shard_map/ppermute | solution.py:306
  97.2 7.1 %collective-permute-start.13 = (bf16[512,512]{1,0:T(8,128)(2,1)S(1)}, bf16[512,512]{1,0:T(8,128)(2,1)S(1)}, u32[]{:S(2)}, u32[]{:S(2)}) collective-permute-start(bf16[512,512]{1,0:T(8,128)(2,1)S(1)} %get-tuple-element.45), channel_id=1, source_target_pairs={{0,1},{1,0},{2,3},{3,2},{4,5},{5,4},{6,7},{7,6},{8,9},{9,8},{10,11... | collective-permute-start | bytes 1572872 | tf_op jit(solution)/shard_map/ppermute | solution.py:306
  98.7 11.7 %collective-permute-start.21 = (bf16[256,512]{1,0:T(8,128)(2,1)S(1)}, bf16[256,512]{1,0:T(8,128)(2,1)S(1)}, u32[]{:S(2)}, u32[]{:S(2)}) collective-permute-start(bf16[256,512]{1,0:T(8,128)(2,1)S(1)} %get-tuple-element.58), channel_id=1, source_target_pairs={{0,16},{8,24},{16,0},{24,8},{1,17},{9,25},{17,1},{25,9},{2,18},{10... | collective-permute-start | bytes 786440 | tf_op jit(solution)/shard_map/ppermute | solution.py:306
  104.0 9.0 %collective-permute-start.17 = (bf16[512,512]{1,0:T(8,128)(2,1)S(1)}, bf16[512,512]{1,0:T(8,128)(2,1)S(1)}, u32[]{:S(2)}, u32[]{:S(2)}) collective-permute-start(bf16[512,512]{1,0:T(8,128)(2,1)S(1)} %get-tuple-element.54), channel_id=1, source_target_pairs={{0,1},{1,0},{2,3},{3,2},{4,5},{5,4},{6,7},{7,6},{8,9},{9,8},{10,11... | collective-permute-start | bytes 1572872 | tf_op jit(solution)/shard_map/ppermute | solution.py:306
  104.3 8.7 %collective-permute-start.18 = (bf16[256,512]{1,0:T(8,128)(2,1)S(1)}, bf16[256,512]{1,0:T(8,128)(2,1)S(1)}, u32[]{:S(2)}, u32[]{:S(2)}) collective-permute-start(bf16[256,512]{1,0:T(8,128)(2,1)S(1)} %get-tuple-element.55), channel_id=1, source_target_pairs={{0,8},{8,0},{16,24},{24,16},{1,9},{9,1},{17,25},{25,17},{2,10},{10... | collective-permute-start | bytes 786440 | tf_op jit(solution)/shard_map/ppermute | solution.py:306
  109.7 14.5 %collective-permute-start.14 = (bf16[512,512]{1,0:T(8,128)(2,1)S(1)}, bf16[512,512]{1,0:T(8,128)(2,1)S(1)}, u32[]{:S(2)}, u32[]{:S(2)}) collective-permute-start(bf16[512,512]{1,0:T(8,128)(2,1)S(1)} %get-tuple-element.48), channel_id=1, source_target_pairs={{0,1},{1,0},{2,3},{3,2},{4,5},{5,4},{6,7},{7,6},{8,9},{9,8},{10,11... | collective-permute-start | bytes 1572872 | tf_op jit(solution)/shard_map/ppermute | solution.py:306
  109.8 9.1 %collective-permute-start.15 = (bf16[256,512]{1,0:T(8,128)(2,1)S(1)}, bf16[256,512]{1,0:T(8,128)(2,1)S(1)}, u32[]{:S(2)}, u32[]{:S(2)}) collective-permute-start(bf16[256,512]{1,0:T(8,128)(2,1)S(1)} %add_convert_fusion.7), channel_id=1, source_target_pairs={{0,8},{8,0},{16,24},{24,16},{1,9},{9,1},{17,25},{25,17},{2,10},{10... | collective-permute-start | bytes 786440 | tf_op jit(solution)/shard_map/ppermute | solution.py:306
  110.5 13.7 %collective-permute-start.22 = (bf16[256,512]{1,0:T(8,128)(2,1)S(1)}, bf16[256,512]{1,0:T(8,128)(2,1)S(1)}, u32[]{:S(2)}, u32[]{:S(2)}) collective-permute-start(bf16[256,512]{1,0:T(8,128)(2,1)S(1)} %add_convert_fusion.2), channel_id=1, source_target_pairs={{0,8},{8,0},{16,24},{24,16},{1,9},{9,1},{17,25},{25,17},{2,10},{10... | collective-permute-start | bytes 786440 | tf_op jit(solution)/shard_map/ppermute | solution.py:306
  113.2 11.0 %collective-permute-start.19 = (bf16[256,512]{1,0:T(8,128)(2,1)S(1)}, bf16[256,512]{1,0:T(8,128)(2,1)S(1)}, u32[]{:S(2)}, u32[]{:S(2)}) collective-permute-start(bf16[256,512]{1,0:T(8,128)(2,1)S(1)} %get-tuple-element.63), channel_id=1, source_target_pairs={{0,16},{8,24},{16,0},{24,8},{1,17},{9,25},{17,1},{25,9},{2,18},{10... | collective-permute-start | bytes 786440 | tf_op jit(solution)/shard_map/ppermute | solution.py:306
  113.7 12.8 %collective-permute-start.23 = (bf16[256,512]{1,0:T(8,128)(2,1)S(1)}, bf16[256,512]{1,0:T(8,128)(2,1)S(1)}, u32[]{:S(2)}, u32[]{:S(2)}) collective-permute-start(bf16[256,512]{1,0:T(8,128)(2,1)S(1)} %get-tuple-element.64), channel_id=1, source_target_pairs={{0,16},{8,24},{16,0},{24,8},{1,17},{9,25},{17,1},{25,9},{2,18},{10... | collective-permute-start | bytes 786440 | tf_op jit(solution)/shard_map/ppermute | solution.py:306
  126.9 11.8 %collective-permute-start.24 = (bf16[128,512]{1,0:T(8,128)(2,1)S(1)}, bf16[128,512]{1,0:T(8,128)(2,1)S(1)}, u32[]{:S(2)}, u32[]{:S(2)}) collective-permute-start(bf16[128,512]{1,0:T(8,128)(2,1)S(1)} %get-tuple-element.67), channel_id=1, source_target_pairs={{0,4},{2,6},{4,0},{6,2},{1,5},{3,7},{5,1},{7,3},{8,12},{10,14},{12... | collective-permute-start | bytes 393224 | tf_op jit(solution)/shard_map/ppermute | solution.py:311
  129.5 9.2 %collective-permute-start.25 = (bf16[128,512]{1,0:T(8,128)(2,1)S(1)}, bf16[128,512]{1,0:T(8,128)(2,1)S(1)}, u32[]{:S(2)}, u32[]{:S(2)}) collective-permute-start(bf16[128,512]{1,0:T(8,128)(2,1)S(1)} %get-tuple-element.68), channel_id=1, source_target_pairs={{0,2},{2,4},{4,6},{6,0},{1,3},{3,5},{5,7},{7,1},{8,10},{10,12},{12... | collective-permute-start | bytes 393224 | tf_op jit(solution)/shard_map/ppermute | solution.py:311
  131.0 7.8 %collective-permute-start.20 = (bf16[128,512]{1,0:T(8,128)(2,1)S(1)}, bf16[128,512]{1,0:T(8,128)(2,1)S(1)}, u32[]{:S(2)}, u32[]{:S(2)}) collective-permute-start(bf16[128,512]{1,0:T(8,128)(2,1)S(1)} %unstack.21), channel_id=1, source_target_pairs={{0,6},{2,0},{4,2},{6,4},{1,7},{3,1},{5,3},{7,5},{8,14},{10,8},{12,... | collective-permute-start | bytes 393224 | tf_op jit(solution)/shard_map/ppermute | solution.py:311
  (12 other events, 60.9 us)

commit v2 on v0

v2 whole, which is shorter than its diff:
```python
import functools

import jax
import jax.numpy as jnp
from jax import lax
from jax.experimental import pallas as pl
from jax.experimental.pallas import tpu as pltpu
from jax.sharding import PartitionSpec as P

STRIDE = 4
BLOCK_ROWS = 8
MAXCH = 4
CAP = 32
UNIT_TILE = 512

BETA_ONE = 0.9
BETA_TWO = 0.95
LEARN_RATE = 0.03
ADAM_EPS = 1e-08
FIRST_FIX = 1.0 - 0.9**10
SECOND_FIX = 1.0 - 0.95**10

F32 = jnp.float32
BF16 = jnp.bfloat16
SMALL_VMEM = 16 * 2**20
STAGE_VMEM = 16 * 2**20


def in_hbm(value):
    return pltpu.with_memory_space_constraint(value, pltpu.HBM)


def as_column(ref, k):
    row = jnp.concatenate([ref[s, k : k + 1, :].astype(F32) for s in range(ref.shape[0])], axis=1)
    return jnp.transpose(jnp.broadcast_to(row, (row.shape[1], row.shape[1])))[:, 0:1]


def pack_kernel(groups, owned, meta_ref, tokens_ref, route_ref, *refs):
    sends, (own_ref, pick_ref) = refs[: groups - 1], refs[groups - 1 :]
    steps, block, width = tokens_ref.shape
    rows = steps * block
    cols = sends[0].shape[1]
    per_expert = steps * CAP
    per_group = owned * per_expert
    slots = groups * per_group
    token = lax.broadcasted_iota(jnp.int32, (rows, rows), 0)
    lane = lax.broadcasted_iota(jnp.int32, (rows, rows), 1)
    before = jnp.where((lane < token) & (lane // block == token // block), 1.0, 0.0).astype(BF16)
    named = [as_column(route_ref, k) for k in range(2)]
    lane = lane.astype(F32)
    member = jnp.where((lane == named[0]) | (lane == named[1]), 1.0, 0.0).astype(BF16)
    earlier = jnp.dot(before, member, preferred_element_type=F32)
    slot = lax.broadcasted_iota(jnp.int32, (rows, slots), 1)
    step = lax.broadcasted_iota(jnp.int32, (rows, slots), 0) // block
    group = (meta_ref[0] + slot // per_group) % groups
    expert = (group * owned + slot % per_group // per_expert).astype(F32)
    here = (slot % per_expert // CAP == step)
    spot = (slot % CAP).astype(F32)
    total = jnp.zeros((rows, slots), F32)
    for k in range(2):
        position = jnp.sum(jnp.where(lane == named[k], earlier, 0.0), axis=1, keepdims=True)
        pick = jnp.where((expert == named[k]) & here & (spot == position), 1.0, 0.0)
        pick_ref[k] = pick.astype(BF16)
        total = total + pick
    select = jnp.transpose(total).astype(BF16)
    lanes = pl.ds(pl.multiple_of(meta_ref[meta_ref.shape[0] - 1] * cols, cols), cols)
    share = jnp.concatenate([tokens_ref[s, :, lanes] for s in range(steps)], axis=0)
    for k in range(1, groups):
        sends[k - 1][...] = jnp.dot(
            select[k * per_group : (k + 1) * per_group], share, preferred_element_type=F32
        ).astype(BF16)
    every = jnp.concatenate([tokens_ref[s] for s in range(steps)], axis=0)
    own_ref[...] = jnp.dot(select[:per_group], every, preferred_element_type=F32).astype(BF16)


def pack_slots(meta, tokens, route, groups, owned, cols):
    steps, block, width = tokens.shape
    rows = steps * block
    per_group = owned * steps * CAP
    vmem = pl.BlockSpec(memory_space=pltpu.VMEM)
    return pl.pallas_call(
        functools.partial(pack_kernel, groups, owned),
        grid_spec=pltpu.PrefetchScalarGridSpec(
            num_scalar_prefetch=1, grid=(), in_specs=[vmem, vmem], out_specs=[vmem] * (groups + 1)
        ),
        out_shape=[jax.ShapeDtypeStruct((per_group, cols), BF16)] * (groups - 1)
        + [
            jax.ShapeDtypeStruct((per_group, width), BF16),
            jax.ShapeDtypeStruct((2, rows, groups * per_group), BF16),
        ],
        compiler_params=pltpu.CompilerParams(vmem_limit_bytes=SMALL_VMEM),
        cost_estimate=pl.CostEstimate(flops=10**7, bytes_accessed=4 * rows * width, transcendentals=0),
        name="pack_slots",
    )(meta, tokens, route.transpose(0, 2, 1))


def combine_kernel(pick_ref, weight_ref, *refs):
    out_ref = refs[-1]
    steps, block, _ = out_ref.shape
    rows = jnp.concatenate([ref[...] for ref in refs[:-1]], axis=0)
    total = jnp.zeros((steps * block, out_ref.shape[2]), F32)
    for k in range(2):
        total = total + as_column(weight_ref, k) * jnp.dot(pick_ref[k], rows, preferred_element_type=F32)
    for s in range(steps):
        out_ref[s] = total[s * block : (s + 1) * block].astype(BF16)


def combine_slots(pick, weight, parts):
    steps, block, _ = weight.shape
    cols = parts[0].shape[1]
    vmem = pl.BlockSpec(memory_space=pltpu.VMEM)
    return pl.pallas_call(
        combine_kernel,
        in_specs=[vmem] * (2 + len(parts)),
        out_specs=vmem,
        out_shape=jax.ShapeDtypeStruct((steps, block, cols), BF16),
        compiler_params=pltpu.CompilerParams(vmem_limit_bytes=SMALL_VMEM),
        cost_estimate=pl.CostEstimate(flops=10**7, bytes_accessed=10**6, transcendentals=0),
        name="combine_slots",
    )(pick, weight.transpose(0, 2, 1), *parts)


def delta_kernel(list_ref, count_ref, first_ref, second_ref, grad_ref, delta_out, first_buf, second_buf, grad_buf, sem):
    experts = delta_out.shape[0]

    def copies(expert, entry):
        block = list_ref[expert * MAXCH + entry]
        rows = pl.ds(pl.multiple_of(block * BLOCK_ROWS, BLOCK_ROWS), BLOCK_ROWS)
        pair = pl.ds(pl.multiple_of(block // 2 * (2 * BLOCK_ROWS), 2 * BLOCK_ROWS), 2 * BLOCK_ROWS)
        return (
            pltpu.make_async_copy(first_ref.at[expert, rows, :], first_buf.at[expert, entry], sem.at[0, expert, entry]),
            pltpu.make_async_copy(second_ref.at[expert, rows, :], second_buf.at[expert, entry], sem.at[1, expert, entry]),
            pltpu.make_async_copy(grad_ref.at[expert, pair, :], grad_buf.at[expert, entry], sem.at[2, expert, entry]),
        )

    for expert in range(experts):
        for entry in range(MAXCH):
            for copy in copies(expert, entry):
                copy.start()
    for expert in range(experts):
        parts = []
        for entry in range(MAXCH):
            for copy in copies(expert, entry):
                copy.wait()
            odd = list_ref[expert * MAXCH + entry] % 2 == 1
            grads = grad_buf[expert, entry].astype(F32)
            grad = jnp.where(odd, grads[BLOCK_ROWS:], grads[:BLOCK_ROWS])
            first = BETA_ONE * first_buf[expert, entry] + (1.0 - BETA_ONE) * grad
            second = BETA_TWO * second_buf[expert, entry] + (1.0 - BETA_TWO) * grad * grad
            step = LEARN_RATE * (first / FIRST_FIX) / (jnp.sqrt(second / SECOND_FIX) + ADAM_EPS)
            parts.append(jnp.where(entry < count_ref[expert], -step, 0.0))
        delta_out[expert] = jnp.concatenate(parts, axis=0).astype(BF16)


def listed_deltas(adam_first, adam_second, gradient, block_list, block_count):
    experts, _, cols = adam_first.shape
    hbm = pl.BlockSpec(memory_space=pltpu.HBM)
    return pl.pallas_call(
        delta_kernel,
        grid_spec=pltpu.PrefetchScalarGridSpec(
            num_scalar_prefetch=2,
            grid=(),
            in_specs=[hbm, hbm, hbm],
            out_specs=pl.BlockSpec(memory_space=pltpu.VMEM),
            scratch_shapes=[
                pltpu.VMEM((experts, MAXCH, BLOCK_ROWS, cols), F32),
                pltpu.VMEM((experts, MAXCH, BLOCK_ROWS, cols), F32),
                pltpu.VMEM((experts, MAXCH, 2 * BLOCK_ROWS, cols), BF16),
                pltpu.SemaphoreType.DMA((3, experts, MAXCH)),
            ],
        ),
        out_shape=jax.ShapeDtypeStruct((experts, MAXCH * BLOCK_ROWS, cols), BF16),
        compiler_params=pltpu.CompilerParams(vmem_limit_bytes=SMALL_VMEM),
        cost_estimate=pl.CostEstimate(flops=10**6, bytes_accessed=experts * MAXCH * 96 * cols, transcendentals=0),
        name="listed_deltas",
    )(block_list, block_count, in_hbm(adam_first), in_hbm(adam_second), in_hbm(gradient))


def adam_kernel(first_ref, second_ref, grad_ref, *refs):
    first_out, second_out = refs[-2:]
    grad = grad_ref[...].astype(F32)
    first_out[...] = BETA_ONE * first_ref[...] + (1.0 - BETA_ONE) * grad
    second_out[...] = BETA_TWO * second_ref[...] + (1.0 - BETA_TWO) * grad * grad


def adam_part(adam_first, adam_second, gradient, begin, end, filled=()):
    _, rows, cols = adam_first.shape
    block = pl.BlockSpec((1, rows, cols), lambda e: (begin + e, 0, 0))
    size = (end - begin) * rows * cols
    return pl.pallas_call(
        adam_kernel,
        grid=(end - begin,),
        in_specs=[block, block, block] + [pl.BlockSpec(memory_space=pltpu.HBM)] * len(filled),
        out_specs=[block, block],
        out_shape=[jax.ShapeDtypeStruct(adam_first.shape, F32)] * 2,
        input_output_aliases={3 + i: i for i in range(len(filled))},
        compiler_params=pltpu.CompilerParams(vmem_limit_bytes=SMALL_VMEM),
        cost_estimate=pl.CostEstimate(flops=8 * size, bytes_accessed=18 * size, transcendentals=0),
        name="adam_moments",
    )(in_hbm(adam_first), in_hbm(adam_second), in_hbm(gradient), *filled)


def gate_up_kernel(begin, shares, across, within, first, last, meta_ref, own_ref, *refs):
    recv = [refs[i * within : (i + 1) * within] for i in range(shares)]
    refs = refs[shares * within :]
    if first:
        gate_up_ref, out_ref, rows_ref = refs
    else:
        gate_up_ref, sums_ref, out_ref, rows_ref = refs
    expert, share = pl.program_id(0), pl.program_id(2)
    owned, slots = rows_ref.shape[1:3]
    tile = gate_up_ref.shape[3]
    cols = recv[0][0].shape[2]
    per_expert = own_ref.shape[0] // owned
    groups = slots // per_expert

    @pl.when((expert == 0) & (pl.program_id(1) == 0) & (share == 0))
    def _():
        for i in range(shares):
            for q in range(within):
                place = meta_ref[1 + across + q]
                start = (meta_ref[1 + begin + i] * within + place) * cols
                lanes = pl.ds(pl.multiple_of(start, cols), cols)
                into = pl.ds(pl.multiple_of(place * cols, cols), cols)
                for e in range(owned):
                    mine = slice(e * per_expert, (e + 1) * per_expert)
                    rows_ref[i, e, 0:per_expert, into] = own_ref[mine, lanes]
                    for k in range(1, groups):
                        rows_ref[i, e, k * per_expert : (k + 1) * per_expert, into] = recv[i][q][k - 1, mine, :]

    rows = rows_ref[share, expert]
    units = pl.ds(pl.multiple_of(pl.program_id(1) * tile, tile), tile)
    gate = jnp.dot(rows, gate_up_ref[0, 0], preferred_element_type=F32)
    up = jnp.dot(rows, gate_up_ref[0, 1], preferred_element_type=F32)
    if last:
        gate, up = gate + sums_ref[expert, 0, :, units], up + sums_ref[expert, 1, :, units]
        out_ref[expert, :, units] = (gate * jax.nn.sigmoid(gate) * up).astype(BF16)
    elif first:
        out_ref[expert, 0, :, units] = gate
        out_ref[expert, 1, :, units] = up
    else:

        @pl.when(share == 0)
        def _():
            out_ref[expert, 0, :, units] = sums_ref[expert, 0, :, units] + gate
            out_ref[expert, 1, :, units] = sums_ref[expert, 1, :, units] + up

        @pl.when(share > 0)
        def _():
            out_ref[expert, 0, :, units] += gate
            out_ref[expert, 1, :, units] += up


def gate_up_stage(meta, begin, across, own, received, gate_up, sums, last):
    owned, _, width, units = gate_up.shape
    shares, within = len(received), len(received[0])
    assert shares == 1 or not (last or sums is None)
    depth = within * received[0][0].shape[2]
    slots = own.shape[0] // owned * (1 + received[0][0].shape[0])
    tile = min(UNIT_TILE, units)
    vmem = pl.BlockSpec(memory_space=pltpu.VMEM)
    first = sums is None
    if last:
        out_shape = jax.ShapeDtypeStruct((owned, slots, units), BF16)
    else:
        out_shape = jax.ShapeDtypeStruct((owned, 2, slots, units), F32)
    inputs = [own, *sum([list(r) for r in received], []), in_hbm(gate_up)]
    return pl.pallas_call(
        functools.partial(gate_up_kernel, begin, shares, across, within, first, last),
        grid_spec=pltpu.PrefetchScalarGridSpec(
            num_scalar_prefetch=1,
            grid=(owned, units // tile, shares),
            in_specs=[vmem] * (1 + shares * within)
            + [pl.BlockSpec((1, 2, depth, tile), lambda e, j, i, meta: (e, 0, meta[1 + begin + i], j))]
            + ([] if first else [vmem]),
            out_specs=vmem,
            scratch_shapes=[pltpu.VMEM((shares, owned, slots, depth), BF16)],
        ),
        out_shape=out_shape,
        input_output_aliases={} if first or last else {1 + len(inputs): 0},
        compiler_params=pltpu.CompilerParams(vmem_limit_bytes=STAGE_VMEM),
        cost_estimate=pl.CostEstimate(
            flops=4 * owned * slots * depth * units * shares,
            bytes_accessed=4 * owned * depth * units * shares,
            transcendentals=0,
        ),
        name="gate_up_stage",
    )(meta, *inputs, *([] if first else [sums]))


def fetch_kernel(down_ref, out_ref, sem):
    copies = [
        pltpu.make_async_copy(down_ref.at[e], out_ref.at[e], sem.at[e]) for e in range(down_ref.shape[0])
    ]
    for copy in copies:
        copy.start()
    for copy in copies:
        copy.wait()


def fetch_down(down_weight):
    return pl.pallas_call(
        fetch_kernel,
        in_specs=[pl.BlockSpec(memory_space=pltpu.HBM)],
        out_specs=pl.BlockSpec(memory_space=pltpu.VMEM),
        out_shape=pltpu.VMEM(down_weight.shape, down_weight.dtype),
        scratch_shapes=[pltpu.SemaphoreType.DMA((down_weight.shape[0],))],
        compiler_params=pltpu.CompilerParams(vmem_limit_bytes=SMALL_VMEM),
        cost_estimate=pl.CostEstimate(flops=0, bytes_accessed=2 * down_weight.size, transcendentals=0),
        name="fetch_down",
    )(in_hbm(down_weight))


def down_kernel(share, across, within, per_expert, meta_ref, list_ref, hidden_ref, delta_ref, down_ref, *outs):
    owned, units, _ = down_ref.shape
    cols = outs[0].shape[1]
    src_cols = delta_ref.shape[3]
    groups = hidden_ref.shape[1] // per_expert
    listed = MAXCH * BLOCK_ROWS
    span = BLOCK_ROWS * STRIDE
    row = lax.broadcasted_iota(jnp.int32, (MAXCH * span, listed), 0)
    col = lax.broadcasted_iota(jnp.int32, (MAXCH * span, listed), 1)
    spread = ((row // STRIDE == col) & (row % STRIDE == 0)).astype(F32).astype(BF16)
    unit = lax.broadcasted_iota(jnp.int32, (1, units), 1)
    line = lax.broadcasted_iota(jnp.int32, (units, MAXCH * span), 0)
    place = lax.broadcasted_iota(jnp.int32, (units, MAXCH * span), 1)
    blocks, rest, taken = [], [], []
    for e in range(owned):
        blocks.append([list_ref[(meta_ref[0] * owned + e) * MAXCH + entry] for entry in range(MAXCH)])
        hit = unit // span == blocks[e][0]
        base = jnp.zeros_like(place)
        for entry in range(MAXCH):
            hit = hit | (unit // span == blocks[e][entry])
            base = jnp.where(place // span == entry, blocks[e][entry] * span, base)
        pick = jnp.where(line == base + place % span, 1.0, 0.0).astype(BF16)
        taken.append(jnp.dot(hidden_ref[e], pick, preferred_element_type=F32).astype(BF16))
        rest.append(hidden_ref[e] * jnp.where(hit, 0.0, 1.0).astype(BF16))
    for q in list(range(1, within)) + [0]:
        first_col = (meta_ref[1 + share] * within + meta_ref[1 + across + q]) * cols
        source = first_col // src_cols
        there = pl.ds(pl.multiple_of(first_col - source * src_cols, cols), cols)
        lanes = pl.ds(pl.multiple_of(first_col, cols), cols)
        for e in range(owned):
            added = jnp.dot(spread, delta_ref[source, e, :, there], preferred_element_type=F32)
            old = jnp.concatenate(
                [down_ref[e, pl.ds(pl.multiple_of(b * span, span), span), lanes] for b in blocks[e]], axis=0
            )
            fresh = (old.astype(F32) + added).astype(BF16)
            part = jnp.dot(rest[e], down_ref[e, :, lanes], preferred_element_type=F32)
            part = (part + jnp.dot(taken[e], fresh, preferred_element_type=F32)).astype(BF16)
            for k in range(groups):
                at = (k * owned + e) * per_expert
                outs[q][at : at + per_expert, :] = part[k * per_expert : (k + 1) * per_expert]


def down_pieces(meta, share, across, within, per_expert, block_list, hidden, delta, down_weight, cols):
    owned, units, _ = down_weight.shape
    slots = hidden.shape[1]
    rows = owned * slots
    vmem = pl.BlockSpec(memory_space=pltpu.VMEM)
    return pl.pallas_call(
        functools.partial(down_kernel, share, across, within, per_expert),
        grid_spec=pltpu.PrefetchScalarGridSpec(
            num_scalar_prefetch=2, grid=(), in_specs=[vmem] * 3, out_specs=[vmem] * within
        ),
        out_shape=[jax.ShapeDtypeStruct((rows, cols), BF16)] * within,
        compiler_params=pltpu.CompilerParams(vmem_limit_bytes=SMALL_VMEM),
        cost_estimate=pl.CostEstimate(
            flops=2 * owned * slots * units * cols * within,
            bytes_accessed=2 * owned * units * cols * within,
            transcendentals=0,
        ),
        name="down_mixed",
    )(meta, block_list, hidden, delta, down_weight)


def swap(value, axis, distance):
    return lax.ppermute(value, axis, [(i, i ^ distance) for i in range(lax.axis_size(axis))])


def shift(value, axis, distance):
    size = lax.axis_size(axis)
    return lax.ppermute(value, axis, [(i, (i + distance) % size) for i in range(size)])


def on_device(
    tokens,
    route,
    route_weight,
    gate_up,
    down_weight,
    adam_first,
    adam_second,
    gradient,
    block_list,
    block_count,
):
    groups = lax.axis_size("expert")
    across, within = lax.axis_size("fsdp"), lax.axis_size("tensor")
    at_z, at_f, at_t = lax.axis_index("expert"), lax.axis_index("fsdp"), lax.axis_index("tensor")
    owned = gate_up.shape[0]
    steps, block, width = tokens.shape
    cols = width // (across * within)
    lists = block_list.reshape(-1)
    counts = block_count.reshape(-1)

    meta = jnp.stack(
        [at_z]
        + [at_f ^ r for r in range(across)]
        + [at_t ^ q for q in range(within)]
        + [at_f * within + at_t]
    ).astype(jnp.int32)

    *sends, mine, pick = pack_slots(meta, tokens, route, groups, owned, cols)
    arrived = [shift(send, "expert", k) for k, send in enumerate(sends, 1)]
    delta = listed_deltas(adam_first, adam_second, gradient, lists, counts)
    down_local = fetch_down(down_weight)
    arrived, delta, down_local = lax.optimization_barrier((arrived, delta, down_local))
    away = jnp.stack(arrived)
    by_owner = delta.reshape(groups, owned, *delta.shape[1:])
    incoming = lax.all_to_all(by_owner, "expert", split_axis=0, concat_axis=0, tiled=True)

    def stage(begin, columns, sums, last):
        received = [[c] + [swap(c, "tensor", q) for q in range(1, within)] for c in columns]
        return gate_up_stage(meta, begin, across, mine, received, gate_up, sums, last)

    near = [swap(away, "fsdp", r) for r in range(1, across - 1)]
    sums = stage(0, [away], None, False)
    away, sums = lax.optimization_barrier((away, sums))
    far = swap(away, "fsdp", across - 1)
    near, sums = lax.optimization_barrier((near, sums))
    sums = stage(1, near, sums, False)
    incoming, far, sums = lax.optimization_barrier((incoming, far, sums))
    hidden = stage(across - 1, [far], sums, True)

    def down(r, order):
        pieces = down_pieces(order, r, across, within, steps * CAP, lists, hidden, incoming, down_local, cols)
        return pieces[0], [swap(pieces[q], "tensor", q) for q in range(1, within)]

    def add(*terms):
        total = terms[0].astype(F32)
        for term in terms[1:]:
            total = total + term.astype(F32)
        return total.astype(BF16)

    rows = groups * owned * steps * CAP
    upper, lower = slice(0, rows // 2), slice(rows // 2, rows)

    def summed(pair, at):
        return add(pair[0][at], *[other[at] for other in pair[1]])

    if across == 4:
        far = down(3, meta)
        one = down(1, meta)
        far_up, far_low = summed(far, upper), summed(far, lower)
        order, far_up, far_low = lax.optimization_barrier((meta, far_up, far_low))
        by_one, by_two = swap(far_up, "fsdp", 1), swap(far_low, "fsdp", 2)
        two = down(2, order)
        one_sum = add(one[0], *one[1], jnp.pad(by_two, ((rows // 2, 0), (0, 0))))
        order, one_sum = lax.optimization_barrier((order, one_sum))
        others = [swap(one_sum, "fsdp", 1)]
        own = down(0, order)
        two_sum = add(two[0], *two[1], jnp.pad(by_one, ((0, rows // 2), (0, 0))))
        others.append(swap(two_sum, "fsdp", 2))
    else:
        others = [swap(summed(down(r, meta), slice(0, rows)), "fsdp", r) for r in range(1, across)]
        own = down(0, meta)
    middle = adam_first.shape[0] // 2
    adam_in, own = lax.optimization_barrier(((adam_first, adam_second, gradient), own))
    filled = adam_part(*adam_in, 0, middle)
    parts = add(own[0], *own[1], *others).reshape(groups, rows // groups, cols)
    adam_in, filled, parts = lax.optimization_barrier((adam_in, filled, parts))
    back = [shift(parts[k], "expert", -k) for k in range(1, groups)]
    first_new, second_new = adam_part(*adam_in, middle, adam_first.shape[0], filled)
    return (combine_slots(pick, route_weight, [parts[0], *back]), first_new, second_new)


def solution(mesh):
    return jax.shard_map(
        on_device,
        mesh=mesh,
        in_specs=(
            P(None, "expert", None),
            P(None, "expert", None),
            P(None, "expert", None),
            P("expert", None, None, ("fsdp", "tensor")),
            P("expert", ("fsdp", "tensor"), None),
            P(None, ("fsdp", "tensor"), "expert"),
            P(None, ("fsdp", "tensor"), "expert"),
            P(None, ("fsdp", "tensor"), "expert"),
            P(None, ("fsdp", "tensor"), None),
            P(None, ("fsdp", "tensor")),
        ),
        out_specs=(
            P(None, "expert", ("fsdp", "tensor")),
            P(None, ("fsdp", "tensor"), "expert"),
            P(None, ("fsdp", "tensor"), "expert"),
        ),
        check_vma=False,
    )
```

time: 510 us -> 129 us (0.25)
  waiting for transfers between devices: 252 us -> 12.8 us
  local copies, waits for them, and re-layouts: 108 us -> 23.5 us
  Pallas kernels: 0 us -> 64.8 us
  other arithmetic: 61.2 us -> 0.79 us
  matrix products: 48.5 us -> 0 us
  between operations: 14 us -> 0.91 us
    all_to_all x5 -> x1, waiting for transfers between devices: 116 us -> 0.01 us  [on_device(): lax.all_to_all(by_owner, 'expert', split_axis=0, concat_axis=0, tiled=True)]
    psum x1 -> x0, waiting for transfers between devices: 80.5 us -> none  [on_device(): lax.psum(rounded.astype(jnp.float32).reshape(slots_all, width).astype(jnp...]
    pallas_call x0 -> x13, Pallas kernels: none -> 64.8 us  [the longest x3 24.6 us: gate_up_stage(): pl.pallas_call(functools.partial(gate_up_kernel, begin, shares, across, w...]
    reduce_scatter x2 -> x0, waiting for transfers between devices: 55.6 us -> none  [on_device(): lax.psum_scatter(token_part.astype(jnp.bfloat16), ('fsdp', 'tensor'), sca...]
    reshape x6 -> x1, local copies, waits for them, and re-layouts: 53.7 us -> 0.08 us  [on_device(): lists = block_list.reshape(-1)]
    dot_general x8 -> x0, matrix products: 48.5 us -> none  [the longest x2 28.5 us: on_device(): jnp.einsum('cxed,xgdh->cxegh', slot_block, gate_up, preferred_element_typ...]
    convert_element_type x7 -> x4, other arithmetic: 38 us -> 0.74 us  [add(): return total.astype(BF16)]
    convert_element_type x8 -> x0, local copies, waits for them, and re-layouts: 32.6 us -> none  [the longest x2 26.3 us: on_device(): incoming.astype(jnp.float32)]
  transfers between devices with their start and end apart: 8 -> 22, of which waited for: 8 -> 7; matrix products, arithmetic and copies ran while one was open for 18% -> 1% of each run, Pallas kernels for 0% -> 41%
where the time goes in v2:
time: 129 us; the launch traced here: 128 us
  Pallas kernels  64.8 us (50%)
  starting transfers between devices  25.5 us (20%)
  local copies, waits for them, and re-layouts  23.5 us (18%)
  waiting for transfers between devices  12.8 us (10%)
    pallas_call x3, Pallas kernels, gate_up_stage(): pl.pallas_call(functools.partial(gate_up_kernel, begin, shares, across, w...  24.6 us
    unnamed x25, local copies, waits for them, and re-layouts  23.3 us
    pallas_call x2, Pallas kernels, adam_part(): pl.pallas_call(adam_kernel, grid=(end - begin,), in_specs=[block, block,...  15.1 us
    ppermute x15, waiting for transfers between devices, swap(): lax.ppermute(value, axis, [(i, i ^ distance) for i in range(lax.axis_size...  12.8 us
    ppermute x6, starting transfers between devices, shift(): lax.ppermute(value, axis, [(i, (i + distance) % size) for i in range(size)])  12.6 us
    pallas_call x4, Pallas kernels, down_pieces(): pl.pallas_call(functools.partial(down_kernel, share, across, within, per_...  12.3 us
    ppermute x15, starting transfers between devices, swap(): lax.ppermute(value, axis, [(i, i ^ distance) for i in range(lax.axis_size...  9.31 us
    pallas_call x1, Pallas kernels, fetch_down(): pl.pallas_call(fetch_kernel, in_specs=[pl.BlockSpec(memory_space=pltpu.HB...  5.8 us
  transfers between devices with their start and end apart: 22, of which 7 were waited for; matrix products, arithmetic and copies ran while one was open for 1% of the time, Pallas kernels for 41%

profile of v2, /device:TPU:0, one launch (start us, length us, event | category | flops | bytes accessed | tf_op | source)
XLA Modules:
  0.0 128.3 jit_solution(8452502828378323451)
XLA Ops:
  4.9 3.0 %collective-permute-start = (bf16[128,512]{1,0:T(8,128)(2,1)S(1)}, bf16[128,512]{1,0:T(8,128)(2,1)S(1)}, u32[]{:S(2)}, u32[]{:S(2)}) collective-permute-start(bf16[128,512]{1,0:T(8,128)(2,1)S(1)} %get-tuple-element.51), channel_id=1, source_target_pairs={{0,2},{2,4},{4,6},{6,0},{1,3},{3,5},{5,7},{7,1},{8,10},{10,12},{12... | collective-permute-start | bytes 393224 | tf_op jit(solution)/shard_map/ppermute | solution.py:383
  8.0 2.6 %collective-permute-start.1 = (bf16[128,512]{1,0:T(8,128)(2,1)S(1)}, bf16[128,512]{1,0:T(8,128)(2,1)S(1)}, u32[]{:S(2)}, u32[]{:S(2)}) collective-permute-start(bf16[128,512]{1,0:T(8,128)(2,1)S(1)} %get-tuple-element.52), channel_id=1, source_target_pairs={{0,4},{2,6},{4,0},{6,2},{1,5},{3,7},{5,1},{7,3},{8,12},{10,14},{12... | collective-permute-start | bytes 393224 | tf_op jit(solution)/shard_map/ppermute | solution.py:383
  12.7 5.8 %fetch_down.1.down_ref = bf16[2,1024,4096]{2,1,0:T(8,128)(2,1)S(1)} custom-call(bf16[2,1024,4096]{2,1,0:T(8,128)(2,1)} %down_ref.1), custom_call_target="tpu_custom_call" | custom-call | bytes 16777216 | tf_op jit(solution)/shard_map/fetch_down/pallas_call | solution.py:302
  18.6 5.7 %copy-done = bf16[2,1024,4096]{2,1,0:T(8,128)(2,1)} copy-done((bf16[2,1024,4096]{2,1,0:T(8,128)(2,1)}, bf16[2,1024,4096]{2,1,0:T(8,128)(2,1)S(1)}, u32[]{:S(2)}) %copy-start) | copy-done | bytes 16777240
  24.3 4.4 %listed_deltas.1 = bf16[8,32,1024]{2,1,0:T(8,128)(2,1)} custom-call(s32[32]{0:T(128)S(1)} %reshape.18.list_ref, s32[8]{0:T(128)S(1)} %bitcast.28, f32[8,256,1024]{2,1,0:T(8,128)} %first_ref.3, f32[8,256,1024]{2,1,0:T(8,128)} %second_ref.3, bf16[8,256,1024]{2,1,0:T(8,128)(2,1)} %grad_ref.3), custom_call_target="tpu_custom_call" | custom-call | flops 1000000 | bytes 3145728 | tf_op jit(solution)/shard_map/listed_deltas/pallas_call | solution.py:158
  32.0 6.2 %gate_up_stage.3.refs_5_ = f32[2,2,256,1024]{3,2,1,0:T(8,128)S(1)} custom-call(s32[8]{0:T(128)S(1)} %stack.47.meta_ref, bf16[128,4096]{1,0:T(8,128)(2,1)S(1)} %get-tuple-element.50.own_ref, bf16[3,128,512]{2,1,0:T(8,128)(2,1)S(1)} %pad_maximum_fusion.refs_0_, bf16[3,128,512]{2,1,0:T(8,128)(2,1)S(1)} %collective-permute-done.3.refs_1_, ...), custom_call_target="tpu_custom_call" | custom-call | flops 2147483648 | bytes 8388608 | tf_op jit(solution)/shard_map/gate_up_stage/pallas_call | solution.py:268
  38.2 2.0 %copy-done.2 = f32[2,2,256,1024]{3,2,1,0:T(8,128)} copy-done((f32[2,2,256,1024]{3,2,1,0:T(8,128)}, f32[2,2,256,1024]{3,2,1,0:T(8,128)S(1)}, u32[]{:S(2)}) %copy-start.2) | copy-done | bytes 4194328
  42.1 3.7 %all-to-all-start = ((bf16[4,2,32,1024]{3,2,1,0:T(8,128)(2,1)}), bf16[4,2,32,1024]{3,2,1,0:T(8,128)(2,1)S(1)}, u32[]{:S(2)}, u32[]{:S(2)}) async-start(bf16[4,2,32,1024]{3,2,1,0:T(8,128)(2,1)} %bitcast.11), calls=%async_computation | async-start | bytes 1048576 | tf_op jit(solution)/shard_map/all_to_all | solution.py:421
  47.3 2.2 %copy-done.3 = f32[2,2,256,1024]{3,2,1,0:T(8,128)S(1)} copy-done((f32[2,2,256,1024]{3,2,1,0:T(8,128)S(1)}, f32[2,2,256,1024]{3,2,1,0:T(8,128)}, u32[]{:S(2)}) %copy-start.3) | copy-done | bytes 4194328
  49.5 12.1 %gate_up_stage.4.refs_3_ = f32[2,2,256,1024]{3,2,1,0:T(8,128)S(1)} custom-call(s32[8]{0:T(128)S(1)} %stack.47.meta_ref, bf16[128,4096]{1,0:T(8,128)(2,1)S(1)} %get-tuple-element.50.own_ref, bf16[3,128,512]{2,1,0:T(8,128)(2,1)S(1)} %collective-permute-done.5.refs_0_, ...), custom_call_target="tpu_custom_call", output_to_operand_aliasing={{}: (7, {})} | custom-call | flops 4294967296 | bytes 16777216 | tf_op jit(solution)/shard_map/gate_up_stage/pallas_call | solution.py:268
  61.6 2.0 %copy-done.4 = f32[2,2,256,1024]{3,2,1,0:T(8,128)} copy-done((f32[2,2,256,1024]{3,2,1,0:T(8,128)}, f32[2,2,256,1024]{3,2,1,0:T(8,128)S(1)}, u32[]{:S(2)}) %copy-start.4) | copy-done | bytes 4194328
  65.3 2.2 %copy-done.5 = f32[2,2,256,1024]{3,2,1,0:T(8,128)S(1)} copy-done((f32[2,2,256,1024]{3,2,1,0:T(8,128)S(1)}, f32[2,2,256,1024]{3,2,1,0:T(8,128)}, u32[]{:S(2)}) %copy-start.5) | copy-done | bytes 4194328
  67.5 6.3 %gate_up_stage.5.hidden_ref = bf16[2,256,1024]{2,1,0:T(8,128)(2,1)S(1)} custom-call(s32[8]{0:T(128)S(1)} %stack.47.meta_ref, bf16[128,4096]{1,0:T(8,128)(2,1)S(1)} %get-tuple-element.50.own_ref, bf16[3,128,512]{2,1,0:T(8,128)(2,1)S(1)} %collective-permute-done.4.refs_0_, bf16[3,128,512]{2,1,0:T(8,128)(2,1)S(1)} %collective-permute-done.9.refs_1_, ...), custom_call_target="tpu_custom_call" | custom-call | flops 2147483648 | bytes 8388608 | tf_op jit(solution)/shard_map/gate_up_stage/pallas_call | solution.py:268
  73.8 5.8 %copy-done.1 = bf16[2,1024,4096]{2,1,0:T(8,128)(2,1)S(1)} copy-done((bf16[2,1024,4096]{2,1,0:T(8,128)(2,1)S(1)}, bf16[2,1024,4096]{2,1,0:T(8,128)(2,1)}, u32[]{:S(2)}) %copy-start.1) | copy-done | bytes 16777240
  79.6 3.1 %down_mixed.4 = (bf16[512,512]{1,0:T(8,128)(2,1)S(1)}, bf16[512,512]{1,0:T(8,128)(2,1)S(1)}) custom-call(s32[8]{0:T(128)S(1)} %stack.47.meta_ref, s32[32]{0:T(128)S(1)} %reshape.18.list_ref, bf16[2,256,1024]{2,1,0:T(8,128)(2,1)S(1)} %gate_up_stage.5.hidden_ref, bf16[4,2,32,1024]{3,2,1,0:T(8,128)(2,1)S(1)} %all-to-all-done.delta_ref, ...), custom_call_target="tpu_custom_call" | custom-call | flops 1073741824 | bytes 4194304 | tf_op jit(solution)/shard_map/down_mixed/pallas_call | solution.py:361
  82.9 3.1 %down_mixed.5 = (bf16[512,512]{1,0:T(8,128)(2,1)S(1)}, bf16[512,512]{1,0:T(8,128)(2,1)S(1)}) custom-call(s32[8]{0:T(128)S(1)} %stack.47.meta_ref, s32[32]{0:T(128)S(1)} %reshape.18.list_ref, bf16[2,256,1024]{2,1,0:T(8,128)(2,1)S(1)} %gate_up_stage.5.hidden_ref, bf16[4,2,32,1024]{3,2,1,0:T(8,128)(2,1)S(1)} %all-to-all-done.delta_ref, ...), custom_call_target="tpu_custom_call" | custom-call | flops 1073741824 | bytes 4194304 | tf_op jit(solution)/shard_map/down_mixed/pallas_call | solution.py:361
  88.2 3.1 %down_mixed.7 = (bf16[512,512]{1,0:T(8,128)(2,1)S(1)}, bf16[512,512]{1,0:T(8,128)(2,1)S(1)}) custom-call(s32[8]{0:T(128)S(1)} %stack.47.meta_ref, s32[32]{0:T(128)S(1)} %reshape.18.list_ref, bf16[2,256,1024]{2,1,0:T(8,128)(2,1)S(1)} %gate_up_stage.5.hidden_ref, bf16[4,2,32,1024]{3,2,1,0:T(8,128)(2,1)S(1)} %all-to-all-done.delta_ref, ...), custom_call_target="tpu_custom_call" | custom-call | flops 1073741824 | bytes 4194304 | tf_op jit(solution)/shard_map/down_mixed/pallas_call | solution.py:361
  91.9 3.0 %collective-permute-done.12 = bf16[256,512]{1,0:T(8,128)(2,1)S(1)} collective-permute-done((bf16[256,512]{1,0:T(8,128)(2,1)S(1)}, bf16[256,512]{1,0:T(8,128)(2,1)S(1)}, u32[]{:S(2)}, u32[]{:S(2)}) %collective-permute-start.12) | collective-permute-done | bytes 262176 | tf_op jit(solution)/shard_map/ppermute | solution.py:378
  95.7 3.1 %down_mixed.6 = (bf16[512,512]{1,0:T(8,128)(2,1)S(1)}, bf16[512,512]{1,0:T(8,128)(2,1)S(1)}) custom-call(s32[8]{0:T(128)S(1)} %stack.47.meta_ref, s32[32]{0:T(128)S(1)} %reshape.18.list_ref, bf16[2,256,1024]{2,1,0:T(8,128)(2,1)S(1)} %gate_up_stage.5.hidden_ref, bf16[4,2,32,1024]{3,2,1,0:T(8,128)(2,1)S(1)} %all-to-all-done.delta_ref, ...), custom_call_target="tpu_custom_call" | custom-call | flops 1073741824 | bytes 4194304 | tf_op jit(solution)/shard_map/down_mixed/pallas_call | solution.py:361
  101.2 7.5 %adam_moments.2 = (f32[8,256,1024]{2,1,0:T(8,128)}, f32[8,256,1024]{2,1,0:T(8,128)}) custom-call(f32[8,256,1024]{2,1,0:T(8,128)} %first_ref.3, f32[8,256,1024]{2,1,0:T(8,128)} %second_ref.3, bf16[8,256,1024]{2,1,0:T(8,128)(2,1)} %grad_ref.3), custom_call_target="tpu_custom_call" | custom-call | flops 8388608 | bytes 18874368 | tf_op jit(solution)/shard_map/adam_moments/pallas_call | solution.py:190
  108.8 2.5 %collective-permute-done.14 = bf16[512,512]{1,0:T(8,128)(2,1)S(1)} collective-permute-done((bf16[512,512]{1,0:T(8,128)(2,1)S(1)}, bf16[512,512]{1,0:T(8,128)(2,1)S(1)}, u32[]{:S(2)}, u32[]{:S(2)}) %collective-permute-start.14) | collective-permute-done | bytes 524320 | tf_op jit(solution)/shard_map/ppermute | solution.py:378
  111.3 2.5 %collective-permute-done.17 = bf16[512,512]{1,0:T(8,128)(2,1)S(1)} collective-permute-done((bf16[512,512]{1,0:T(8,128)(2,1)S(1)}, bf16[512,512]{1,0:T(8,128)(2,1)S(1)}, u32[]{:S(2)}, u32[]{:S(2)}) %collective-permute-start.17) | collective-permute-done | bytes 524320 | tf_op jit(solution)/shard_map/ppermute | solution.py:378
  115.9 2.4 %collective-permute-start.19 = (bf16[128,512]{1,0:T(8,128)(2,1)S(1)}, bf16[128,512]{1,0:T(8,128)(2,1)S(1)}, u32[]{:S(2)}, u32[]{:S(2)}) collective-permute-start(bf16[128,512]{1,0:T(8,128)(2,1)S(1)} %get-tuple-element.98), channel_id=1, source_target_pairs={{0,4},{2,6},{4,0},{6,2},{1,5},{3,7},{5,1},{7,3},{8,12},{10,14},{12... | collective-permute-start | bytes 393224 | tf_op jit(solution)/shard_map/ppermute | solution.py:383
  119.8 7.5 %adam_moments.3 = (f32[8,256,1024]{2,1,0:T(8,128)}, f32[8,256,1024]{2,1,0:T(8,128)}) custom-call(f32[8,256,1024]{2,1,0:T(8,128)} %first_ref.3, f32[8,256,1024]{2,1,0:T(8,128)} %second_ref.3, bf16[8,256,1024]{2,1,0:T(8,128)(2,1)} %grad_ref.3, f32[8,256,1024]{2,1,0:T(8,128)} %get-tuple-element.91.refs_0_, ...), custom_call_target="tpu_custom_call", output_to_operand_aliasing={{0}: (3, {}), {1}: (4, {})} | custom-call | flops 8388608 | bytes 18874368 | tf_op jit(solution)/shard_map/adam_moments/pallas_call | solution.py:190
  (66 shorter events, 25.6 us)
Async XLA Ops:
  4.9 23.8 %collective-permute-start = (bf16[128,512]{1,0:T(8,128)(2,1)S(1)}, bf16[128,512]{1,0:T(8,128)(2,1)S(1)}, u32[]{:S(2)}, u32[]{:S(2)}) collective-permute-start(bf16[128,512]{1,0:T(8,128)(2,1)S(1)} %get-tuple-element.51), channel_id=1, source_target_pairs={{0,2},{2,4},{4,6},{6,0},{1,3},{3,5},{5,7},{7,1},{8,10},{10,12},{12... | collective-permute-start | bytes 393224 | tf_op jit(solution)/shard_map/ppermute | solution.py:383
  8.0 20.7 %collective-permute-start.1 = (bf16[128,512]{1,0:T(8,128)(2,1)S(1)}, bf16[128,512]{1,0:T(8,128)(2,1)S(1)}, u32[]{:S(2)}, u32[]{:S(2)}) collective-permute-start(bf16[128,512]{1,0:T(8,128)(2,1)S(1)} %get-tuple-element.52), channel_id=1, source_target_pairs={{0,4},{2,6},{4,0},{6,2},{1,5},{3,7},{5,1},{7,3},{8,12},{10,14},{12... | collective-permute-start | bytes 393224 | tf_op jit(solution)/shard_map/ppermute | solution.py:383
  10.5 18.2 %collective-permute-start.2 = (bf16[128,512]{1,0:T(8,128)(2,1)S(1)}, bf16[128,512]{1,0:T(8,128)(2,1)S(1)}, u32[]{:S(2)}, u32[]{:S(2)}) collective-permute-start(bf16[128,512]{1,0:T(8,128)(2,1)S(1)} %get-tuple-element.53), channel_id=1, source_target_pairs={{0,6},{2,0},{4,2},{6,4},{1,7},{3,1},{5,3},{7,5},{8,14},{10,8},{12,... | collective-permute-start | bytes 393224 | tf_op jit(solution)/shard_map/ppermute | solution.py:383
  12.7 11.6 %copy-start.11 = (s32[8,1]{0,1:T(1,128)S(1)}, s32[8,1]{0,1:T(1,128)}, u32[]{:S(2)}) copy-start(s32[8,1]{0,1:T(1,128)} %param.19) | copy-start | bytes 100
  28.8 3.2 %collective-permute-start.3 = (bf16[3,128,512]{2,1,0:T(8,128)(2,1)S(1)}, bf16[3,128,512]{2,1,0:T(8,128)(2,1)S(1)}, u32[]{:S(2)}, u32[]{:S(2)}) collective-permute-start(bf16[3,128,512]{2,1,0:T(8,128)(2,1)S(1)} %pad_maximum_fusion.refs_0_), channel_id=1, source_target_pairs={{0,1},{1,0},{2,3},{3,2},{4,5},{5,4},{6,7},{7,6},{8,9},{9,8},{10,11... | collective-permute-start | bytes 1179656 | tf_op jit(solution)/shard_map/ppermute | solution.py:378
  28.9 11.5 %collective-permute-start.6 = (bf16[3,128,512]{2,1,0:T(8,128)(2,1)S(1)}, bf16[3,128,512]{2,1,0:T(8,128)(2,1)S(1)}, u32[]{:S(2)}, u32[]{:S(2)}) collective-permute-start(bf16[3,128,512]{2,1,0:T(8,128)(2,1)S(1)} %pad_maximum_fusion.refs_0_), channel_id=1, source_target_pairs={{0,16},{8,24},{16,0},{24,8},{1,17},{9,25},{17,1},{25,9},{2,18},{10... | collective-permute-start | bytes 1179656 | tf_op jit(solution)/shard_map/ppermute | solution.py:378
  30.4 11.2 %collective-permute-start.5 = (bf16[3,128,512]{2,1,0:T(8,128)(2,1)S(1)}, bf16[3,128,512]{2,1,0:T(8,128)(2,1)S(1)}, u32[]{:S(2)}, u32[]{:S(2)}) collective-permute-start(bf16[3,128,512]{2,1,0:T(8,128)(2,1)S(1)} %pad_maximum_fusion.refs_0_), channel_id=1, source_target_pairs={{0,8},{8,0},{16,24},{24,16},{1,9},{9,1},{17,25},{25,17},{2,10},{10... | collective-permute-start | bytes 1179656 | tf_op jit(solution)/shard_map/ppermute | solution.py:378
  41.6 5.7 %collective-permute-start.7 = (bf16[3,128,512]{2,1,0:T(8,128)(2,1)S(1)}, bf16[3,128,512]{2,1,0:T(8,128)(2,1)S(1)}, u32[]{:S(2)}, u32[]{:S(2)}) collective-permute-start(bf16[3,128,512]{2,1,0:T(8,128)(2,1)S(1)} %collective-permute-done.5.refs_0_), channel_id=1, source_target_pairs={{0,1},{1,0},{2,3},{3,2},{4,5},{5,4},{6,7},{7,6},{8,9},{9,8},{10,11... | collective-permute-start | bytes 1179656 | tf_op jit(solution)/shard_map/ppermute | solution.py:378
  41.6 5.7 %collective-permute-start.8 = (bf16[3,128,512]{2,1,0:T(8,128)(2,1)S(1)}, bf16[3,128,512]{2,1,0:T(8,128)(2,1)}, u32[]{:S(2)}, u32[]{:S(2)}) collective-permute-start(bf16[3,128,512]{2,1,0:T(8,128)(2,1)S(1)} %collective-permute-done.6.refs_2_), channel_id=1, source_target_pairs={{0,1},{1,0},{2,3},{3,2},{4,5},{5,4},{6,7},{7,6},{8,9},{9,8},{10,11... | collective-permute-start | bytes 1179656 | tf_op jit(solution)/shard_map/ppermute | solution.py:378
  42.1 21.5 %all-to-all-start = ((bf16[4,2,32,1024]{3,2,1,0:T(8,128)(2,1)}), bf16[4,2,32,1024]{3,2,1,0:T(8,128)(2,1)S(1)}, u32[]{:S(2)}, u32[]{:S(2)}) async-start(bf16[4,2,32,1024]{3,2,1,0:T(8,128)(2,1)} %bitcast.11), calls=%async_computation | async-start | bytes 1048576 | tf_op jit(solution)/shard_map/all_to_all | solution.py:421
  45.8 17.8 %collective-permute-start.4 = (bf16[3,128,512]{2,1,0:T(8,128)(2,1)S(1)}, bf16[3,128,512]{2,1,0:T(8,128)(2,1)S(1)}, u32[]{:S(2)}, u32[]{:S(2)}) collective-permute-start(bf16[3,128,512]{2,1,0:T(8,128)(2,1)S(1)} %pad_maximum_fusion.refs_0_), channel_id=1, source_target_pairs={{0,24},{8,16},{16,8},{24,0},{1,25},{9,17},{17,9},{25,1},{2,26},{10... | collective-permute-start | bytes 1179656 | tf_op jit(solution)/shard_map/ppermute | solution.py:378
  63.6 1.7 %collective-permute-start.9 = (bf16[3,128,512]{2,1,0:T(8,128)(2,1)S(1)}, bf16[3,128,512]{2,1,0:T(8,128)(2,1)S(1)}, u32[]{:S(2)}, u32[]{:S(2)}) collective-permute-start(bf16[3,128,512]{2,1,0:T(8,128)(2,1)S(1)} %collective-permute-done.4.refs_0_), channel_id=1, source_target_pairs={{0,1},{1,0},{2,3},{3,2},{4,5},{5,4},{6,7},{7,6},{8,9},{9,8},{10,11... | collective-permute-start | bytes 1179656 | tf_op jit(solution)/shard_map/ppermute | solution.py:378
  82.7 3.7 %collective-permute-start.10 = (bf16[512,512]{1,0:T(8,128)(2,1)S(1)}, bf16[512,512]{1,0:T(8,128)(2,1)S(1)}, u32[]{:S(2)}, u32[]{:S(2)}) collective-permute-start(bf16[512,512]{1,0:T(8,128)(2,1)S(1)} %get-tuple-element.68), channel_id=1, source_target_pairs={{0,1},{1,0},{2,3},{3,2},{4,5},{5,4},{6,7},{7,6},{8,9},{9,8},{10,11... | collective-permute-start | bytes 1572872 | tf_op jit(solution)/shard_map/ppermute | solution.py:378
  86.0 6.0 %collective-permute-start.11 = (bf16[512,512]{1,0:T(8,128)(2,1)S(1)}, bf16[512,512]{1,0:T(8,128)(2,1)S(1)}, u32[]{:S(2)}, u32[]{:S(2)}) collective-permute-start(bf16[512,512]{1,0:T(8,128)(2,1)S(1)} %get-tuple-element.71), channel_id=1, source_target_pairs={{0,1},{1,0},{2,3},{3,2},{4,5},{5,4},{6,7},{7,6},{8,9},{9,8},{10,11... | collective-permute-start | bytes 1572872 | tf_op jit(solution)/shard_map/ppermute | solution.py:378
  86.5 8.4 %collective-permute-start.12 = (bf16[256,512]{1,0:T(8,128)(2,1)S(1)}, bf16[256,512]{1,0:T(8,128)(2,1)S(1)}, u32[]{:S(2)}, u32[]{:S(2)}) collective-permute-start(bf16[256,512]{1,0:T(8,128)(2,1)S(1)} %get-tuple-element.72), channel_id=1, source_target_pairs={{0,16},{8,24},{16,0},{24,8},{1,17},{9,25},{17,1},{25,9},{2,18},{10... | collective-permute-start | bytes 786440 | tf_op jit(solution)/shard_map/ppermute | solution.py:378
  91.3 9.3 %collective-permute-start.15 = (bf16[512,512]{1,0:T(8,128)(2,1)S(1)}, bf16[512,512]{1,0:T(8,128)(2,1)S(1)}, u32[]{:S(2)}, u32[]{:S(2)}) collective-permute-start(bf16[512,512]{1,0:T(8,128)(2,1)S(1)} %get-tuple-element.85), channel_id=1, source_target_pairs={{0,1},{1,0},{2,3},{3,2},{4,5},{5,4},{6,7},{7,6},{8,9},{9,8},{10,11... | collective-permute-start | bytes 1572872 | tf_op jit(solution)/shard_map/ppermute | solution.py:378
  91.4 9.2 %collective-permute-start.16 = (bf16[256,512]{1,0:T(8,128)(2,1)S(1)}, bf16[256,512]{1,0:T(8,128)(2,1)S(1)}, u32[]{:S(2)}, u32[]{:S(2)}) collective-permute-start(bf16[256,512]{1,0:T(8,128)(2,1)S(1)} %get-tuple-element.86), channel_id=1, source_target_pairs={{0,8},{8,0},{16,24},{24,16},{1,9},{9,1},{17,25},{25,17},{2,10},{10... | collective-permute-start | bytes 786440 | tf_op jit(solution)/shard_map/ppermute | solution.py:378
  95.1 16.2 %collective-permute-start.14 = (bf16[512,512]{1,0:T(8,128)(2,1)S(1)}, bf16[512,512]{1,0:T(8,128)(2,1)S(1)}, u32[]{:S(2)}, u32[]{:S(2)}) collective-permute-start(bf16[512,512]{1,0:T(8,128)(2,1)S(1)} %add_convert_fusion.2), channel_id=1, source_target_pairs={{0,8},{8,0},{16,24},{24,16},{1,9},{9,1},{17,25},{25,17},{2,10},{10... | collective-permute-start | bytes 1572872 | tf_op jit(solution)/shard_map/ppermute | solution.py:378
  98.8 2.4 %collective-permute-start.13 = (bf16[512,512]{1,0:T(8,128)(2,1)S(1)}, bf16[512,512]{1,0:T(8,128)(2,1)S(1)}, u32[]{:S(2)}, u32[]{:S(2)}) collective-permute-start(bf16[512,512]{1,0:T(8,128)(2,1)S(1)} %get-tuple-element.75), channel_id=1, source_target_pairs={{0,1},{1,0},{2,3},{3,2},{4,5},{5,4},{6,7},{7,6},{8,9},{9,8},{10,11... | collective-permute-start | bytes 1572872 | tf_op jit(solution)/shard_map/ppermute | solution.py:378
  100.7 13.1 %collective-permute-start.17 = (bf16[512,512]{1,0:T(8,128)(2,1)S(1)}, bf16[512,512]{1,0:T(8,128)(2,1)S(1)}, u32[]{:S(2)}, u32[]{:S(2)}) collective-permute-start(bf16[512,512]{1,0:T(8,128)(2,1)S(1)} %add_convert_fusion.1), channel_id=1, source_target_pairs={{0,16},{8,24},{16,0},{24,8},{1,17},{9,25},{17,1},{25,9},{2,18},{10... | collective-permute-start | bytes 1572872 | tf_op jit(solution)/shard_map/ppermute | solution.py:378
  114.1 13.2 %collective-permute-start.20 = (bf16[128,512]{1,0:T(8,128)(2,1)S(1)}, bf16[128,512]{1,0:T(8,128)(2,1)S(1)}, u32[]{:S(2)}, u32[]{:S(2)}) collective-permute-start(bf16[128,512]{1,0:T(8,128)(2,1)S(1)} %get-tuple-element.97), channel_id=1, source_target_pairs={{0,2},{2,4},{4,6},{6,0},{1,3},{3,5},{5,7},{7,1},{8,10},{10,12},{12... | collective-permute-start | bytes 393224 | tf_op jit(solution)/shard_map/ppermute | solution.py:383
  115.9 11.4 %collective-permute-start.19 = (bf16[128,512]{1,0:T(8,128)(2,1)S(1)}, bf16[128,512]{1,0:T(8,128)(2,1)S(1)}, u32[]{:S(2)}, u32[]{:S(2)}) collective-permute-start(bf16[128,512]{1,0:T(8,128)(2,1)S(1)} %get-tuple-element.98), channel_id=1, source_target_pairs={{0,4},{2,6},{4,0},{6,2},{1,5},{3,7},{5,1},{7,3},{8,12},{10,14},{12... | collective-permute-start | bytes 393224 | tf_op jit(solution)/shard_map/ppermute | solution.py:383
  118.3 9.1 %copy-start.10 = (f32[2,64,2]{1,2,0:T(2,128)S(1)}, f32[2,64,2]{1,2,0:T(2,128)}, u32[]{:S(2)}) copy-start(f32[2,64,2]{1,2,0:T(2,128)} %param.12) | copy-start | bytes 3076
  118.3 9.0 %collective-permute-start.18 = (bf16[128,512]{1,0:T(8,128)(2,1)S(1)}, bf16[128,512]{1,0:T(8,128)(2,1)S(1)}, u32[]{:S(2)}, u32[]{:S(2)}) collective-permute-start(bf16[128,512]{1,0:T(8,128)(2,1)S(1)} %get-tuple-element.99), channel_id=1, source_target_pairs={{0,6},{2,0},{4,2},{6,4},{1,7},{3,1},{5,3},{7,5},{8,14},{10,8},{12,... | collective-permute-start | bytes 393224 | tf_op jit(solution)/shard_map/ppermute | solution.py:383
  (10 other events, 31.6 us)

commit v3 on v2

v3 whole, which is shorter than its diff:
```python
import functools

import jax
import jax.numpy as jnp
from jax import lax
from jax.experimental import pallas as pl
from jax.experimental.pallas import tpu as pltpu
from jax.sharding import PartitionSpec as P

STRIDE = 4
BLOCK_ROWS = 8
MAXCH = 4
CAP = 32
PIECES = 2
UNIT_TILE = 256

BETA_ONE = 0.9
BETA_TWO = 0.95
LEARN_RATE = 0.03
ADAM_EPS = 1e-08
FIRST_FIX = 1.0 - 0.9**10
SECOND_FIX = 1.0 - 0.95**10

SHORT = pl.CostEstimate(flops=1, bytes_accessed=1, transcendentals=0)

F32 = jnp.float32
BF16 = jnp.bfloat16
SMALL_VMEM = 16 * 2**20
STAGE_VMEM = 20 * 2**20


def in_hbm(value):
    return pltpu.with_memory_space_constraint(value, pltpu.HBM)


def as_column(ref, k):
    row = jnp.concatenate([ref[s, k : k + 1, :].astype(F32) for s in range(ref.shape[0])], axis=1)
    return jnp.transpose(jnp.broadcast_to(row, (row.shape[1], row.shape[1])))[:, 0:1]


def pack_kernel(groups, owned, block, meta_ref, tokens_ref, route_ref, *refs):
    sends, (select_ref, pick_ref, share, sem) = refs[: groups - 1], refs[groups - 1 :]
    rows, cols = share.shape
    steps = rows // block
    lanes = pl.ds(pl.multiple_of(meta_ref[meta_ref.shape[0] - 1] * cols, cols), cols)
    copies = [
        pltpu.make_async_copy(tokens_ref.at[s, :, lanes], share.at[pl.ds(s * block, block)], sem.at[s])
        for s in range(steps)
    ]
    for copy in copies:
        copy.start()
    per_expert = steps * CAP
    per_group = owned * per_expert
    slots = groups * per_group
    token = lax.broadcasted_iota(jnp.int32, (rows, rows), 0)
    lane = lax.broadcasted_iota(jnp.int32, (rows, rows), 1)
    before = jnp.where((lane < token) & (lane // block == token // block), 1.0, 0.0).astype(BF16)
    named = [as_column(route_ref, k) for k in range(2)]
    lane = lane.astype(F32)
    member = jnp.where((lane == named[0]) | (lane == named[1]), 1.0, 0.0).astype(BF16)
    earlier = jnp.dot(before, member, preferred_element_type=F32)
    slot = lax.broadcasted_iota(jnp.int32, (rows, slots), 1)
    step = lax.broadcasted_iota(jnp.int32, (rows, slots), 0) // block
    group = (meta_ref[0] + slot // per_group) % groups
    expert = (group * owned + slot % per_group // per_expert).astype(F32)
    here = slot % per_expert // CAP == step
    spot = (slot % CAP).astype(F32)
    total = jnp.zeros((rows, slots), F32)
    for k in range(2):
        position = jnp.sum(jnp.where(lane == named[k], earlier, 0.0), axis=1, keepdims=True)
        pick = jnp.where((expert == named[k]) & here & (spot == position), 1.0, 0.0)
        pick_ref[k] = pick.astype(BF16)
        total = total + pick
    select = jnp.transpose(total).astype(BF16)
    select_ref[...] = select[:per_group]
    for copy in copies:
        copy.wait()
    for k in range(1, groups):
        sends[k - 1][...] = jnp.dot(
            select[k * per_group : (k + 1) * per_group], share[...], preferred_element_type=F32
        ).astype(BF16)


def pack_slots(meta, tokens, route, groups, owned, cols):
    steps, block, width = tokens.shape
    rows = steps * block
    per_group = owned * steps * CAP
    vmem = pl.BlockSpec(memory_space=pltpu.VMEM)
    return pl.pallas_call(
        functools.partial(pack_kernel, groups, owned, block),
        grid_spec=pltpu.PrefetchScalarGridSpec(
            num_scalar_prefetch=1,
            grid=(),
            in_specs=[pl.BlockSpec(memory_space=pltpu.HBM), vmem],
            out_specs=[vmem] * (groups + 1),
            scratch_shapes=[pltpu.VMEM((rows, cols), BF16), pltpu.SemaphoreType.DMA((steps,))],
        ),
        out_shape=[jax.ShapeDtypeStruct((per_group, cols), BF16)] * (groups - 1)
        + [
            jax.ShapeDtypeStruct((per_group, rows), BF16),
            jax.ShapeDtypeStruct((2, rows, groups * per_group), BF16),
        ],
        compiler_params=pltpu.CompilerParams(vmem_limit_bytes=SMALL_VMEM),
        cost_estimate=pl.CostEstimate(flops=10**7, bytes_accessed=4 * rows * cols, transcendentals=0),
        name="pack_slots",
    )(meta, in_hbm(tokens), route.transpose(0, 2, 1))


def own_kernel(select_ref, tokens_ref, out_ref):
    every = jnp.concatenate([tokens_ref[s] for s in range(tokens_ref.shape[0])], axis=0)
    out_ref[...] = jnp.dot(select_ref[...], every, preferred_element_type=F32).astype(BF16)


def own_slots(select, tokens):
    vmem = pl.BlockSpec(memory_space=pltpu.VMEM)
    return pl.pallas_call(
        own_kernel,
        in_specs=[vmem, vmem],
        out_specs=vmem,
        out_shape=jax.ShapeDtypeStruct((select.shape[0], tokens.shape[2]), BF16),
        compiler_params=pltpu.CompilerParams(vmem_limit_bytes=SMALL_VMEM),
        cost_estimate=pl.CostEstimate(flops=10**8, bytes_accessed=4 * tokens.size, transcendentals=0),
        name="own_slots",
    )(select, tokens)


def combine_kernel(pick_ref, weight_ref, *refs):
    out_ref = refs[-1]
    steps, block, _ = out_ref.shape
    rows = jnp.concatenate([ref[...] for ref in refs[:-1]], axis=0)
    total = jnp.zeros((steps * block, out_ref.shape[2]), F32)
    for k in range(2):
        total = total + as_column(weight_ref, k) * jnp.dot(pick_ref[k], rows, preferred_element_type=F32)
    for s in range(steps):
        out_ref[s] = total[s * block : (s + 1) * block].astype(BF16)


def combine_slots(pick, weight, parts):
    steps, block, _ = weight.shape
    cols = parts[0].shape[1]
    vmem = pl.BlockSpec(memory_space=pltpu.VMEM)
    return pl.pallas_call(
        combine_kernel,
        in_specs=[vmem] * (2 + len(parts)),
        out_specs=vmem,
        out_shape=jax.ShapeDtypeStruct((steps, block, cols), BF16),
        compiler_params=pltpu.CompilerParams(vmem_limit_bytes=SMALL_VMEM),
        cost_estimate=pl.CostEstimate(flops=10**7, bytes_accessed=10**6, transcendentals=0),
        name="combine_slots",
    )(pick, weight.transpose(0, 2, 1), *parts)


def delta_kernel(groups, meta_ref, list_ref, count_ref, first_ref, second_ref, grad_ref, *refs):
    outs, (first_buf, second_buf, grad_buf, sem) = refs[:groups], refs[groups:]
    owned = outs[0].shape[0]

    def copies(at, entry):
        expert = lax.rem(meta_ref[0] + at // owned, groups) * owned + at % owned
        block = list_ref[expert, entry]
        rows = pl.ds(pl.multiple_of(block * BLOCK_ROWS, BLOCK_ROWS), BLOCK_ROWS)
        pair = pl.ds(pl.multiple_of(block // 2 * (2 * BLOCK_ROWS), 2 * BLOCK_ROWS), 2 * BLOCK_ROWS)
        return (
            pltpu.make_async_copy(first_ref.at[expert, rows, :], first_buf.at[at, entry], sem.at[0, at, entry]),
            pltpu.make_async_copy(second_ref.at[expert, rows, :], second_buf.at[at, entry], sem.at[1, at, entry]),
            pltpu.make_async_copy(grad_ref.at[expert, pair, :], grad_buf.at[at, entry], sem.at[2, at, entry]),
        )

    order = [(k % groups) * owned + e for k in range(1, groups + 1) for e in range(owned)]
    for at in order:
        for entry in range(MAXCH):
            for copy in copies(at, entry):
                copy.start()
    for at in order:
        expert = lax.rem(meta_ref[0] + at // owned, groups) * owned + at % owned
        parts = []
        for entry in range(MAXCH):
            for copy in copies(at, entry):
                copy.wait()
            odd = list_ref[expert, entry] % 2 == 1
            grads = grad_buf[at, entry].astype(F32)
            grad = jnp.where(odd, grads[BLOCK_ROWS:], grads[:BLOCK_ROWS])
            first = BETA_ONE * first_buf[at, entry] + (1.0 - BETA_ONE) * grad
            second = BETA_TWO * second_buf[at, entry] + (1.0 - BETA_TWO) * grad * grad
            step = LEARN_RATE * (first / FIRST_FIX) / (jnp.sqrt(second / SECOND_FIX) + ADAM_EPS)
            parts.append(jnp.where(entry < count_ref[expert], -step, 0.0))
        outs[at // owned][at % owned] = jnp.concatenate(parts, axis=0).astype(BF16)


def listed_deltas(meta, adam_first, adam_second, gradient, block_list, block_count, groups):
    experts, _, cols = adam_first.shape
    hbm = pl.BlockSpec(memory_space=pltpu.HBM)
    return pl.pallas_call(
        functools.partial(delta_kernel, groups),
        grid_spec=pltpu.PrefetchScalarGridSpec(
            num_scalar_prefetch=3,
            grid=(),
            in_specs=[hbm, hbm, hbm],
            out_specs=[pl.BlockSpec(memory_space=pltpu.VMEM)] * groups,
            scratch_shapes=[
                pltpu.VMEM((experts, MAXCH, BLOCK_ROWS, cols), F32),
                pltpu.VMEM((experts, MAXCH, BLOCK_ROWS, cols), F32),
                pltpu.VMEM((experts, MAXCH, 2 * BLOCK_ROWS, cols), BF16),
                pltpu.SemaphoreType.DMA((3, experts, MAXCH)),
            ],
        ),
        out_shape=[jax.ShapeDtypeStruct((experts // groups, MAXCH * BLOCK_ROWS, cols), BF16)] * groups,
        compiler_params=pltpu.CompilerParams(vmem_limit_bytes=SMALL_VMEM),
        cost_estimate=pl.CostEstimate(flops=10**6, bytes_accessed=experts * MAXCH * 96 * cols, transcendentals=0),
        name="listed_deltas",
    )(meta, block_list, block_count, in_hbm(adam_first), in_hbm(adam_second), in_hbm(gradient))


def adam_kernel(first_ref, second_ref, grad_ref, *refs):
    first_out, second_out = refs[-2:]
    grad = grad_ref[...].astype(F32)
    first_out[...] = BETA_ONE * first_ref[...] + (1.0 - BETA_ONE) * grad
    second_out[...] = BETA_TWO * second_ref[...] + (1.0 - BETA_TWO) * grad * grad


def adam_part(adam_first, adam_second, gradient, begin, end, filled=(), cost=None):
    _, rows, cols = adam_first.shape
    block = pl.BlockSpec((1, rows, cols), lambda e: (begin + e, 0, 0))
    size = (end - begin) * rows * cols
    return pl.pallas_call(
        adam_kernel,
        grid=(end - begin,),
        in_specs=[block, block, block] + [pl.BlockSpec(memory_space=pltpu.HBM)] * len(filled),
        out_specs=[block, block],
        out_shape=[jax.ShapeDtypeStruct(adam_first.shape, F32)] * 2,
        input_output_aliases={3 + i: i for i in range(len(filled))},
        compiler_params=pltpu.CompilerParams(vmem_limit_bytes=SMALL_VMEM),
        cost_estimate=cost or pl.CostEstimate(flops=8 * size, bytes_accessed=18 * size, transcendentals=0),
        name="adam_moments",
    )(in_hbm(adam_first), in_hbm(adam_second), in_hbm(gradient), *filled)


def gate_up_kernel(begin, shares, across, within, first, last, meta_ref, list_ref, own_ref, *refs):
    recv = [refs[i * within : (i + 1) * within] for i in range(shares)]
    refs = refs[shares * within :]
    weights, refs = refs[:shares], refs[shares:]
    sums_ref, refs = (None, refs) if first else (refs[0], refs[1:])
    out_ref, taken_ref, rows_ref = (refs[0], None, refs[1]) if not last else refs
    expert = pl.program_id(0)
    owned, slots = rows_ref.shape[1:3]
    tile = weights[0].shape[3]
    cols = recv[0][0].shape[2]
    per_expert = own_ref.shape[0] // owned
    groups = slots // per_expert

    @pl.when((expert == 0) & (pl.program_id(1) == 0))
    def _():
        for i in range(shares):
            for q in range(within):
                place = meta_ref[1 + across + q]
                start = (meta_ref[1 + begin + i] * within + place) * cols
                lanes = pl.ds(pl.multiple_of(start, cols), cols)
                into = pl.ds(pl.multiple_of(place * cols, cols), cols)
                for e in range(owned):
                    mine = slice(e * per_expert, (e + 1) * per_expert)
                    rows_ref[i, e, 0:per_expert, into] = own_ref[mine, lanes]
                    for k in range(1, groups):
                        rows_ref[i, e, k * per_expert : (k + 1) * per_expert, into] = recv[i][q][k - 1, mine, :]

    first_unit = pl.program_id(1) * tile
    units = pl.ds(pl.multiple_of(first_unit, tile), tile)

    def product(side):
        total = jnp.dot(rows_ref[0, expert], weights[0][0, side], preferred_element_type=F32)
        for i in range(1, shares):
            total = total + jnp.dot(rows_ref[i, expert], weights[i][0, side], preferred_element_type=F32)
        return total if first else total + sums_ref[expert, side, :, units]

    if not last:
        for side in range(2):
            out_ref[expert, side, :, units] = product(side)
        return
    gate, up = product(0), product(1)
    hidden = (gate * jax.nn.sigmoid(gate) * up).astype(BF16)
    span = BLOCK_ROWS * STRIDE
    unit = first_unit + lax.broadcasted_iota(jnp.int32, (1, tile), 1)
    line = first_unit + lax.broadcasted_iota(jnp.int32, (tile, MAXCH * span), 0)
    place = lax.broadcasted_iota(jnp.int32, (tile, MAXCH * span), 1)
    hit = unit < 0
    source = place % span
    for entry in range(MAXCH):
        block = list_ref[meta_ref[0] * owned + expert, entry]
        hit = hit | (unit // span == block)
        source = source + jnp.where(place // span == entry, block * span, 0)
    pick = jnp.where(line == source, 1.0, 0.0).astype(BF16)
    taken = jnp.dot(hidden, pick, preferred_element_type=F32).astype(BF16)
    out_ref[expert, :, units] = hidden * jnp.where(hit, 0.0, 1.0).astype(BF16)

    @pl.when(pl.program_id(1) == 0)
    def _():
        taken_ref[expert] = taken

    @pl.when(pl.program_id(1) > 0)
    def _():
        taken_ref[expert] += taken


def gate_up_stage(meta, block_list, begin, across, own, received, gate_up, sums, last):
    owned, _, width, units = gate_up.shape
    shares, within = len(received), len(received[0])
    depth = within * received[0][0].shape[2]
    slots = own.shape[0] // owned * (1 + received[0][0].shape[0])
    tile = min(UNIT_TILE, units)
    vmem = pl.BlockSpec(memory_space=pltpu.VMEM)
    first = sums is None
    if last:
        out_shape = [
            jax.ShapeDtypeStruct((owned, slots, units), BF16),
            jax.ShapeDtypeStruct((owned, slots, MAXCH * BLOCK_ROWS * STRIDE), BF16),
        ]
    else:
        out_shape = [jax.ShapeDtypeStruct((owned, 2, slots, units), F32)]
    weights = [
        pl.BlockSpec((1, 2, depth, tile), lambda e, j, meta, _, i=i: (e, 0, meta[1 + begin + i], j))
        for i in range(shares)
    ]
    inputs = [own, *sum([list(r) for r in received], []), *[in_hbm(gate_up)] * shares]
    return pl.pallas_call(
        functools.partial(gate_up_kernel, begin, shares, across, within, first, last),
        grid_spec=pltpu.PrefetchScalarGridSpec(
            num_scalar_prefetch=2,
            grid=(owned, units // tile),
            in_specs=[vmem] * (1 + shares * within) + weights + ([] if first else [vmem]),
            out_specs=[vmem] * len(out_shape),
            scratch_shapes=[pltpu.VMEM((shares, owned, slots, depth), BF16)],
        ),
        out_shape=out_shape,
        input_output_aliases={} if first or last else {2 + len(inputs): 0},
        compiler_params=pltpu.CompilerParams(vmem_limit_bytes=STAGE_VMEM),
        cost_estimate=pl.CostEstimate(
            flops=4 * owned * slots * depth * units * shares,
            bytes_accessed=4 * owned * depth * units * shares,
            transcendentals=0,
        ),
        name="gate_up_stage",
    )(meta, block_list, *inputs, *([] if first else [sums]))


def fetch_kernel(down_ref, out_ref, sem):
    copies = [
        pltpu.make_async_copy(down_ref.at[e], out_ref.at[e], sem.at[e]) for e in range(down_ref.shape[0])
    ]
    for copy in copies:
        copy.start()
    for copy in copies:
        copy.wait()


def fetch_down(down_weight):
    return pl.pallas_call(
        fetch_kernel,
        in_specs=[pl.BlockSpec(memory_space=pltpu.HBM)],
        out_specs=pl.BlockSpec(memory_space=pltpu.VMEM),
        out_shape=pltpu.VMEM(down_weight.shape, down_weight.dtype),
        scratch_shapes=[pltpu.SemaphoreType.DMA((down_weight.shape[0],))],
        compiler_params=pltpu.CompilerParams(vmem_limit_bytes=SMALL_VMEM),
        cost_estimate=pl.CostEstimate(flops=0, bytes_accessed=2 * down_weight.size, transcendentals=0),
        name="fetch_down",
    )(in_hbm(down_weight))


def down_kernel(share, across, within, per_expert, meta_ref, list_ref, rest_ref, taken_ref, delta_ref, down_ref, *outs):
    owned = down_ref.shape[0]
    rows, cols = outs[0].shape
    src_cols = delta_ref.shape[3]
    groups = rest_ref.shape[1] // per_expert
    listed = MAXCH * BLOCK_ROWS
    span = BLOCK_ROWS * STRIDE
    row = lax.broadcasted_iota(jnp.int32, (MAXCH * span, listed), 0)
    col = lax.broadcasted_iota(jnp.int32, (MAXCH * span, listed), 1)
    spread = ((row // STRIDE == col) & (row % STRIDE == 0)).astype(F32).astype(BF16)
    for q in list(range(1, within)) + [0]:
        first_col = (meta_ref[1 + share] * within + meta_ref[1 + across + q]) * cols
        source = first_col // src_cols
        there = pl.ds(pl.multiple_of(first_col - source * src_cols, cols), cols)
        lanes = pl.ds(pl.multiple_of(first_col, cols), cols)
        distance = lax.rem(meta_ref[0] - source + groups, groups)
        for e in range(owned):
            added = jnp.dot(spread, delta_ref[distance, e, :, there], preferred_element_type=F32)
            old = []
            for entry in range(MAXCH):
                block = list_ref[meta_ref[0] * owned + e, entry]
                old.append(down_ref[e, pl.ds(pl.multiple_of(block * span, span), span), lanes])
            fresh = (jnp.concatenate(old, axis=0).astype(F32) + added).astype(BF16)
            part = jnp.dot(rest_ref[e], down_ref[e, :, lanes], preferred_element_type=F32)
            part = (part + jnp.dot(taken_ref[e], fresh, preferred_element_type=F32)).astype(BF16)
            for k in range(groups):
                at = (k * owned + e) * per_expert
                part_of = PIECES * at // rows
                into = outs[0] if q == 0 else outs[PIECES * (q - 1) + 1 + part_of]
                at = at if q == 0 else at - part_of * (rows // PIECES)
                into[at : at + per_expert, :] = part[k * per_expert : (k + 1) * per_expert]


def down_pieces(meta, share, across, within, per_expert, block_list, rest, taken, delta, down_weight, cols):
    owned, units, _ = down_weight.shape
    slots = rest.shape[1]
    rows = owned * slots
    vmem = pl.BlockSpec(memory_space=pltpu.VMEM)
    return pl.pallas_call(
        functools.partial(down_kernel, share, across, within, per_expert),
        grid_spec=pltpu.PrefetchScalarGridSpec(
            num_scalar_prefetch=2, grid=(), in_specs=[vmem] * 4, out_specs=[vmem] * (1 + PIECES * (within - 1))
        ),
        out_shape=[jax.ShapeDtypeStruct((rows, cols), BF16)]
        + [jax.ShapeDtypeStruct((rows // PIECES, cols), BF16)] * (PIECES * (within - 1)),
        compiler_params=pltpu.CompilerParams(vmem_limit_bytes=SMALL_VMEM),
        cost_estimate=pl.CostEstimate(
            flops=2 * owned * slots * units * cols * within,
            bytes_accessed=2 * owned * units * cols * within,
            transcendentals=0,
        ),
        name="down_mixed",
    )(meta, block_list, rest, taken, delta, down_weight)


def swap(value, axis, distance):
    return lax.ppermute(value, axis, [(i, i ^ distance) for i in range(lax.axis_size(axis))])


def shift(value, axis, distance):
    size = lax.axis_size(axis)
    return lax.ppermute(value, axis, [(i, (i + distance) % size) for i in range(size)])


def on_device(
    tokens,
    route,
    route_weight,
    gate_up,
    down_weight,
    adam_first,
    adam_second,
    gradient,
    block_list,
    block_count,
):
    groups = lax.axis_size("expert")
    across, within = lax.axis_size("fsdp"), lax.axis_size("tensor")
    at_z, at_f, at_t = lax.axis_index("expert"), lax.axis_index("fsdp"), lax.axis_index("tensor")
    owned = gate_up.shape[0]
    steps, block, width = tokens.shape
    cols = width // (across * within)
    lists = block_list.reshape(block_list.shape[0], MAXCH)
    counts = block_count.reshape(-1)

    meta = jnp.stack(
        [at_z]
        + [at_f ^ r for r in range(across)]
        + [at_t ^ q for q in range(within)]
        + [at_f * within + at_t]
    ).astype(jnp.int32)

    *sends, select, pick = pack_slots(meta, tokens, route, groups, owned, cols)
    arrived = [shift(send, "expert", k) for k, send in enumerate(sends, 1)]
    mine = own_slots(select, tokens)
    deltas = listed_deltas(meta, adam_first, adam_second, gradient, lists, counts, groups)
    down_source, deltas = lax.optimization_barrier((down_weight, deltas))
    down_local = fetch_down(down_source)
    arrived, deltas, mine, down_local = lax.optimization_barrier((arrived, deltas, mine, down_local))
    away = jnp.stack(arrived)
    early = {k: shift(deltas[k], "expert", k) for k in (1, groups - 1)}

    def stage(begin, columns, sums, last):
        received = [[c] + [swap(c, "tensor", q) for q in range(1, within)] for c in columns]
        return gate_up_stage(meta, lists, begin, across, mine, received, gate_up, sums, last)

    others = [swap(away, "fsdp", r) for r in range(1, across)]
    (sums,) = stage(0, [away], None, False)
    experts = adam_first.shape[0]
    parts_at = (experts // 4, experts // 4 + experts * 3 // 8, experts)
    adam_in = (adam_first, adam_second, gradient)
    adam_in, deltas, early, sums = lax.optimization_barrier((adam_in, deltas, early, sums))
    late = {k: shift(deltas[k], "expert", k) for k in range(2, groups - 1)}
    filled = adam_part(*adam_in, 0, parts_at[0], cost=SHORT)
    others, late, filled, sums = lax.optimization_barrier((others, late, filled, sums))
    incoming = [{0: deltas[0], **early, **late}[k] for k in range(groups)]
    incoming = jnp.stack(incoming)
    rest, taken = stage(1, others, sums, True)

    def down(r, order):
        pieces = down_pieces(
            order, r, across, within, steps * CAP, lists, rest, taken, incoming, down_local, cols
        )
        return pieces[0], [swap(pieces[i], "tensor", (i - 1) // PIECES + 1) for i in range(1, len(pieces))]

    def add(*terms):
        total = terms[0].astype(F32)
        for term in terms[1:]:
            total = total + term.astype(F32)
        return total.astype(BF16)

    rows = groups * owned * steps * CAP

    def joined(pair):
        return [jnp.concatenate(pair[1][i : i + PIECES]) for i in range(0, len(pair[1]), PIECES)]

    def summed(pair, *more):
        return add(pair[0], *joined(pair), *more)

    far_sum = summed(down(across - 1, meta))
    if across == 4:
        far_up, far_low = far_sum[: rows // 2], far_sum[rows // 2 :]
        order, far_up, far_low = lax.optimization_barrier((meta, far_up, far_low))
        by_one, by_two = swap(far_up, "fsdp", 1), swap(far_low, "fsdp", 2)
        near = [down(r, order) for r in (1, 2)]
        by_one, by_two, near = lax.optimization_barrier((by_one, by_two, near))
        passed = [jnp.pad(by_two, ((rows // 2, 0), (0, 0))), jnp.pad(by_one, ((0, rows // 2), (0, 0)))]
        others = [swap(summed(near[i], passed[i]), "fsdp", i + 1) for i in range(2)]
    else:
        order, far_sum = lax.optimization_barrier((meta, far_sum))
        others = [swap(summed(down(r, order)), "fsdp", r) for r in range(1, across - 1)]
        others.append(swap(far_sum, "fsdp", across - 1))
    last = down(0, order)
    adam_in, filled, raw = lax.optimization_barrier((adam_in, filled, last[0]))
    filled = adam_part(*adam_in, parts_at[0], parts_at[1], filled)
    parts = add(raw, *joined(last), *others).reshape(groups, rows // groups, cols)
    adam_in, filled, parts = lax.optimization_barrier((adam_in, filled, parts))
    back = [shift(parts[k], "expert", -k) for k in range(1, groups)]
    first_new, second_new = adam_part(*adam_in, parts_at[1], parts_at[2], filled)
    return (combine_slots(pick, route_weight, [parts[0], *back]), first_new, second_new)


def solution(mesh):
    return jax.shard_map(
        on_device,
        mesh=mesh,
        in_specs=(
            P(None, "expert", None),
            P(None, "expert", None),
            P(None, "expert", None),
            P("expert", None, None, ("fsdp", "tensor")),
            P("expert", ("fsdp", "tensor"), None),
            P(None, ("fsdp", "tensor"), "expert"),
            P(None, ("fsdp", "tensor"), "expert"),
            P(None, ("fsdp", "tensor"), "expert"),
            P(None, ("fsdp", "tensor"), None),
            P(None, ("fsdp", "tensor")),
        ),
        out_specs=(
            P(None, "expert", ("fsdp", "tensor")),
            P(None, ("fsdp", "tensor"), "expert"),
            P(None, ("fsdp", "tensor"), "expert"),
        ),
        check_vma=False,
    )
```

time: 129 us -> 107 us (0.83)
  local copies, waits for them, and re-layouts: 23.5 us -> 2.37 us
  waiting for transfers between devices: 12.8 us -> 11.4 us
    unnamed x25 -> x8, local copies, waits for them, and re-layouts: 23.3 us -> 1.45 us
    ppermute x15 -> x19, waiting for transfers between devices: 12.8 us -> 8.49 us  [swap(): lax.ppermute(value, axis, [(i, i ^ distance) for i in range(lax.axis_size...]
    all_to_all x1 -> x0, starting transfers between devices: 3.65 us -> none  [on_device(): lax.all_to_all(by_owner, 'expert', split_axis=0, concat_axis=0, tiled=True)]
    ppermute x6 -> x9, waiting for transfers between devices: 0.02 us -> 2.91 us  [shift(): lax.ppermute(value, axis, [(i, (i + distance) % size) for i in range(size)])]
    pallas_call x2 -> x3, Pallas kernels: 15.1 us -> 17.6 us  [adam_part(): pl.pallas_call(adam_kernel, grid=(end - begin,), in_specs=[block, block,...]
    ppermute x6 -> x9, starting transfers between devices: 12.6 us -> 14.8 us  [shift(): lax.ppermute(value, axis, [(i, (i + distance) % size) for i in range(size)])]
    ppermute x15 -> x19, starting transfers between devices: 9.31 us -> 11.4 us  [swap(): lax.ppermute(value, axis, [(i, i ^ distance) for i in range(lax.axis_size...]
    pallas_call x3 -> x2, Pallas kernels: 24.6 us -> 23.2 us  [gate_up_stage(): pl.pallas_call(functools.partial(gate_up_kernel, begin, shares, across, w...]
  transfers between devices with their start and end apart: 22 -> 28, of which waited for: 7 -> 13; matrix products, arithmetic and copies ran while one was open for 1% -> 1% of each run, Pallas kernels for 41% -> 41%
where the time goes in v3:
time: 107 us
  Pallas kernels  65 us (61%)
  starting transfers between devices  26.2 us (24%)
  waiting for transfers between devices  11.4 us (11%)
  local copies, waits for them, and re-layouts  2.37 us (2%)
    pallas_call x2, Pallas kernels, gate_up_stage(): pl.pallas_call(functools.partial(gate_up_kernel, begin, shares, across, w...  23.2 us
    pallas_call x3, Pallas kernels, adam_part(): pl.pallas_call(adam_kernel, grid=(end - begin,), in_specs=[block, block,...  17.6 us
    ppermute x9, starting transfers between devices, shift(): lax.ppermute(value, axis, [(i, (i + distance) % size) for i in range(size)])  14.8 us
    ppermute x19, starting transfers between devices, swap(): lax.ppermute(value, axis, [(i, i ^ distance) for i in range(lax.axis_size...  11.4 us
    pallas_call x4, Pallas kernels, down_pieces(): pl.pallas_call(functools.partial(down_kernel, share, across, within, per_...  11.1 us
    ppermute x19, waiting for transfers between devices, swap(): lax.ppermute(value, axis, [(i, i ^ distance) for i in range(lax.axis_size...  8.49 us
    pallas_call x1, Pallas kernels, fetch_down(): pl.pallas_call(fetch_kernel, in_specs=[pl.BlockSpec(memory_space=pltpu.HB...  5.88 us
    pallas_call x1, Pallas kernels, listed_deltas(): pl.pallas_call(functools.partial(delta_kernel, groups), grid_spec=pltpu.P...  3.66 us
  transfers between devices with their start and end apart: 28, of which 13 were waited for; matrix products, arithmetic and copies ran while one was open for 1% of the time, Pallas kernels for 41%

profile of v3, /device:TPU:0, one launch (start us, length us, event | category | flops | bytes accessed | tf_op | source)
XLA Modules:
  0.0 106.7 jit_solution(14454003303328404906)
XLA Ops:
  1.4 2.2 %pack_slots.1 = (bf16[128,512]{1,0:T(8,128)(2,1)S(1)}, bf16[128,512]{1,0:T(8,128)(2,1)S(1)}, bf16[128,512]{1,0:T(8,128)(2,1)S(1)}, bf16[128,128]{1,0:T(8,128)(2,1)S(1)}, bf16[2,128,512]{2,1,0:T(8,128)(2,1)S(1)}) custom-call(s32[8]{0:T(128)S(1)} %stack.62.meta_ref, bf16[2,64,4096]{2,1,0:T(8,128)(2,1)} %tokens_ref.3, s32[2,2,64]{2,1,0:T(2,128)S(1)} %bitcast.29), custom_call_target="tpu_custom_call" | custom-call | flops 10000000 | bytes 262144 | tf_op jit(solution)/shard_map/pack_slots/pallas_call | solution.py:89
  3.6 3.1 %collective-permute-start = (bf16[128,512]{1,0:T(8,128)(2,1)S(1)}, bf16[128,512]{1,0:T(8,128)(2,1)S(1)}, u32[]{:S(2)}, u32[]{:S(2)}) collective-permute-start(bf16[128,512]{1,0:T(8,128)(2,1)S(1)} %get-tuple-element.85), channel_id=1, source_target_pairs={{0,2},{2,4},{4,6},{6,0},{1,3},{3,5},{5,7},{7,1},{8,10},{10,12},{12... | collective-permute-start | bytes 393224 | tf_op jit(solution)/shard_map/ppermute | solution.py:427
  6.7 2.6 %collective-permute-start.1 = (bf16[128,512]{1,0:T(8,128)(2,1)S(1)}, bf16[128,512]{1,0:T(8,128)(2,1)S(1)}, u32[]{:S(2)}, u32[]{:S(2)}) collective-permute-start(bf16[128,512]{1,0:T(8,128)(2,1)S(1)} %get-tuple-element.86), channel_id=1, source_target_pairs={{0,4},{2,6},{4,0},{6,2},{1,5},{3,7},{5,1},{7,3},{8,12},{10,14},{12... | collective-permute-start | bytes 393224 | tf_op jit(solution)/shard_map/ppermute | solution.py:427
  9.3 1.3 %collective-permute-start.2 = (bf16[128,512]{1,0:T(8,128)(2,1)S(1)}, bf16[128,512]{1,0:T(8,128)(2,1)S(1)}, u32[]{:S(2)}, u32[]{:S(2)}) collective-permute-start(bf16[128,512]{1,0:T(8,128)(2,1)S(1)} %get-tuple-element.87), channel_id=1, source_target_pairs={{0,6},{2,0},{4,2},{6,4},{1,7},{3,1},{5,3},{7,5},{8,14},{10,8},{12,... | collective-permute-start | bytes 393224 | tf_op jit(solution)/shard_map/ppermute | solution.py:427
  12.0 3.7 %listed_deltas.1 = (bf16[2,32,1024]{2,1,0:T(8,128)(2,1)S(1)}, bf16[2,32,1024]{2,1,0:T(8,128)(2,1)S(1)}, bf16[2,32,1024]{2,1,0:T(8,128)(2,1)S(1)}, bf16[2,32,1024]{2,1,0:T(8,128)(2,1)S(1)}) custom-call(s32[8]{0:T(128)S(1)} %stack.62.meta_ref, s32[8,4]{1,0:T(8,128)S(1)} %copy.17.list_ref, s32[8]{0:T(128)S(1)} %bitcast.31, f32[8,256,1024]{2,1,0:T(8,128)} %first_ref.4, ...), custom_call_target="tpu_custom_call" | custom-call | flops 1000000 | bytes 3145728 | tf_op jit(solution)/shard_map/listed_deltas/pallas_call | solution.py:192
  15.7 5.9 %fetch_down.1.down_ref = bf16[2,1024,4096]{2,1,0:T(8,128)(2,1)S(1)} custom-call(bf16[2,1024,4096]{2,1,0:T(8,128)(2,1)} %down_ref), custom_call_target="tpu_custom_call" | custom-call | bytes 16777216 | tf_op jit(solution)/shard_map/fetch_down/pallas_call | solution.py:354
  22.3 2.5 %collective-permute-start.8 = (bf16[3,128,512]{2,1,0:T(8,128)(2,1)S(1)}, bf16[3,128,512]{2,1,0:T(8,128)(2,1)S(1)}, u32[]{:S(2)}, u32[]{:S(2)}) collective-permute-start(bf16[3,128,512]{2,1,0:T(8,128)(2,1)S(1)} %pad_maximum_fusion.1.refs_0_), channel_id=1, source_target_pairs={{0,24},{8,16},{16,8},{24,0},{1,25},{9,17},{17,9},{25,1},{2,26},{10... | collective-permute-start | bytes 1179656 | tf_op jit(solution)/shard_map/ppermute | solution.py:422
  26.5 3.1 %collective-permute-start.4 = (bf16[2,32,1024]{2,1,0:T(8,128)(2,1)S(1)}, bf16[2,32,1024]{2,1,0:T(8,128)(2,1)S(1)}, u32[]{:S(2)}, u32[]{:S(2)}) collective-permute-start(bf16[2,32,1024]{2,1,0:T(8,128)(2,1)S(1)} %get-tuple-element.101), channel_id=1, source_target_pairs={{0,6},{2,0},{4,2},{6,4},{1,7},{3,1},{5,3},{7,5},{8,14},{10,8},{12,... | collective-permute-start | bytes 393224 | tf_op jit(solution)/shard_map/ppermute | solution.py:427
  29.7 8.2 %gate_up_stage.2.refs_9_ = f32[2,2,256,1024]{3,2,1,0:T(8,128)S(1)} custom-call(s32[8]{0:T(128)S(1)} %stack.62.meta_ref, s32[8,4]{1,0:T(8,128)S(1)} %copy.17.list_ref, bf16[128,4096]{1,0:T(8,128)(2,1)S(1)} %own_slots.1.own_ref, bf16[3,128,512]{2,1,0:T(8,128)(2,1)S(1)} %pad_maximum_fusion.1.refs_0_, bf16[3,128,512]{2,1,0:T(8,128)(2,1)S(1)} %collective-permute-done.5.refs_1_, ...), custom_call_target="tpu_custom_call" | custom-call | flops 2147483648 | bytes 8388608 | tf_op jit(solution)/shard_map/gate_up_stage/pallas_call | solution.py:322
  38.0 4.0 %adam_moments.3 = (f32[8,256,1024]{2,1,0:T(8,128)}, f32[8,256,1024]{2,1,0:T(8,128)}) custom-call(f32[8,256,1024]{2,1,0:T(8,128)} %first_ref.4, f32[8,256,1024]{2,1,0:T(8,128)} %second_ref.4, bf16[8,256,1024]{2,1,0:T(8,128)(2,1)} %grad_ref.4), custom_call_target="tpu_custom_call" | custom-call | flops 1 | bytes 1 | tf_op jit(solution)/shard_map/adam_moments/pallas_call | solution.py:224
  43.2 1.5 %collective-permute-done.9 = bf16[2,32,1024]{2,1,0:T(8,128)(2,1)S(1)} collective-permute-done((bf16[2,32,1024]{2,1,0:T(8,128)(2,1)S(1)}, bf16[2,32,1024]{2,1,0:T(8,128)(2,1)S(1)}, u32[]{:S(2)}, u32[]{:S(2)}) %collective-permute-start.9) | collective-permute-done | bytes 131104 | tf_op jit(solution)/shard_map/ppermute | solution.py:427
  47.6 14.9 %gate_up_stage.3 = (bf16[2,256,1024]{2,1,0:T(8,128)(2,1)S(1)}, bf16[2,256,128]{2,1,0:T(8,128)(2,1)S(1)}) custom-call(s32[8]{0:T(128)S(1)} %stack.62.meta_ref, s32[8,4]{1,0:T(8,128)S(1)} %copy.17.list_ref, bf16[128,4096]{1,0:T(8,128)(2,1)S(1)} %own_slots.1.own_ref, bf16[3,128,512]{2,1,0:T(8,128)(2,1)S(1)} %collective-permute-done.6.refs_0_, ...), custom_call_target="tpu_custom_call" | custom-call | flops 6442450944 | bytes 25165824 | tf_op jit(solution)/shard_map/gate_up_stage/pallas_call | solution.py:322
  62.5 2.8 %down_mixed.4 = (bf16[512,512]{1,0:T(8,128)(2,1)S(1)}, bf16[256,512]{1,0:T(8,128)(2,1)S(1)}, bf16[256,512]{1,0:T(8,128)(2,1)S(1)}) custom-call(s32[8]{0:T(128)S(1)} %stack.62.meta_ref, s32[8,4]{1,0:T(8,128)S(1)} %copy.17.list_ref, bf16[2,256,1024]{2,1,0:T(8,128)(2,1)S(1)} %get-tuple-element.119.rest_ref, ...), custom_call_target="tpu_custom_call" | custom-call | flops 1073741824 | bytes 4194304 | tf_op jit(solution)/shard_map/down_mixed/pallas_call | solution.py:404
  67.5 1.6 %collective-permute-start.17 = (bf16[256,512]{1,0:T(8,128)(2,1)S(1)}, bf16[256,512]{1,0:T(8,128)(2,1)S(1)}, u32[]{:S(2)}, u32[]{:S(2)}) collective-permute-start(bf16[256,512]{1,0:T(8,128)(2,1)S(1)} %get-tuple-element.141), channel_id=1, source_target_pairs={{0,8},{8,0},{16,24},{24,16},{1,9},{9,1},{17,25},{25,17},{2,10},{10... | collective-permute-start | bytes 786440 | tf_op jit(solution)/shard_map/ppermute | solution.py:422
  69.0 1.5 %collective-permute-start.18 = (bf16[256,512]{1,0:T(8,128)(2,1)S(1)}, bf16[256,512]{1,0:T(8,128)(2,1)S(1)}, u32[]{:S(2)}, u32[]{:S(2)}) collective-permute-start(bf16[256,512]{1,0:T(8,128)(2,1)S(1)} %get-tuple-element.142), channel_id=1, source_target_pairs={{0,16},{8,24},{16,0},{24,8},{1,17},{9,25},{17,1},{25,9},{2,18},{10... | collective-permute-start | bytes 786440 | tf_op jit(solution)/shard_map/ppermute | solution.py:422
  70.6 2.8 %down_mixed.7 = (bf16[512,512]{1,0:T(8,128)(2,1)S(1)}, bf16[256,512]{1,0:T(8,128)(2,1)S(1)}, bf16[256,512]{1,0:T(8,128)(2,1)S(1)}) custom-call(s32[8]{0:T(128)S(1)} %stack.62.meta_ref, s32[8,4]{1,0:T(8,128)S(1)} %copy.17.list_ref, bf16[2,256,1024]{2,1,0:T(8,128)(2,1)S(1)} %get-tuple-element.119.rest_ref, ...), custom_call_target="tpu_custom_call" | custom-call | flops 1073741824 | bytes 4194304 | tf_op jit(solution)/shard_map/down_mixed/pallas_call | solution.py:404
  73.9 2.8 %down_mixed.6 = (bf16[512,512]{1,0:T(8,128)(2,1)S(1)}, bf16[256,512]{1,0:T(8,128)(2,1)S(1)}, bf16[256,512]{1,0:T(8,128)(2,1)S(1)}) custom-call(s32[8]{0:T(128)S(1)} %stack.62.meta_ref, s32[8,4]{1,0:T(8,128)S(1)} %copy.17.list_ref, bf16[2,256,1024]{2,1,0:T(8,128)(2,1)S(1)} %get-tuple-element.119.rest_ref, ...), custom_call_target="tpu_custom_call" | custom-call | flops 1073741824 | bytes 4194304 | tf_op jit(solution)/shard_map/down_mixed/pallas_call | solution.py:404
  80.9 2.8 %down_mixed.5 = (bf16[512,512]{1,0:T(8,128)(2,1)S(1)}, bf16[256,512]{1,0:T(8,128)(2,1)S(1)}, bf16[256,512]{1,0:T(8,128)(2,1)S(1)}) custom-call(s32[8]{0:T(128)S(1)} %stack.62.meta_ref, s32[8,4]{1,0:T(8,128)S(1)} %copy.17.list_ref, bf16[2,256,1024]{2,1,0:T(8,128)(2,1)S(1)} %get-tuple-element.119.rest_ref, ...), custom_call_target="tpu_custom_call" | custom-call | flops 1073741824 | bytes 4194304 | tf_op jit(solution)/shard_map/down_mixed/pallas_call | solution.py:404
  84.3 6.8 %adam_moments.4 = (f32[8,256,1024]{2,1,0:T(8,128)}, f32[8,256,1024]{2,1,0:T(8,128)}) custom-call(f32[8,256,1024]{2,1,0:T(8,128)} %first_ref.4, f32[8,256,1024]{2,1,0:T(8,128)} %second_ref.4, bf16[8,256,1024]{2,1,0:T(8,128)(2,1)} %grad_ref.4, f32[8,256,1024]{2,1,0:T(8,128)} %get-tuple-element.134.refs_0_, ...), custom_call_target="tpu_custom_call", output_to_operand_aliasing={{0}: (3, {}), {1}: (4, {})} | custom-call | flops 6291456 | bytes 14155776 | tf_op jit(solution)/shard_map/adam_moments/pallas_call | solution.py:224
  91.1 1.8 %collective-permute-done.24 = bf16[512,512]{1,0:T(8,128)(2,1)S(1)} collective-permute-done((bf16[512,512]{1,0:T(8,128)(2,1)S(1)}, bf16[512,512]{1,0:T(8,128)(2,1)S(1)}, u32[]{:S(2)}, u32[]{:S(2)}) %collective-permute-start.24) | collective-permute-done | bytes 524320 | tf_op jit(solution)/shard_map/ppermute | solution.py:422
  93.7 2.2 %collective-permute-start.26 = (bf16[128,512]{1,0:T(8,128)(2,1)S(1)}, bf16[128,512]{1,0:T(8,128)(2,1)S(1)}, u32[]{:S(2)}, u32[]{:S(2)}) collective-permute-start(bf16[128,512]{1,0:T(8,128)(2,1)S(1)} %get-tuple-element.166), channel_id=1, source_target_pairs={{0,4},{2,6},{4,0},{6,2},{1,5},{3,7},{5,1},{7,3},{8,12},{10,14},{12... | collective-permute-start | bytes 393224 | tf_op jit(solution)/shard_map/ppermute | solution.py:427
  96.0 1.6 %collective-permute-start.25 = (bf16[128,512]{1,0:T(8,128)(2,1)S(1)}, bf16[128,512]{1,0:T(8,128)(2,1)S(1)}, u32[]{:S(2)}, u32[]{:S(2)}) collective-permute-start(bf16[128,512]{1,0:T(8,128)(2,1)S(1)} %get-tuple-element.167), channel_id=1, source_target_pairs={{0,6},{2,0},{4,2},{6,4},{1,7},{3,1},{5,3},{7,5},{8,14},{10,8},{12,... | collective-permute-start | bytes 393224 | tf_op jit(solution)/shard_map/ppermute | solution.py:427
  97.5 6.8 %adam_moments.5 = (f32[8,256,1024]{2,1,0:T(8,128)}, f32[8,256,1024]{2,1,0:T(8,128)}) custom-call(f32[8,256,1024]{2,1,0:T(8,128)} %first_ref.4, f32[8,256,1024]{2,1,0:T(8,128)} %second_ref.4, bf16[8,256,1024]{2,1,0:T(8,128)(2,1)} %grad_ref.4, f32[8,256,1024]{2,1,0:T(8,128)} %get-tuple-element.161.refs_0_, ...), custom_call_target="tpu_custom_call", output_to_operand_aliasing={{0}: (3, {}), {1}: (4, {})} | custom-call | flops 6291456 | bytes 14155776 | tf_op jit(solution)/shard_map/adam_moments/pallas_call | solution.py:224
  104.3 1.4 %collective-permute-done.26.refs_2_ = bf16[128,512]{1,0:T(8,128)(2,1)S(1)} collective-permute-done((bf16[128,512]{1,0:T(8,128)(2,1)S(1)}, bf16[128,512]{1,0:T(8,128)(2,1)S(1)}, u32[]{:S(2)}, u32[]{:S(2)}) %collective-permute-start.26) | collective-permute-done | bytes 131104 | tf_op jit(solution)/shard_map/ppermute | solution.py:427
  (64 shorter events, 17.9 us)
Async XLA Ops:
  3.6 18.5 %collective-permute-start = (bf16[128,512]{1,0:T(8,128)(2,1)S(1)}, bf16[128,512]{1,0:T(8,128)(2,1)S(1)}, u32[]{:S(2)}, u32[]{:S(2)}) collective-permute-start(bf16[128,512]{1,0:T(8,128)(2,1)S(1)} %get-tuple-element.85), channel_id=1, source_target_pairs={{0,2},{2,4},{4,6},{6,0},{1,3},{3,5},{5,7},{7,1},{8,10},{10,12},{12... | collective-permute-start | bytes 393224 | tf_op jit(solution)/shard_map/ppermute | solution.py:427
  6.7 15.5 %collective-permute-start.1 = (bf16[128,512]{1,0:T(8,128)(2,1)S(1)}, bf16[128,512]{1,0:T(8,128)(2,1)S(1)}, u32[]{:S(2)}, u32[]{:S(2)}) collective-permute-start(bf16[128,512]{1,0:T(8,128)(2,1)S(1)} %get-tuple-element.86), channel_id=1, source_target_pairs={{0,4},{2,6},{4,0},{6,2},{1,5},{3,7},{5,1},{7,3},{8,12},{10,14},{12... | collective-permute-start | bytes 393224 | tf_op jit(solution)/shard_map/ppermute | solution.py:427
  9.3 12.9 %collective-permute-start.2 = (bf16[128,512]{1,0:T(8,128)(2,1)S(1)}, bf16[128,512]{1,0:T(8,128)(2,1)S(1)}, u32[]{:S(2)}, u32[]{:S(2)}) collective-permute-start(bf16[128,512]{1,0:T(8,128)(2,1)S(1)} %get-tuple-element.87), channel_id=1, source_target_pairs={{0,6},{2,0},{4,2},{6,4},{1,7},{3,1},{5,3},{7,5},{8,14},{10,8},{12,... | collective-permute-start | bytes 393224 | tf_op jit(solution)/shard_map/ppermute | solution.py:427
  22.2 4.3 %collective-permute-start.5 = (bf16[3,128,512]{2,1,0:T(8,128)(2,1)S(1)}, bf16[3,128,512]{2,1,0:T(8,128)(2,1)S(1)}, u32[]{:S(2)}, u32[]{:S(2)}) collective-permute-start(bf16[3,128,512]{2,1,0:T(8,128)(2,1)S(1)} %pad_maximum_fusion.1.refs_0_), channel_id=1, source_target_pairs={{0,1},{1,0},{2,3},{3,2},{4,5},{5,4},{6,7},{7,6},{8,9},{9,8},{10,11... | collective-permute-start | bytes 1179656 | tf_op jit(solution)/shard_map/ppermute | solution.py:422
  22.3 19.8 %collective-permute-start.8 = (bf16[3,128,512]{2,1,0:T(8,128)(2,1)S(1)}, bf16[3,128,512]{2,1,0:T(8,128)(2,1)S(1)}, u32[]{:S(2)}, u32[]{:S(2)}) collective-permute-start(bf16[3,128,512]{2,1,0:T(8,128)(2,1)S(1)} %pad_maximum_fusion.1.refs_0_), channel_id=1, source_target_pairs={{0,24},{8,16},{16,8},{24,0},{1,25},{9,17},{17,9},{25,1},{2,26},{10... | collective-permute-start | bytes 1179656 | tf_op jit(solution)/shard_map/ppermute | solution.py:422
  24.8 18.3 %collective-permute-start.7 = (bf16[3,128,512]{2,1,0:T(8,128)(2,1)S(1)}, bf16[3,128,512]{2,1,0:T(8,128)(2,1)S(1)}, u32[]{:S(2)}, u32[]{:S(2)}) collective-permute-start(bf16[3,128,512]{2,1,0:T(8,128)(2,1)S(1)} %pad_maximum_fusion.1.refs_0_), channel_id=1, source_target_pairs={{0,16},{8,24},{16,0},{24,8},{1,17},{9,25},{17,1},{25,9},{2,18},{10... | collective-permute-start | bytes 1179656 | tf_op jit(solution)/shard_map/ppermute | solution.py:422
  25.3 17.9 %collective-permute-start.6 = (bf16[3,128,512]{2,1,0:T(8,128)(2,1)S(1)}, bf16[3,128,512]{2,1,0:T(8,128)(2,1)S(1)}, u32[]{:S(2)}, u32[]{:S(2)}) collective-permute-start(bf16[3,128,512]{2,1,0:T(8,128)(2,1)S(1)} %pad_maximum_fusion.1.refs_0_), channel_id=1, source_target_pairs={{0,8},{8,0},{16,24},{24,16},{1,9},{9,1},{17,25},{25,17},{2,10},{10... | collective-permute-start | bytes 1179656 | tf_op jit(solution)/shard_map/ppermute | solution.py:422
  25.8 12.1 %collective-permute-start.3 = (bf16[2,32,1024]{2,1,0:T(8,128)(2,1)S(1)}, bf16[2,32,1024]{2,1,0:T(8,128)(2,1)S(1)}, u32[]{:S(2)}, u32[]{:S(2)}) collective-permute-start(bf16[2,32,1024]{2,1,0:T(8,128)(2,1)S(1)} %get-tuple-element.99), channel_id=1, source_target_pairs={{0,2},{2,4},{4,6},{6,0},{1,3},{3,5},{5,7},{7,1},{8,10},{10,12},{12... | collective-permute-start | bytes 393224 | tf_op jit(solution)/shard_map/ppermute | solution.py:427
  26.5 11.4 %collective-permute-start.4 = (bf16[2,32,1024]{2,1,0:T(8,128)(2,1)S(1)}, bf16[2,32,1024]{2,1,0:T(8,128)(2,1)S(1)}, u32[]{:S(2)}, u32[]{:S(2)}) collective-permute-start(bf16[2,32,1024]{2,1,0:T(8,128)(2,1)S(1)} %get-tuple-element.101), channel_id=1, source_target_pairs={{0,6},{2,0},{4,2},{6,4},{1,7},{3,1},{5,3},{7,5},{8,14},{10,8},{12,... | collective-permute-start | bytes 393224 | tf_op jit(solution)/shard_map/ppermute | solution.py:427
  37.9 6.8 %collective-permute-start.9 = (bf16[2,32,1024]{2,1,0:T(8,128)(2,1)S(1)}, bf16[2,32,1024]{2,1,0:T(8,128)(2,1)S(1)}, u32[]{:S(2)}, u32[]{:S(2)}) collective-permute-start(bf16[2,32,1024]{2,1,0:T(8,128)(2,1)S(1)} %get-tuple-element.109), channel_id=1, source_target_pairs={{0,4},{2,6},{4,0},{6,2},{1,5},{3,7},{5,1},{7,3},{8,12},{10,14},{12... | collective-permute-start | bytes 393224 | tf_op jit(solution)/shard_map/ppermute | solution.py:427
  44.8 2.3 %collective-permute-start.11 = (bf16[3,128,512]{2,1,0:T(8,128)(2,1)S(1)}, bf16[3,128,512]{2,1,0:T(8,128)(2,1)S(1)}, u32[]{:S(2)}, u32[]{:S(2)}) collective-permute-start(bf16[3,128,512]{2,1,0:T(8,128)(2,1)S(1)} %collective-permute-done.7.refs_2_), channel_id=1, source_target_pairs={{0,1},{1,0},{2,3},{3,2},{4,5},{5,4},{6,7},{7,6},{8,9},{9,8},{10,11... | collective-permute-start | bytes 1179656 | tf_op jit(solution)/shard_map/ppermute | solution.py:422
  45.3 2.3 %collective-permute-start.12 = (bf16[3,128,512]{2,1,0:T(8,128)(2,1)S(1)}, bf16[3,128,512]{2,1,0:T(8,128)(2,1)S(1)}, u32[]{:S(2)}, u32[]{:S(2)}) collective-permute-start(bf16[3,128,512]{2,1,0:T(8,128)(2,1)S(1)} %collective-permute-done.8.refs_4_), channel_id=1, source_target_pairs={{0,1},{1,0},{2,3},{3,2},{4,5},{5,4},{6,7},{7,6},{8,9},{9,8},{10,11... | collective-permute-start | bytes 1179656 | tf_op jit(solution)/shard_map/ppermute | solution.py:422
  67.5 9.4 %collective-permute-start.17 = (bf16[256,512]{1,0:T(8,128)(2,1)S(1)}, bf16[256,512]{1,0:T(8,128)(2,1)S(1)}, u32[]{:S(2)}, u32[]{:S(2)}) collective-permute-start(bf16[256,512]{1,0:T(8,128)(2,1)S(1)} %get-tuple-element.141), channel_id=1, source_target_pairs={{0,8},{8,0},{16,24},{24,16},{1,9},{9,1},{17,25},{25,17},{2,10},{10... | collective-permute-start | bytes 786440 | tf_op jit(solution)/shard_map/ppermute | solution.py:422
  69.0 8.2 %collective-permute-start.18 = (bf16[256,512]{1,0:T(8,128)(2,1)S(1)}, bf16[256,512]{1,0:T(8,128)(2,1)S(1)}, u32[]{:S(2)}, u32[]{:S(2)}) collective-permute-start(bf16[256,512]{1,0:T(8,128)(2,1)S(1)} %get-tuple-element.142), channel_id=1, source_target_pairs={{0,16},{8,24},{16,0},{24,8},{1,17},{9,25},{17,1},{25,9},{2,18},{10... | collective-permute-start | bytes 786440 | tf_op jit(solution)/shard_map/ppermute | solution.py:422
  73.3 3.9 %collective-permute-start.21 = (bf16[256,512]{1,0:T(8,128)(2,1)S(1)}, bf16[256,512]{1,0:T(8,128)(2,1)S(1)}, u32[]{:S(2)}, u32[]{:S(2)}) collective-permute-start(bf16[256,512]{1,0:T(8,128)(2,1)S(1)} %get-tuple-element.147), channel_id=1, source_target_pairs={{0,1},{1,0},{2,3},{3,2},{4,5},{5,4},{6,7},{7,6},{8,9},{9,8},{10,11... | collective-permute-start | bytes 786440 | tf_op jit(solution)/shard_map/ppermute | solution.py:422
  73.4 3.9 %collective-permute-start.22 = (bf16[256,512]{1,0:T(8,128)(2,1)S(1)}, bf16[256,512]{1,0:T(8,128)(2,1)S(1)}, u32[]{:S(2)}, u32[]{:S(2)}) collective-permute-start(bf16[256,512]{1,0:T(8,128)(2,1)S(1)} %get-tuple-element.148), channel_id=1, source_target_pairs={{0,1},{1,0},{2,3},{3,2},{4,5},{5,4},{6,7},{7,6},{8,9},{9,8},{10,11... | collective-permute-start | bytes 786440 | tf_op jit(solution)/shard_map/ppermute | solution.py:422
  76.8 1.8 %collective-permute-start.20 = (bf16[256,512]{1,0:T(8,128)(2,1)S(1)}, bf16[256,512]{1,0:T(8,128)(2,1)S(1)}, u32[]{:S(2)}, u32[]{:S(2)}) collective-permute-start(bf16[256,512]{1,0:T(8,128)(2,1)S(1)} %get-tuple-element.145), channel_id=1, source_target_pairs={{0,1},{1,0},{2,3},{3,2},{4,5},{5,4},{6,7},{7,6},{8,9},{9,8},{10,11... | collective-permute-start | bytes 786440 | tf_op jit(solution)/shard_map/ppermute | solution.py:422
  78.8 14.0 %collective-permute-start.24 = (bf16[512,512]{1,0:T(8,128)(2,1)S(1)}, bf16[512,512]{1,0:T(8,128)(2,1)S(1)}, u32[]{:S(2)}, u32[]{:S(2)}) collective-permute-start(bf16[512,512]{1,0:T(8,128)(2,1)S(1)} %add_convert_fusion.1), channel_id=1, source_target_pairs={{0,16},{8,24},{16,0},{24,8},{1,17},{9,25},{17,1},{25,9},{2,18},{10... | collective-permute-start | bytes 1572872 | tf_op jit(solution)/shard_map/ppermute | solution.py:422
  79.6 13.8 %collective-permute-start.23 = (bf16[512,512]{1,0:T(8,128)(2,1)S(1)}, bf16[512,512]{1,0:T(8,128)(2,1)S(1)}, u32[]{:S(2)}, u32[]{:S(2)}) collective-permute-start(bf16[512,512]{1,0:T(8,128)(2,1)S(1)} %add_convert_fusion.2), channel_id=1, source_target_pairs={{0,8},{8,0},{16,24},{24,16},{1,9},{9,1},{17,25},{25,17},{2,10},{10... | collective-permute-start | bytes 1572872 | tf_op jit(solution)/shard_map/ppermute | solution.py:422
  83.7 7.4 %collective-permute-start.15 = (bf16[256,512]{1,0:T(8,128)(2,1)S(1)}, bf16[256,512]{1,0:T(8,128)(2,1)S(1)}, u32[]{:S(2)}, u32[]{:S(2)}) collective-permute-start(bf16[256,512]{1,0:T(8,128)(2,1)S(1)} %get-tuple-element.139), channel_id=1, source_target_pairs={{0,1},{1,0},{2,3},{3,2},{4,5},{5,4},{6,7},{7,6},{8,9},{9,8},{10,11... | collective-permute-start | bytes 786440 | tf_op jit(solution)/shard_map/ppermute | solution.py:422
  83.8 7.3 %collective-permute-start.16 = (bf16[256,512]{1,0:T(8,128)(2,1)S(1)}, bf16[256,512]{1,0:T(8,128)(2,1)S(1)}, u32[]{:S(2)}, u32[]{:S(2)}) collective-permute-start(bf16[256,512]{1,0:T(8,128)(2,1)S(1)} %get-tuple-element.140), channel_id=1, source_target_pairs={{0,1},{1,0},{2,3},{3,2},{4,5},{5,4},{6,7},{7,6},{8,9},{9,8},{10,11... | collective-permute-start | bytes 786440 | tf_op jit(solution)/shard_map/ppermute | solution.py:422
  93.6 10.7 %collective-permute-start.27 = (bf16[128,512]{1,0:T(8,128)(2,1)S(1)}, bf16[128,512]{1,0:T(8,128)(2,1)S(1)}, u32[]{:S(2)}, u32[]{:S(2)}) collective-permute-start(bf16[128,512]{1,0:T(8,128)(2,1)S(1)} %get-tuple-element.165), channel_id=1, source_target_pairs={{0,2},{2,4},{4,6},{6,0},{1,3},{3,5},{5,7},{7,1},{8,10},{10,12},{12... | collective-permute-start | bytes 393224 | tf_op jit(solution)/shard_map/ppermute | solution.py:427
  93.7 12.0 %collective-permute-start.26 = (bf16[128,512]{1,0:T(8,128)(2,1)S(1)}, bf16[128,512]{1,0:T(8,128)(2,1)S(1)}, u32[]{:S(2)}, u32[]{:S(2)}) collective-permute-start(bf16[128,512]{1,0:T(8,128)(2,1)S(1)} %get-tuple-element.166), channel_id=1, source_target_pairs={{0,4},{2,6},{4,0},{6,2},{1,5},{3,7},{5,1},{7,3},{8,12},{10,14},{12... | collective-permute-start | bytes 393224 | tf_op jit(solution)/shard_map/ppermute | solution.py:427
  96.0 9.8 %collective-permute-start.25 = (bf16[128,512]{1,0:T(8,128)(2,1)S(1)}, bf16[128,512]{1,0:T(8,128)(2,1)S(1)}, u32[]{:S(2)}, u32[]{:S(2)}) collective-permute-start(bf16[128,512]{1,0:T(8,128)(2,1)S(1)} %get-tuple-element.167), channel_id=1, source_target_pairs={{0,6},{2,0},{4,2},{6,4},{1,7},{3,1},{5,3},{7,5},{8,14},{10,8},{12,... | collective-permute-start | bytes 393224 | tf_op jit(solution)/shard_map/ppermute | solution.py:427
  (8 other events, 23.8 us)

commit v4 on v3

--- a/solution.py
+++ b/solution.py
@@ -12,7 +12,8 @@
 MAXCH = 4
 CAP = 32
 PIECES = 2
-UNIT_TILE = 256
+RING = 12
+UNIT_TILE = 512
 
 BETA_ONE = 0.9
 BETA_TWO = 0.95
@@ -26,7 +27,7 @@
 F32 = jnp.float32
 BF16 = jnp.bfloat16
 SMALL_VMEM = 16 * 2**20
-STAGE_VMEM = 20 * 2**20
+STAGE_VMEM = 24 * 2**20
 
 
 def in_hbm(value):
@@ -234,102 +235,92 @@
     )(in_hbm(adam_first), in_hbm(adam_second), in_hbm(gradient), *filled)
 
 
-def gate_up_kernel(begin, shares, across, within, first, last, meta_ref, list_ref, own_ref, *refs):
+def gate_up_kernel(begin, shares, across, within, tile, first, last, meta_ref, own_ref, *refs):
     recv = [refs[i * within : (i + 1) * within] for i in range(shares)]
-    refs = refs[shares * within :]
-    weights, refs = refs[:shares], refs[shares:]
+    gate_up_ref, refs = refs[shares * within], refs[shares * within + 1 :]
     sums_ref, refs = (None, refs) if first else (refs[0], refs[1:])
-    out_ref, taken_ref, rows_ref = (refs[0], None, refs[1]) if not last else refs
-    expert = pl.program_id(0)
-    owned, slots = rows_ref.shape[1:3]
-    tile = weights[0].shape[3]
+    out_ref, rows_ref, buf, sem = refs
+    _, owned, slots, depth = rows_ref.shape
+    ring = buf.shape[0]
+    units = gate_up_ref.shape[3]
     cols = recv[0][0].shape[2]
     per_expert = own_ref.shape[0] // owned
     groups = slots // per_expert
-
-    @pl.when((expert == 0) & (pl.program_id(1) == 0))
-    def _():
-        for i in range(shares):
-            for q in range(within):
-                place = meta_ref[1 + across + q]
-                start = (meta_ref[1 + begin + i] * within + place) * cols
-                lanes = pl.ds(pl.multiple_of(start, cols), cols)
-                into = pl.ds(pl.multiple_of(place * cols, cols), cols)
-                for e in range(owned):
-                    mine = slice(e * per_expert, (e + 1) * per_expert)
-                    rows_ref[i, e, 0:per_expert, into] = own_ref[mine, lanes]
-                    for k in range(1, groups):
-                        rows_ref[i, e, k * per_expert : (k + 1) * per_expert, into] = recv[i][q][k - 1, mine, :]
-
-    first_unit = pl.program_id(1) * tile
-    units = pl.ds(pl.multiple_of(first_unit, tile), tile)
-
-    def product(side):
-        total = jnp.dot(rows_ref[0, expert], weights[0][0, side], preferred_element_type=F32)
-        for i in range(1, shares):
-            total = total + jnp.dot(rows_ref[i, expert], weights[i][0, side], preferred_element_type=F32)
-        return total if first else total + sums_ref[expert, side, :, units]
-
-    if not last:
-        for side in range(2):
-            out_ref[expert, side, :, units] = product(side)
-        return
-    gate, up = product(0), product(1)
-    hidden = (gate * jax.nn.sigmoid(gate) * up).astype(BF16)
-    span = BLOCK_ROWS * STRIDE
-    unit = first_unit + lax.broadcasted_iota(jnp.int32, (1, tile), 1)
-    line = first_unit + lax.broadcasted_iota(jnp.int32, (tile, MAXCH * span), 0)
-    place = lax.broadcasted_iota(jnp.int32, (tile, MAXCH * span), 1)
-    hit = unit < 0
-    source = place % span
-    for entry in range(MAXCH):
-        block = list_ref[meta_ref[0] * owned + expert, entry]
-        hit = hit | (unit // span == block)
-        source = source + jnp.where(place // span == entry, block * span, 0)
-    pick = jnp.where(line == source, 1.0, 0.0).astype(BF16)
-    taken = jnp.dot(hidden, pick, preferred_element_type=F32).astype(BF16)
-    out_ref[expert, :, units] = hidden * jnp.where(hit, 0.0, 1.0).astype(BF16)
-
-    @pl.when(pl.program_id(1) == 0)
-    def _():
-        taken_ref[expert] = taken
-
-    @pl.when(pl.program_id(1) > 0)
-    def _():
-        taken_ref[expert] += taken
-
-
-def gate_up_stage(meta, block_list, begin, across, own, received, gate_up, sums, last):
+    work = [
+        (e, at, side, i)
+        for e in range(owned)
+        for at in range(0, units, tile)
+        for side in range(2)
+        for i in range(shares)
+    ]
+
+    def fetch(n):
+        e, at, side, i = work[n]
+        deep = pl.ds(pl.multiple_of(meta_ref[1 + begin + i] * depth, depth), depth)
+        source = gate_up_ref.at[e, side, deep, pl.ds(at, tile)]
+        return pltpu.make_async_copy(source, buf.at[n % ring], sem.at[n % ring])
+
+    for n in range(min(ring, len(work))):
+        fetch(n).start()
+    for i in range(shares):
+        for q in range(within):
+            place = meta_ref[1 + across + q]
+            start = (meta_ref[1 + begin + i] * within + place) * cols
+            lanes = pl.ds(pl.multiple_of(start, cols), cols)
+            into = pl.ds(pl.multiple_of(place * cols, cols), cols)
+            for e in range(owned):
+                mine = slice(e * per_expert, (e + 1) * per_expert)
+                rows_ref[i, e, 0:per_expert, into] = own_ref[mine, lanes]
+                for k in range(1, groups):
+                    rows_ref[i, e, k * per_expert : (k + 1) * per_expert, into] = recv[i][q][k - 1, mine, :]
+    total = gate = None
+    for n, (e, at, side, i) in enumerate(work):
+        fetch(n).wait()
+        product = jnp.dot(rows_ref[i, e], buf[n % ring], preferred_element_type=F32)
+        total = product if i == 0 else total + product
+        if n + ring < len(work):
+            fetch(n + ring).start()
+        if i < shares - 1:
+            continue
+        if not first:
+            total = total + sums_ref[e, side, :, at : at + tile]
+        if not last:
+            out_ref[e, side, :, at : at + tile] = total
+        elif side == 0:
+            gate = total
+        else:
+            out_ref[e, :, at : at + tile] = (gate * jax.nn.sigmoid(gate) * total).astype(BF16)
+
+
+def gate_up_stage(meta, begin, across, own, received, gate_up, sums, last):
     owned, _, width, units = gate_up.shape
     shares, within = len(received), len(received[0])
     depth = within * received[0][0].shape[2]
     slots = own.shape[0] // owned * (1 + received[0][0].shape[0])
     tile = min(UNIT_TILE, units)
+    ring = min(RING, owned * 2 * shares * (units // tile))
     vmem = pl.BlockSpec(memory_space=pltpu.VMEM)
     first = sums is None
     if last:
-        out_shape = [
-            jax.ShapeDtypeStruct((owned, slots, units), BF16),
-            jax.ShapeDtypeStruct((owned, slots, MAXCH * BLOCK_ROWS * STRIDE), BF16),
-        ]
+        out_shape = jax.ShapeDtypeStruct((owned, slots, units), BF16)
     else:
-        out_shape = [jax.ShapeDtypeStruct((owned, 2, slots, units), F32)]
-    weights = [
-        pl.BlockSpec((1, 2, depth, tile), lambda e, j, meta, _, i=i: (e, 0, meta[1 + begin + i], j))
-        for i in range(shares)
-    ]
-    inputs = [own, *sum([list(r) for r in received], []), *[in_hbm(gate_up)] * shares]
-    return pl.pallas_call(
-        functools.partial(gate_up_kernel, begin, shares, across, within, first, last),
+        out_shape = jax.ShapeDtypeStruct((owned, 2, slots, units), F32)
+    return pl.pallas_call(
+        functools.partial(gate_up_kernel, begin, shares, across, within, tile, first, last),
         grid_spec=pltpu.PrefetchScalarGridSpec(
-            num_scalar_prefetch=2,
-            grid=(owned, units // tile),
-            in_specs=[vmem] * (1 + shares * within) + weights + ([] if first else [vmem]),
-            out_specs=[vmem] * len(out_shape),
-            scratch_shapes=[pltpu.VMEM((shares, owned, slots, depth), BF16)],
+            num_scalar_prefetch=1,
+            grid=(),
+            in_specs=[vmem] * (1 + shares * within)
+            + [pl.BlockSpec(memory_space=pltpu.HBM)]
+            + ([] if first else [vmem]),
+            out_specs=vmem,
+            scratch_shapes=[
+                pltpu.VMEM((shares, owned, slots, depth), BF16),
+                pltpu.VMEM((ring, depth, tile), BF16),
+                pltpu.SemaphoreType.DMA((ring,)),
+            ],
         ),
         out_shape=out_shape,
-        input_output_aliases={} if first or last else {2 + len(inputs): 0},
         compiler_params=pltpu.CompilerParams(vmem_limit_bytes=STAGE_VMEM),
         cost_estimate=pl.CostEstimate(
             flops=4 * owned * slots * depth * units * shares,
@@ -337,57 +328,74 @@
             transcendentals=0,
         ),
         name="gate_up_stage",
-    )(meta, block_list, *inputs, *([] if first else [sums]))
-
-
-def fetch_kernel(down_ref, out_ref, sem):
-    copies = [
-        pltpu.make_async_copy(down_ref.at[e], out_ref.at[e], sem.at[e]) for e in range(down_ref.shape[0])
-    ]
-    for copy in copies:
-        copy.start()
-    for copy in copies:
-        copy.wait()
-
-
-def fetch_down(down_weight):
-    return pl.pallas_call(
-        fetch_kernel,
+    )(meta, own, *sum([list(r) for r in received], []), in_hbm(gate_up), *([] if first else [sums]))
+
+
+def fetch_kernel(expert, down_ref, out_ref, sem):
+    copy = pltpu.make_async_copy(down_ref.at[expert], out_ref, sem)
+    copy.start()
+    copy.wait()
+
+
+def fetch_down(down_weight, expert):
+    return pl.pallas_call(
+        functools.partial(fetch_kernel, expert),
         in_specs=[pl.BlockSpec(memory_space=pltpu.HBM)],
         out_specs=pl.BlockSpec(memory_space=pltpu.VMEM),
-        out_shape=pltpu.VMEM(down_weight.shape, down_weight.dtype),
-        scratch_shapes=[pltpu.SemaphoreType.DMA((down_weight.shape[0],))],
-        compiler_params=pltpu.CompilerParams(vmem_limit_bytes=SMALL_VMEM),
-        cost_estimate=pl.CostEstimate(flops=0, bytes_accessed=2 * down_weight.size, transcendentals=0),
+        out_shape=pltpu.VMEM(down_weight.shape[1:], down_weight.dtype),
+        scratch_shapes=[pltpu.SemaphoreType.DMA],
+        compiler_params=pltpu.CompilerParams(vmem_limit_bytes=SMALL_VMEM),
+        cost_estimate=SHORT,
         name="fetch_down",
     )(in_hbm(down_weight))
 
 
-def down_kernel(share, across, within, per_expert, meta_ref, list_ref, rest_ref, taken_ref, delta_ref, down_ref, *outs):
-    owned = down_ref.shape[0]
-    rows, cols = outs[0].shape
-    src_cols = delta_ref.shape[3]
-    groups = rest_ref.shape[1] // per_expert
+def patch_kernel(groups, owned, meta_ref, list_ref, *refs):
+    deltas, downs, outs = refs[:groups], refs[groups : groups + owned], refs[groups + owned :]
+    cols = deltas[0].shape[2]
     listed = MAXCH * BLOCK_ROWS
     span = BLOCK_ROWS * STRIDE
     row = lax.broadcasted_iota(jnp.int32, (MAXCH * span, listed), 0)
     col = lax.broadcasted_iota(jnp.int32, (MAXCH * span, listed), 1)
     spread = ((row // STRIDE == col) & (row % STRIDE == 0)).astype(F32).astype(BF16)
+    for k in range(groups):
+        source = lax.rem(meta_ref[0] - k + groups, groups)
+        lanes = pl.ds(pl.multiple_of(source * cols, cols), cols)
+        for e in range(owned):
+            added = jnp.dot(spread, deltas[k][e], preferred_element_type=F32)
+            for entry in range(MAXCH):
+                block = list_ref[meta_ref[0] * owned + e, entry]
+                where = pl.ds(pl.multiple_of(block * span, span), span)
+                fresh = downs[e][where, lanes].astype(F32) + added[entry * span : (entry + 1) * span]
+                outs[e][where, lanes] = fresh.astype(BF16)
+
+
+def patch_down(meta, block_list, deltas, downs):
+    groups, owned = len(deltas), len(downs)
+    vmem = pl.BlockSpec(memory_space=pltpu.VMEM)
+    return pl.pallas_call(
+        functools.partial(patch_kernel, groups, owned),
+        grid_spec=pltpu.PrefetchScalarGridSpec(
+            num_scalar_prefetch=2, grid=(), in_specs=[vmem] * (groups + owned), out_specs=[vmem] * owned
+        ),
+        out_shape=[pltpu.VMEM(d.shape, d.dtype) for d in downs],
+        input_output_aliases={2 + groups + e: e for e in range(owned)},
+        compiler_params=pltpu.CompilerParams(vmem_limit_bytes=SMALL_VMEM),
+        cost_estimate=SHORT,
+        name="patch_down",
+    )(meta, block_list, *deltas, *[pltpu.with_memory_space_constraint(d, pltpu.VMEM) for d in downs])
+
+
+def down_kernel(share, across, within, per_expert, meta_ref, hidden_ref, *refs):
+    owned, slots, _ = hidden_ref.shape
+    downs, outs = refs[:owned], refs[owned:]
+    rows, cols = outs[0].shape
+    groups = slots // per_expert
     for q in list(range(1, within)) + [0]:
         first_col = (meta_ref[1 + share] * within + meta_ref[1 + across + q]) * cols
-        source = first_col // src_cols
-        there = pl.ds(pl.multiple_of(first_col - source * src_cols, cols), cols)
         lanes = pl.ds(pl.multiple_of(first_col, cols), cols)
-        distance = lax.rem(meta_ref[0] - source + groups, groups)
         for e in range(owned):
-            added = jnp.dot(spread, delta_ref[distance, e, :, there], preferred_element_type=F32)
-            old = []
-            for entry in range(MAXCH):
-                block = list_ref[meta_ref[0] * owned + e, entry]
-                old.append(down_ref[e, pl.ds(pl.multiple_of(block * span, span), span), lanes])
-            fresh = (jnp.concatenate(old, axis=0).astype(F32) + added).astype(BF16)
-            part = jnp.dot(rest_ref[e], down_ref[e, :, lanes], preferred_element_type=F32)
-            part = (part + jnp.dot(taken_ref[e], fresh, preferred_element_type=F32)).astype(BF16)
+            part = jnp.dot(hidden_ref[e], downs[e][:, lanes], preferred_element_type=F32).astype(BF16)
             for k in range(groups):
                 at = (k * owned + e) * per_expert
                 part_of = PIECES * at // rows
@@ -396,15 +404,17 @@
                 into[at : at + per_expert, :] = part[k * per_expert : (k + 1) * per_expert]
 
 
-def down_pieces(meta, share, across, within, per_expert, block_list, rest, taken, delta, down_weight, cols):
-    owned, units, _ = down_weight.shape
-    slots = rest.shape[1]
+def down_pieces(meta, share, across, within, per_expert, hidden, downs, cols):
+    owned, slots, units = hidden.shape
     rows = owned * slots
     vmem = pl.BlockSpec(memory_space=pltpu.VMEM)
     return pl.pallas_call(
         functools.partial(down_kernel, share, across, within, per_expert),
         grid_spec=pltpu.PrefetchScalarGridSpec(
-            num_scalar_prefetch=2, grid=(), in_specs=[vmem] * 4, out_specs=[vmem] * (1 + PIECES * (within - 1))
+            num_scalar_prefetch=1,
+            grid=(),
+            in_specs=[vmem] * (1 + owned),
+            out_specs=[vmem] * (1 + PIECES * (within - 1)),
         ),
         out_shape=[jax.ShapeDtypeStruct((rows, cols), BF16)]
         + [jax.ShapeDtypeStruct((rows // PIECES, cols), BF16)] * (PIECES * (within - 1)),
@@ -415,7 +425,7 @@
             transcendentals=0,
         ),
         name="down_mixed",
-    )(meta, block_list, rest, taken, delta, down_weight)
+    )(meta, hidden, *downs)
 
 
 def swap(value, axis, distance):
@@ -460,32 +470,32 @@
     mine = own_slots(select, tokens)
     deltas = listed_deltas(meta, adam_first, adam_second, gradient, lists, counts, groups)
     down_source, deltas = lax.optimization_barrier((down_weight, deltas))
-    down_local = fetch_down(down_source)
-    arrived, deltas, mine, down_local = lax.optimization_barrier((arrived, deltas, mine, down_local))
+    downs = [fetch_down(down_source, 0)]
+    arrived, deltas, mine, downs = lax.optimization_barrier((arrived, deltas, mine, downs))
     away = jnp.stack(arrived)
     early = {k: shift(deltas[k], "expert", k) for k in (1, groups - 1)}
 
     def stage(begin, columns, sums, last):
         received = [[c] + [swap(c, "tensor", q) for q in range(1, within)] for c in columns]
-        return gate_up_stage(meta, lists, begin, across, mine, received, gate_up, sums, last)
+        return gate_up_stage(meta, begin, across, mine, received, gate_up, sums, last)
 
     others = [swap(away, "fsdp", r) for r in range(1, across)]
-    (sums,) = stage(0, [away], None, False)
+    sums = stage(0, [away], None, False)
     experts = adam_first.shape[0]
     parts_at = (experts // 4, experts // 4 + experts * 3 // 8, experts)
     adam_in = (adam_first, adam_second, gradient)
-    adam_in, deltas, early, sums = lax.optimization_barrier((adam_in, deltas, early, sums))
+    adam_in, down_source, deltas, early, sums = lax.optimization_barrier(
+        (adam_in, down_source, deltas, early, sums)
+    )
     late = {k: shift(deltas[k], "expert", k) for k in range(2, groups - 1)}
     filled = adam_part(*adam_in, 0, parts_at[0], cost=SHORT)
-    others, late, filled, sums = lax.optimization_barrier((others, late, filled, sums))
-    incoming = [{0: deltas[0], **early, **late}[k] for k in range(groups)]
-    incoming = jnp.stack(incoming)
-    rest, taken = stage(1, others, sums, True)
+    downs = downs + [fetch_down(down_source, e) for e in range(1, owned)]
+    downs = patch_down(meta, lists, [{0: deltas[0], **early, **late}[k] for k in range(groups)], downs)
+    others, downs, filled, sums = lax.optimization_barrier((others, downs, filled, sums))
+    hidden = stage(1, others, sums, True)
 
     def down(r, order):
-        pieces = down_pieces(
-            order, r, across, within, steps * CAP, lists, rest, taken, incoming, down_local, cols
-        )
+        pieces = down_pieces(order, r, across, within, steps * CAP, hidden, downs, cols)
         return pieces[0], [swap(pieces[i], "tensor", (i - 1) // PIECES + 1) for i in range(1, len(pieces))]
 
     def add(*terms):

time: 107 us -> 101 us (0.944)
  Pallas kernels: 65 us -> 57.1 us
  starting transfers between devices: 26.2 us -> 29 us
  waiting for transfers between devices: 11.4 us -> 9.69 us
    pallas_call x2, Pallas kernels: 23.2 us -> 16.6 us  [gate_up_stage(): pl.pallas_call(functools.partial(gate_up_kernel, begin, shares, across, w...]
    pallas_call x4, Pallas kernels: 11.1 us -> 7.21 us  [down_pieces(): pl.pallas_call(functools.partial(down_kernel, share, across, within, per_...]
    ppermute x9, waiting for transfers between devices: 2.91 us -> 0.27 us  [shift(): lax.ppermute(value, axis, [(i, (i + distance) % size) for i in range(size)])]
    pallas_call x1 -> x3, Pallas kernels: 5.88 us -> 8.19 us  [the longest x2 6.87 us: fetch_down(): pl.pallas_call(functools.partial(fetch_kernel, expert), in_specs=[pl.Bloc...]
    ppermute x9, starting transfers between devices: 14.8 us -> 16.8 us  [shift(): lax.ppermute(value, axis, [(i, (i + distance) % size) for i in range(size)])]
  transfers between devices with their start and end apart: 28 -> 28, of which waited for: 13 -> 11; matrix products, arithmetic and copies ran while one was open for 1% -> 1% of each run, Pallas kernels for 41% -> 41%
where the time goes in v4:
time: 101 us; the launch traced here: 99.9 us
  Pallas kernels  57.1 us (57%)
  starting transfers between devices  29 us (29%)
  waiting for transfers between devices  9.69 us (10%)
  local copies, waits for them, and re-layouts  2.38 us (2%)
    pallas_call x3, Pallas kernels, adam_part(): pl.pallas_call(adam_kernel, grid=(end - begin,), in_specs=[block, block,...  17.8 us
    ppermute x9, starting transfers between devices, shift(): lax.ppermute(value, axis, [(i, (i + distance) % size) for i in range(size)])  16.8 us
    pallas_call x2, Pallas kernels, gate_up_stage(): pl.pallas_call(functools.partial(gate_up_kernel, begin, shares, across, w...  16.6 us
    ppermute x19, starting transfers between devices, swap(): lax.ppermute(value, axis, [(i, i ^ distance) for i in range(lax.axis_size...  12.2 us
    ppermute x19, waiting for transfers between devices, swap(): lax.ppermute(value, axis, [(i, i ^ distance) for i in range(lax.axis_size...  9.42 us
    pallas_call x4, Pallas kernels, down_pieces(): pl.pallas_call(functools.partial(down_kernel, share, across, within, per_...  7.21 us
    pallas_call x2, Pallas kernels, fetch_down(): pl.pallas_call(functools.partial(fetch_kernel, expert), in_specs=[pl.Bloc...  6.87 us
    pallas_call x1, Pallas kernels, listed_deltas(): pl.pallas_call(functools.partial(delta_kernel, groups), grid_spec=pltpu.P...  3.72 us
  transfers between devices with their start and end apart: 28, of which 11 were waited for; matrix products, arithmetic and copies ran while one was open for 1% of the time, Pallas kernels for 41%

profile of v4, /device:TPU:0, one launch (start us, length us, event | category | flops | bytes accessed | tf_op | source)
XLA Modules:
  0.0 99.9 jit_solution(2945829189791064415)
XLA Ops:
  1.4 2.2 %pack_slots.1 = (bf16[128,512]{1,0:T(8,128)(2,1)S(1)}, bf16[128,512]{1,0:T(8,128)(2,1)S(1)}, bf16[128,512]{1,0:T(8,128)(2,1)S(1)}, bf16[128,128]{1,0:T(8,128)(2,1)S(1)}, bf16[2,128,512]{2,1,0:T(8,128)(2,1)S(1)}) custom-call(s32[8]{0:T(128)S(1)} %stack.47.meta_ref, bf16[2,64,4096]{2,1,0:T(8,128)(2,1)} %tokens_ref.3, s32[2,2,64]{2,1,0:T(2,128)S(1)} %bitcast.24), custom_call_target="tpu_custom_call" | custom-call | flops 10000000 | bytes 262144 | tf_op jit(solution)/shard_map/pack_slots/pallas_call | solution.py:90
  3.6 3.1 %collective-permute-start = (bf16[128,512]{1,0:T(8,128)(2,1)S(1)}, bf16[128,512]{1,0:T(8,128)(2,1)S(1)}, u32[]{:S(2)}, u32[]{:S(2)}) collective-permute-start(bf16[128,512]{1,0:T(8,128)(2,1)S(1)} %get-tuple-element.92), channel_id=1, source_target_pairs={{0,2},{2,4},{4,6},{6,0},{1,3},{3,5},{5,7},{7,1},{8,10},{10,12},{12... | collective-permute-start | bytes 393224 | tf_op jit(solution)/shard_map/ppermute | solution.py:437
  6.7 2.6 %collective-permute-start.1 = (bf16[128,512]{1,0:T(8,128)(2,1)S(1)}, bf16[128,512]{1,0:T(8,128)(2,1)S(1)}, u32[]{:S(2)}, u32[]{:S(2)}) collective-permute-start(bf16[128,512]{1,0:T(8,128)(2,1)S(1)} %get-tuple-element.93), channel_id=1, source_target_pairs={{0,4},{2,6},{4,0},{6,2},{1,5},{3,7},{5,1},{7,3},{8,12},{10,14},{12... | collective-permute-start | bytes 393224 | tf_op jit(solution)/shard_map/ppermute | solution.py:437
  12.0 3.7 %listed_deltas.1 = (bf16[2,32,1024]{2,1,0:T(8,128)(2,1)S(1)}, bf16[2,32,1024]{2,1,0:T(8,128)(2,1)S(1)}, bf16[2,32,1024]{2,1,0:T(8,128)(2,1)S(1)}, bf16[2,32,1024]{2,1,0:T(8,128)(2,1)S(1)}) custom-call(s32[8]{0:T(128)S(1)} %stack.47.meta_ref, s32[8,4]{1,0:T(8,128)S(1)} %copy.19.list_ref, s32[8]{0:T(128)S(1)} %bitcast.26, f32[8,256,1024]{2,1,0:T(8,128)} %first_ref.4, ...), custom_call_target="tpu_custom_call" | custom-call | flops 1000000 | bytes 3145728 | tf_op jit(solution)/shard_map/listed_deltas/pallas_call | solution.py:193
  15.8 3.5 %fetch_down.2.refs_4_ = bf16[1024,4096]{1,0:T(8,128)(2,1)S(1)} custom-call(bf16[2,1024,4096]{2,1,0:T(8,128)(2,1)} %down_ref.1), custom_call_target="tpu_custom_call" | custom-call | flops 1 | bytes 1 | tf_op jit(solution)/shard_map/fetch_down/pallas_call | solution.py:341
  20.0 2.4 %collective-permute-start.8 = (bf16[3,128,512]{2,1,0:T(8,128)(2,1)S(1)}, bf16[3,128,512]{2,1,0:T(8,128)(2,1)S(1)}, u32[]{:S(2)}, u32[]{:S(2)}) collective-permute-start(bf16[3,128,512]{2,1,0:T(8,128)(2,1)S(1)} %pad_maximum_fusion.refs_0_), channel_id=1, source_target_pairs={{0,24},{8,16},{16,8},{24,0},{1,25},{9,17},{17,9},{25,1},{2,26},{10... | collective-permute-start | bytes 1179656 | tf_op jit(solution)/shard_map/ppermute | solution.py:432
  24.9 2.5 %collective-permute-start.4 = (bf16[2,32,1024]{2,1,0:T(8,128)(2,1)S(1)}, bf16[2,32,1024]{2,1,0:T(8,128)(2,1)S(1)}, u32[]{:S(2)}, u32[]{:S(2)}) collective-permute-start(bf16[2,32,1024]{2,1,0:T(8,128)(2,1)S(1)} %get-tuple-element.103), channel_id=1, source_target_pairs={{0,6},{2,0},{4,2},{6,4},{1,7},{3,1},{5,3},{7,5},{8,14},{10,8},{12,... | collective-permute-start | bytes 393224 | tf_op jit(solution)/shard_map/ppermute | solution.py:437
  27.3 5.3 %gate_up_stage.2.refs_7_ = f32[2,2,256,1024]{3,2,1,0:T(8,128)S(1)} custom-call(s32[8]{0:T(128)S(1)} %stack.47.meta_ref, bf16[128,4096]{1,0:T(8,128)(2,1)S(1)} %own_slots.1.own_ref, bf16[3,128,512]{2,1,0:T(8,128)(2,1)S(1)} %pad_maximum_fusion.refs_0_, bf16[3,128,512]{2,1,0:T(8,128)(2,1)S(1)} %collective-permute-done.5.refs_1_, bf16[2,2,4096,1024]{3,2,1,0:T(8,128)(2,1)} %refs_6_.1), custom_call_target="tpu_custom_call" | custom-call | flops 2147483648 | bytes 8388608 | tf_op jit(solution)/shard_map/gate_up_stage/pallas_call | solution.py:308
  33.7 3.4 %fetch_down.3.refs_5_ = bf16[1024,4096]{1,0:T(8,128)(2,1)S(1)} custom-call(bf16[2,1024,4096]{2,1,0:T(8,128)(2,1)} %down_ref.1), custom_call_target="tpu_custom_call" | custom-call | flops 1 | bytes 1 | tf_op jit(solution)/shard_map/fetch_down/pallas_call | solution.py:341
  37.1 4.2 %adam_moments.3 = (f32[8,256,1024]{2,1,0:T(8,128)}, f32[8,256,1024]{2,1,0:T(8,128)}) custom-call(f32[8,256,1024]{2,1,0:T(8,128)} %first_ref.4, f32[8,256,1024]{2,1,0:T(8,128)} %second_ref.4, bf16[8,256,1024]{2,1,0:T(8,128)(2,1)} %grad_ref.4), custom_call_target="tpu_custom_call" | custom-call | flops 1 | bytes 1 | tf_op jit(solution)/shard_map/adam_moments/pallas_call | solution.py:225
  45.6 11.2 %gate_up_stage.3.hidden_ref = bf16[2,256,1024]{2,1,0:T(8,128)(2,1)S(1)} custom-call(s32[8]{0:T(128)S(1)} %stack.47.meta_ref, bf16[128,4096]{1,0:T(8,128)(2,1)S(1)} %own_slots.1.own_ref, bf16[3,128,512]{2,1,0:T(8,128)(2,1)S(1)} %collective-permute-done.6.refs_0_, bf16[3,128,512]{2,1,0:T(8,128)(2,1)S(1)} %collective-permute-done.10.refs_1_, ...), custom_call_target="tpu_custom_call" | custom-call | flops 6442450944 | bytes 25165824 | tf_op jit(solution)/shard_map/gate_up_stage/pallas_call | solution.py:308
  56.9 1.8 %down_mixed.4 = (bf16[512,512]{1,0:T(8,128)(2,1)S(1)}, bf16[256,512]{1,0:T(8,128)(2,1)S(1)}, bf16[256,512]{1,0:T(8,128)(2,1)S(1)}) custom-call(s32[8]{0:T(128)S(1)} %stack.47.meta_ref, bf16[2,256,1024]{2,1,0:T(8,128)(2,1)S(1)} %gate_up_stage.3.hidden_ref, bf16[1024,4096]{1,0:T(8,128)(2,1)S(1)} %get-tuple-element.128.refs_0_, ...), custom_call_target="tpu_custom_call" | custom-call | flops 1073741824 | bytes 4194304 | tf_op jit(solution)/shard_map/down_mixed/pallas_call | solution.py:411
  60.9 1.5 %collective-permute-start.17 = (bf16[256,512]{1,0:T(8,128)(2,1)S(1)}, bf16[256,512]{1,0:T(8,128)(2,1)S(1)}, u32[]{:S(2)}, u32[]{:S(2)}) collective-permute-start(bf16[256,512]{1,0:T(8,128)(2,1)S(1)} %get-tuple-element.145), channel_id=1, source_target_pairs={{0,8},{8,0},{16,24},{24,16},{1,9},{9,1},{17,25},{25,17},{2,10},{10... | collective-permute-start | bytes 786440 | tf_op jit(solution)/shard_map/ppermute | solution.py:432
  62.4 1.5 %collective-permute-start.18 = (bf16[256,512]{1,0:T(8,128)(2,1)S(1)}, bf16[256,512]{1,0:T(8,128)(2,1)S(1)}, u32[]{:S(2)}, u32[]{:S(2)}) collective-permute-start(bf16[256,512]{1,0:T(8,128)(2,1)S(1)} %get-tuple-element.146), channel_id=1, source_target_pairs={{0,16},{8,24},{16,0},{24,8},{1,17},{9,25},{17,1},{25,9},{2,18},{10... | collective-permute-start | bytes 786440 | tf_op jit(solution)/shard_map/ppermute | solution.py:432
  63.9 1.8 %down_mixed.7 = (bf16[512,512]{1,0:T(8,128)(2,1)S(1)}, bf16[256,512]{1,0:T(8,128)(2,1)S(1)}, bf16[256,512]{1,0:T(8,128)(2,1)S(1)}) custom-call(s32[8]{0:T(128)S(1)} %stack.47.meta_ref, bf16[2,256,1024]{2,1,0:T(8,128)(2,1)S(1)} %gate_up_stage.3.hidden_ref, bf16[1024,4096]{1,0:T(8,128)(2,1)S(1)} %get-tuple-element.128.refs_0_, ...), custom_call_target="tpu_custom_call" | custom-call | flops 1073741824 | bytes 4194304 | tf_op jit(solution)/shard_map/down_mixed/pallas_call | solution.py:411
  66.2 1.8 %down_mixed.6 = (bf16[512,512]{1,0:T(8,128)(2,1)S(1)}, bf16[256,512]{1,0:T(8,128)(2,1)S(1)}, bf16[256,512]{1,0:T(8,128)(2,1)S(1)}) custom-call(s32[8]{0:T(128)S(1)} %stack.47.meta_ref, bf16[2,256,1024]{2,1,0:T(8,128)(2,1)S(1)} %gate_up_stage.3.hidden_ref, bf16[1024,4096]{1,0:T(8,128)(2,1)S(1)} %get-tuple-element.128.refs_0_, ...), custom_call_target="tpu_custom_call" | custom-call | flops 1073741824 | bytes 4194304 | tf_op jit(solution)/shard_map/down_mixed/pallas_call | solution.py:411
  71.0 1.7 %collective-permute-start.24 = (bf16[512,512]{1,0:T(8,128)(2,1)S(1)}, bf16[512,512]{1,0:T(8,128)(2,1)S(1)}, u32[]{:S(2)}, u32[]{:S(2)}) collective-permute-start(bf16[512,512]{1,0:T(8,128)(2,1)S(1)} %add_convert_fusion.1), channel_id=1, source_target_pairs={{0,16},{8,24},{16,0},{24,8},{1,17},{9,25},{17,1},{25,9},{2,18},{10... | collective-permute-start | bytes 1572872 | tf_op jit(solution)/shard_map/ppermute | solution.py:432
  72.8 1.4 %collective-permute-start.23 = (bf16[512,512]{1,0:T(8,128)(2,1)S(1)}, bf16[512,512]{1,0:T(8,128)(2,1)S(1)}, u32[]{:S(2)}, u32[]{:S(2)}) collective-permute-start(bf16[512,512]{1,0:T(8,128)(2,1)S(1)} %add_convert_fusion.2), channel_id=1, source_target_pairs={{0,8},{8,0},{16,24},{24,16},{1,9},{9,1},{17,25},{25,17},{2,10},{10... | collective-permute-start | bytes 1572872 | tf_op jit(solution)/shard_map/ppermute | solution.py:432
  74.2 1.8 %down_mixed.5 = (bf16[512,512]{1,0:T(8,128)(2,1)S(1)}, bf16[256,512]{1,0:T(8,128)(2,1)S(1)}, bf16[256,512]{1,0:T(8,128)(2,1)S(1)}) custom-call(s32[8]{0:T(128)S(1)} %stack.47.meta_ref, bf16[2,256,1024]{2,1,0:T(8,128)(2,1)S(1)} %gate_up_stage.3.hidden_ref, bf16[1024,4096]{1,0:T(8,128)(2,1)S(1)} %get-tuple-element.128.refs_0_, ...), custom_call_target="tpu_custom_call" | custom-call | flops 1073741824 | bytes 4194304 | tf_op jit(solution)/shard_map/down_mixed/pallas_call | solution.py:411
  76.6 6.8 %adam_moments.4 = (f32[8,256,1024]{2,1,0:T(8,128)}, f32[8,256,1024]{2,1,0:T(8,128)}) custom-call(f32[8,256,1024]{2,1,0:T(8,128)} %first_ref.4, f32[8,256,1024]{2,1,0:T(8,128)} %second_ref.4, bf16[8,256,1024]{2,1,0:T(8,128)(2,1)} %grad_ref.4, f32[8,256,1024]{2,1,0:T(8,128)} %get-tuple-element.138.refs_0_, ...), custom_call_target="tpu_custom_call", output_to_operand_aliasing={{0}: (3, {}), {1}: (4, {})} | custom-call | flops 6291456 | bytes 14155776 | tf_op jit(solution)/shard_map/adam_moments/pallas_call | solution.py:225
  83.4 1.6 %collective-permute-done.24 = bf16[512,512]{1,0:T(8,128)(2,1)S(1)} collective-permute-done((bf16[512,512]{1,0:T(8,128)(2,1)S(1)}, bf16[512,512]{1,0:T(8,128)(2,1)S(1)}, u32[]{:S(2)}, u32[]{:S(2)}) %collective-permute-start.24) | collective-permute-done | bytes 524320 | tf_op jit(solution)/shard_map/ppermute | solution.py:432
  85.0 1.6 %collective-permute-done.23 = bf16[512,512]{1,0:T(8,128)(2,1)S(1)} collective-permute-done((bf16[512,512]{1,0:T(8,128)(2,1)S(1)}, bf16[512,512]{1,0:T(8,128)(2,1)S(1)}, u32[]{:S(2)}, u32[]{:S(2)}) %collective-permute-start.23) | collective-permute-done | bytes 524320 | tf_op jit(solution)/shard_map/ppermute | solution.py:432
  89.0 2.8 %collective-permute-start.25 = (bf16[128,512]{1,0:T(8,128)(2,1)S(1)}, bf16[128,512]{1,0:T(8,128)(2,1)S(1)}, u32[]{:S(2)}, u32[]{:S(2)}) collective-permute-start(bf16[128,512]{1,0:T(8,128)(2,1)S(1)} %get-tuple-element.171), channel_id=1, source_target_pairs={{0,6},{2,0},{4,2},{6,4},{1,7},{3,1},{5,3},{7,5},{8,14},{10,8},{12,... | collective-permute-start | bytes 393224 | tf_op jit(solution)/shard_map/ppermute | solution.py:437
  91.9 6.8 %adam_moments.5 = (f32[8,256,1024]{2,1,0:T(8,128)}, f32[8,256,1024]{2,1,0:T(8,128)}) custom-call(f32[8,256,1024]{2,1,0:T(8,128)} %first_ref.4, f32[8,256,1024]{2,1,0:T(8,128)} %second_ref.4, bf16[8,256,1024]{2,1,0:T(8,128)(2,1)} %grad_ref.4, f32[8,256,1024]{2,1,0:T(8,128)} %get-tuple-element.165.refs_0_, ...), custom_call_target="tpu_custom_call", output_to_operand_aliasing={{0}: (3, {}), {1}: (4, {})} | custom-call | flops 6291456 | bytes 14155776 | tf_op jit(solution)/shard_map/adam_moments/pallas_call | solution.py:225
  (65 shorter events, 21.9 us)
Async XLA Ops:
  3.6 16.2 %collective-permute-start = (bf16[128,512]{1,0:T(8,128)(2,1)S(1)}, bf16[128,512]{1,0:T(8,128)(2,1)S(1)}, u32[]{:S(2)}, u32[]{:S(2)}) collective-permute-start(bf16[128,512]{1,0:T(8,128)(2,1)S(1)} %get-tuple-element.92), channel_id=1, source_target_pairs={{0,2},{2,4},{4,6},{6,0},{1,3},{3,5},{5,7},{7,1},{8,10},{10,12},{12... | collective-permute-start | bytes 393224 | tf_op jit(solution)/shard_map/ppermute | solution.py:437
  6.7 13.1 %collective-permute-start.1 = (bf16[128,512]{1,0:T(8,128)(2,1)S(1)}, bf16[128,512]{1,0:T(8,128)(2,1)S(1)}, u32[]{:S(2)}, u32[]{:S(2)}) collective-permute-start(bf16[128,512]{1,0:T(8,128)(2,1)S(1)} %get-tuple-element.93), channel_id=1, source_target_pairs={{0,4},{2,6},{4,0},{6,2},{1,5},{3,7},{5,1},{7,3},{8,12},{10,14},{12... | collective-permute-start | bytes 393224 | tf_op jit(solution)/shard_map/ppermute | solution.py:437
  9.3 10.5 %collective-permute-start.2 = (bf16[128,512]{1,0:T(8,128)(2,1)S(1)}, bf16[128,512]{1,0:T(8,128)(2,1)S(1)}, u32[]{:S(2)}, u32[]{:S(2)}) collective-permute-start(bf16[128,512]{1,0:T(8,128)(2,1)S(1)} %get-tuple-element.94), channel_id=1, source_target_pairs={{0,6},{2,0},{4,2},{6,4},{1,7},{3,1},{5,3},{7,5},{8,14},{10,8},{12,... | collective-permute-start | bytes 393224 | tf_op jit(solution)/shard_map/ppermute | solution.py:437
  19.9 5.0 %collective-permute-start.5 = (bf16[3,128,512]{2,1,0:T(8,128)(2,1)S(1)}, bf16[3,128,512]{2,1,0:T(8,128)(2,1)S(1)}, u32[]{:S(2)}, u32[]{:S(2)}) collective-permute-start(bf16[3,128,512]{2,1,0:T(8,128)(2,1)S(1)} %pad_maximum_fusion.refs_0_), channel_id=1, source_target_pairs={{0,1},{1,0},{2,3},{3,2},{4,5},{5,4},{6,7},{7,6},{8,9},{9,8},{10,11... | collective-permute-start | bytes 1179656 | tf_op jit(solution)/shard_map/ppermute | solution.py:432
  20.0 22.7 %collective-permute-start.8 = (bf16[3,128,512]{2,1,0:T(8,128)(2,1)S(1)}, bf16[3,128,512]{2,1,0:T(8,128)(2,1)S(1)}, u32[]{:S(2)}, u32[]{:S(2)}) collective-permute-start(bf16[3,128,512]{2,1,0:T(8,128)(2,1)S(1)} %pad_maximum_fusion.refs_0_), channel_id=1, source_target_pairs={{0,24},{8,16},{16,8},{24,0},{1,25},{9,17},{17,9},{25,1},{2,26},{10... | collective-permute-start | bytes 1179656 | tf_op jit(solution)/shard_map/ppermute | solution.py:432
  22.4 20.3 %collective-permute-start.7 = (bf16[3,128,512]{2,1,0:T(8,128)(2,1)S(1)}, bf16[3,128,512]{2,1,0:T(8,128)(2,1)S(1)}, u32[]{:S(2)}, u32[]{:S(2)}) collective-permute-start(bf16[3,128,512]{2,1,0:T(8,128)(2,1)S(1)} %pad_maximum_fusion.refs_0_), channel_id=1, source_target_pairs={{0,16},{8,24},{16,0},{24,8},{1,17},{9,25},{17,1},{25,9},{2,18},{10... | collective-permute-start | bytes 1179656 | tf_op jit(solution)/shard_map/ppermute | solution.py:432
  22.9 19.8 %collective-permute-start.6 = (bf16[3,128,512]{2,1,0:T(8,128)(2,1)S(1)}, bf16[3,128,512]{2,1,0:T(8,128)(2,1)S(1)}, u32[]{:S(2)}, u32[]{:S(2)}) collective-permute-start(bf16[3,128,512]{2,1,0:T(8,128)(2,1)S(1)} %pad_maximum_fusion.refs_0_), channel_id=1, source_target_pairs={{0,8},{8,0},{16,24},{24,16},{1,9},{9,1},{17,25},{25,17},{2,10},{10... | collective-permute-start | bytes 1179656 | tf_op jit(solution)/shard_map/ppermute | solution.py:432
  23.5 9.2 %collective-permute-start.3 = (bf16[2,32,1024]{2,1,0:T(8,128)(2,1)S(1)}, bf16[2,32,1024]{2,1,0:T(8,128)(2,1)S(1)}, u32[]{:S(2)}, u32[]{:S(2)}) collective-permute-start(bf16[2,32,1024]{2,1,0:T(8,128)(2,1)S(1)} %get-tuple-element.101), channel_id=1, source_target_pairs={{0,2},{2,4},{4,6},{6,0},{1,3},{3,5},{5,7},{7,1},{8,10},{10,12},{12... | collective-permute-start | bytes 393224 | tf_op jit(solution)/shard_map/ppermute | solution.py:437
  24.9 7.8 %collective-permute-start.4 = (bf16[2,32,1024]{2,1,0:T(8,128)(2,1)S(1)}, bf16[2,32,1024]{2,1,0:T(8,128)(2,1)S(1)}, u32[]{:S(2)}, u32[]{:S(2)}) collective-permute-start(bf16[2,32,1024]{2,1,0:T(8,128)(2,1)S(1)} %get-tuple-element.103), channel_id=1, source_target_pairs={{0,6},{2,0},{4,2},{6,4},{1,7},{3,1},{5,3},{7,5},{8,14},{10,8},{12,... | collective-permute-start | bytes 393224 | tf_op jit(solution)/shard_map/ppermute | solution.py:437
  32.7 8.7 %collective-permute-start.9 = (bf16[2,32,1024]{2,1,0:T(8,128)(2,1)S(1)}, bf16[2,32,1024]{2,1,0:T(8,128)(2,1)S(1)}, u32[]{:S(2)}, u32[]{:S(2)}) collective-permute-start(bf16[2,32,1024]{2,1,0:T(8,128)(2,1)S(1)} %get-tuple-element.113), channel_id=1, source_target_pairs={{0,4},{2,6},{4,0},{6,2},{1,5},{3,7},{5,1},{7,3},{8,12},{10,14},{12... | collective-permute-start | bytes 393224 | tf_op jit(solution)/shard_map/ppermute | solution.py:437
  42.8 2.3 %collective-permute-start.11 = (bf16[3,128,512]{2,1,0:T(8,128)(2,1)S(1)}, bf16[3,128,512]{2,1,0:T(8,128)(2,1)S(1)}, u32[]{:S(2)}, u32[]{:S(2)}) collective-permute-start(bf16[3,128,512]{2,1,0:T(8,128)(2,1)S(1)} %collective-permute-done.7.refs_2_), channel_id=1, source_target_pairs={{0,1},{1,0},{2,3},{3,2},{4,5},{5,4},{6,7},{7,6},{8,9},{9,8},{10,11... | collective-permute-start | bytes 1179656 | tf_op jit(solution)/shard_map/ppermute | solution.py:432
  43.3 2.3 %collective-permute-start.12 = (bf16[3,128,512]{2,1,0:T(8,128)(2,1)S(1)}, bf16[3,128,512]{2,1,0:T(8,128)(2,1)S(1)}, u32[]{:S(2)}, u32[]{:S(2)}) collective-permute-start(bf16[3,128,512]{2,1,0:T(8,128)(2,1)S(1)} %collective-permute-done.8.refs_4_), channel_id=1, source_target_pairs={{0,1},{1,0},{2,3},{3,2},{4,5},{5,4},{6,7},{7,6},{8,9},{9,8},{10,11... | collective-permute-start | bytes 1179656 | tf_op jit(solution)/shard_map/ppermute | solution.py:432
  60.9 8.4 %collective-permute-start.17 = (bf16[256,512]{1,0:T(8,128)(2,1)S(1)}, bf16[256,512]{1,0:T(8,128)(2,1)S(1)}, u32[]{:S(2)}, u32[]{:S(2)}) collective-permute-start(bf16[256,512]{1,0:T(8,128)(2,1)S(1)} %get-tuple-element.145), channel_id=1, source_target_pairs={{0,8},{8,0},{16,24},{24,16},{1,9},{9,1},{17,25},{25,17},{2,10},{10... | collective-permute-start | bytes 786440 | tf_op jit(solution)/shard_map/ppermute | solution.py:432
  62.4 8.1 %collective-permute-start.18 = (bf16[256,512]{1,0:T(8,128)(2,1)S(1)}, bf16[256,512]{1,0:T(8,128)(2,1)S(1)}, u32[]{:S(2)}, u32[]{:S(2)}) collective-permute-start(bf16[256,512]{1,0:T(8,128)(2,1)S(1)} %get-tuple-element.146), channel_id=1, source_target_pairs={{0,16},{8,24},{16,0},{24,8},{1,17},{9,25},{17,1},{25,9},{2,18},{10... | collective-permute-start | bytes 786440 | tf_op jit(solution)/shard_map/ppermute | solution.py:432
  65.7 4.8 %collective-permute-start.21 = (bf16[256,512]{1,0:T(8,128)(2,1)S(1)}, bf16[256,512]{1,0:T(8,128)(2,1)S(1)}, u32[]{:S(2)}, u32[]{:S(2)}) collective-permute-start(bf16[256,512]{1,0:T(8,128)(2,1)S(1)} %get-tuple-element.151), channel_id=1, source_target_pairs={{0,1},{1,0},{2,3},{3,2},{4,5},{5,4},{6,7},{7,6},{8,9},{9,8},{10,11... | collective-permute-start | bytes 786440 | tf_op jit(solution)/shard_map/ppermute | solution.py:432
  65.8 4.7 %collective-permute-start.22 = (bf16[256,512]{1,0:T(8,128)(2,1)S(1)}, bf16[256,512]{1,0:T(8,128)(2,1)S(1)}, u32[]{:S(2)}, u32[]{:S(2)}) collective-permute-start(bf16[256,512]{1,0:T(8,128)(2,1)S(1)} %get-tuple-element.152), channel_id=1, source_target_pairs={{0,1},{1,0},{2,3},{3,2},{4,5},{5,4},{6,7},{7,6},{8,9},{9,8},{10,11... | collective-permute-start | bytes 786440 | tf_op jit(solution)/shard_map/ppermute | solution.py:432
  68.1 2.4 %collective-permute-start.19 = (bf16[256,512]{1,0:T(8,128)(2,1)S(1)}, bf16[256,512]{1,0:T(8,128)(2,1)S(1)}, u32[]{:S(2)}, u32[]{:S(2)}) collective-permute-start(bf16[256,512]{1,0:T(8,128)(2,1)S(1)} %get-tuple-element.148), channel_id=1, source_target_pairs={{0,1},{1,0},{2,3},{3,2},{4,5},{5,4},{6,7},{7,6},{8,9},{9,8},{10,11... | collective-permute-start | bytes 786440 | tf_op jit(solution)/shard_map/ppermute | solution.py:432
  71.0 14.0 %collective-permute-start.24 = (bf16[512,512]{1,0:T(8,128)(2,1)S(1)}, bf16[512,512]{1,0:T(8,128)(2,1)S(1)}, u32[]{:S(2)}, u32[]{:S(2)}) collective-permute-start(bf16[512,512]{1,0:T(8,128)(2,1)S(1)} %add_convert_fusion.1), channel_id=1, source_target_pairs={{0,16},{8,24},{16,0},{24,8},{1,17},{9,25},{17,1},{25,9},{2,18},{10... | collective-permute-start | bytes 1572872 | tf_op jit(solution)/shard_map/ppermute | solution.py:432
  72.8 13.8 %collective-permute-start.23 = (bf16[512,512]{1,0:T(8,128)(2,1)S(1)}, bf16[512,512]{1,0:T(8,128)(2,1)S(1)}, u32[]{:S(2)}, u32[]{:S(2)}) collective-permute-start(bf16[512,512]{1,0:T(8,128)(2,1)S(1)} %add_convert_fusion.2), channel_id=1, source_target_pairs={{0,8},{8,0},{16,24},{24,16},{1,9},{9,1},{17,25},{25,17},{2,10},{10... | collective-permute-start | bytes 1572872 | tf_op jit(solution)/shard_map/ppermute | solution.py:432
  76.0 7.4 %collective-permute-start.15 = (bf16[256,512]{1,0:T(8,128)(2,1)S(1)}, bf16[256,512]{1,0:T(8,128)(2,1)S(1)}, u32[]{:S(2)}, u32[]{:S(2)}) collective-permute-start(bf16[256,512]{1,0:T(8,128)(2,1)S(1)} %get-tuple-element.143), channel_id=1, source_target_pairs={{0,1},{1,0},{2,3},{3,2},{4,5},{5,4},{6,7},{7,6},{8,9},{9,8},{10,11... | collective-permute-start | bytes 786440 | tf_op jit(solution)/shard_map/ppermute | solution.py:432
  76.1 7.3 %collective-permute-start.16 = (bf16[256,512]{1,0:T(8,128)(2,1)S(1)}, bf16[256,512]{1,0:T(8,128)(2,1)S(1)}, u32[]{:S(2)}, u32[]{:S(2)}) collective-permute-start(bf16[256,512]{1,0:T(8,128)(2,1)S(1)} %get-tuple-element.144), channel_id=1, source_target_pairs={{0,1},{1,0},{2,3},{3,2},{4,5},{5,4},{6,7},{7,6},{8,9},{9,8},{10,11... | collective-permute-start | bytes 786440 | tf_op jit(solution)/shard_map/ppermute | solution.py:432
  86.9 11.7 %collective-permute-start.27 = (bf16[128,512]{1,0:T(8,128)(2,1)S(1)}, bf16[128,512]{1,0:T(8,128)(2,1)S(1)}, u32[]{:S(2)}, u32[]{:S(2)}) collective-permute-start(bf16[128,512]{1,0:T(8,128)(2,1)S(1)} %get-tuple-element.169), channel_id=1, source_target_pairs={{0,2},{2,4},{4,6},{6,0},{1,3},{3,5},{5,7},{7,1},{8,10},{10,12},{12... | collective-permute-start | bytes 393224 | tf_op jit(solution)/shard_map/ppermute | solution.py:437
  88.2 10.7 %collective-permute-start.26 = (bf16[128,512]{1,0:T(8,128)(2,1)S(1)}, bf16[128,512]{1,0:T(8,128)(2,1)S(1)}, u32[]{:S(2)}, u32[]{:S(2)}) collective-permute-start(bf16[128,512]{1,0:T(8,128)(2,1)S(1)} %get-tuple-element.170), channel_id=1, source_target_pairs={{0,4},{2,6},{4,0},{6,2},{1,5},{3,7},{5,1},{7,3},{8,12},{10,14},{12... | collective-permute-start | bytes 393224 | tf_op jit(solution)/shard_map/ppermute | solution.py:437
  89.0 9.9 %collective-permute-start.25 = (bf16[128,512]{1,0:T(8,128)(2,1)S(1)}, bf16[128,512]{1,0:T(8,128)(2,1)S(1)}, u32[]{:S(2)}, u32[]{:S(2)}) collective-permute-start(bf16[128,512]{1,0:T(8,128)(2,1)S(1)} %get-tuple-element.171), channel_id=1, source_target_pairs={{0,6},{2,0},{4,2},{6,4},{1,7},{3,1},{5,3},{7,5},{8,14},{10,8},{12,... | collective-permute-start | bytes 393224 | tf_op jit(solution)/shard_map/ppermute | solution.py:437
  (8 other events, 21.6 us)

commit v5 on v4

--- a/solution.py
+++ b/solution.py
@@ -12,6 +12,7 @@
 MAXCH = 4
 CAP = 32
 PIECES = 2
+ADAM_ROWS = 128
 RING = 12
 UNIT_TILE = 512
 
@@ -220,11 +221,12 @@
 
 def adam_part(adam_first, adam_second, gradient, begin, end, filled=(), cost=None):
     _, rows, cols = adam_first.shape
-    block = pl.BlockSpec((1, rows, cols), lambda e: (begin + e, 0, 0))
+    lines = min(ADAM_ROWS, rows)
+    block = pl.BlockSpec((1, lines, cols), lambda e, j: (begin + e, j, 0))
     size = (end - begin) * rows * cols
     return pl.pallas_call(
         adam_kernel,
-        grid=(end - begin,),
+        grid=(end - begin, rows // lines),
         in_specs=[block, block, block] + [pl.BlockSpec(memory_space=pltpu.HBM)] * len(filled),
         out_specs=[block, block],
         out_shape=[jax.ShapeDtypeStruct(adam_first.shape, F32)] * 2,
@@ -475,14 +477,16 @@
     away = jnp.stack(arrived)
     early = {k: shift(deltas[k], "expert", k) for k in (1, groups - 1)}
 
-    def stage(begin, columns, sums, last):
-        received = [[c] + [swap(c, "tensor", q) for q in range(1, within)] for c in columns]
+    def stage(begin, received, sums, last):
         return gate_up_stage(meta, begin, across, mine, received, gate_up, sums, last)
 
+    def with_other_cores(columns):
+        return [columns] + [swap(columns, "tensor", q) for q in range(1, within)]
+
     others = [swap(away, "fsdp", r) for r in range(1, across)]
-    sums = stage(0, [away], None, False)
+    sums = stage(0, [with_other_cores(away)], None, False)
     experts = adam_first.shape[0]
-    parts_at = (experts // 4, experts // 4 + experts * 3 // 8, experts)
+    parts_at = (experts // 8, experts * 5 // 8, experts)
     adam_in = (adam_first, adam_second, gradient)
     adam_in, down_source, deltas, early, sums = lax.optimization_barrier(
         (adam_in, down_source, deltas, early, sums)
@@ -490,9 +494,11 @@
     late = {k: shift(deltas[k], "expert", k) for k in range(2, groups - 1)}
     filled = adam_part(*adam_in, 0, parts_at[0], cost=SHORT)
     downs = downs + [fetch_down(down_source, e) for e in range(1, owned)]
+    near, downs = lax.optimization_barrier((others[:-1], downs))
+    near = [with_other_cores(columns) for columns in near]
     downs = patch_down(meta, lists, [{0: deltas[0], **early, **late}[k] for k in range(groups)], downs)
-    others, downs, filled, sums = lax.optimization_barrier((others, downs, filled, sums))
-    hidden = stage(1, others, sums, True)
+    far, downs, filled, sums = lax.optimization_barrier((others[-1], downs, filled, sums))
+    hidden = stage(1, near + [with_other_cores(far)], sums, True)
 
     def down(r, order):
         pieces = down_pieces(order, r, across, within, steps * CAP, hidden, downs, cols)

time: 101 us -> 99.4 us (0.984)
  waiting for transfers between devices: 9.69 us -> 6.61 us
  Pallas kernels: 57.1 us -> 58.3 us
    ppermute x19, waiting for transfers between devices: 9.42 us -> 6.15 us  [swap(): lax.ppermute(value, axis, [(i, i ^ distance) for i in range(lax.axis_size...]
    pallas_call x3, Pallas kernels: 17.8 us -> 19.1 us  [adam_part(): pl.pallas_call(adam_kernel, grid=(end - begin, rows // lines), in_specs=[...]
  transfers between devices with their start and end apart: 28 -> 28, of which waited for: 11 -> 8; matrix products, arithmetic and copies ran while one was open for 1% -> 1% of each run, Pallas kernels for 41% -> 43%
where the time goes in v5:
time: 99.4 us; the launch traced here: 98.3 us
  Pallas kernels  58.3 us (59%)
  starting transfers between devices  29.2 us (29%)
  waiting for transfers between devices  6.61 us (7%)
  local copies, waits for them, and re-layouts  2.38 us (2%)
    pallas_call x3, Pallas kernels, adam_part(): pl.pallas_call(adam_kernel, grid=(end - begin, rows // lines), in_specs=[...  19.1 us
    ppermute x9, starting transfers between devices, shift(): lax.ppermute(value, axis, [(i, (i + distance) % size) for i in range(size)])  16.8 us
    pallas_call x2, Pallas kernels, gate_up_stage(): pl.pallas_call(functools.partial(gate_up_kernel, begin, shares, across, w...  16.6 us
    ppermute x19, starting transfers between devices, swap(): lax.ppermute(value, axis, [(i, i ^ distance) for i in range(lax.axis_size...  12.4 us
    pallas_call x4, Pallas kernels, down_pieces(): pl.pallas_call(functools.partial(down_kernel, share, across, within, per_...  7.21 us
    pallas_call x2, Pallas kernels, fetch_down(): pl.pallas_call(functools.partial(fetch_kernel, expert), in_specs=[pl.Bloc...  6.87 us
    ppermute x19, waiting for transfers between devices, swap(): lax.ppermute(value, axis, [(i, i ^ distance) for i in range(lax.axis_size...  6.15 us
    pallas_call x1, Pallas kernels, listed_deltas(): pl.pallas_call(functools.partial(delta_kernel, groups), grid_spec=pltpu.P...  3.66 us
  transfers between devices with their start and end apart: 28, of which 8 were waited for; matrix products, arithmetic and copies ran while one was open for 1% of the time, Pallas kernels for 43%

profile of v5, /device:TPU:0, one launch (start us, length us, event | category | flops | bytes accessed | tf_op | source)
XLA Modules:
  0.0 98.3 jit_solution(958609631434927215)
XLA Ops:
  1.4 2.2 %pack_slots.1 = (bf16[128,512]{1,0:T(8,128)(2,1)S(1)}, bf16[128,512]{1,0:T(8,128)(2,1)S(1)}, bf16[128,512]{1,0:T(8,128)(2,1)S(1)}, bf16[128,128]{1,0:T(8,128)(2,1)S(1)}, bf16[2,128,512]{2,1,0:T(8,128)(2,1)S(1)}) custom-call(s32[8]{0:T(128)S(1)} %stack.47.meta_ref, bf16[2,64,4096]{2,1,0:T(8,128)(2,1)} %tokens_ref.3, s32[2,2,64]{2,1,0:T(2,128)S(1)} %bitcast.24), custom_call_target="tpu_custom_call" | custom-call | flops 10000000 | bytes 262144 | tf_op jit(solution)/shard_map/pack_slots/pallas_call | solution.py:91
  3.6 3.1 %collective-permute-start = (bf16[128,512]{1,0:T(8,128)(2,1)S(1)}, bf16[128,512]{1,0:T(8,128)(2,1)S(1)}, u32[]{:S(2)}, u32[]{:S(2)}) collective-permute-start(bf16[128,512]{1,0:T(8,128)(2,1)S(1)} %get-tuple-element.94), channel_id=1, source_target_pairs={{0,2},{2,4},{4,6},{6,0},{1,3},{3,5},{5,7},{7,1},{8,10},{10,12},{12... | collective-permute-start | bytes 393224 | tf_op jit(solution)/shard_map/ppermute | solution.py:439
  6.7 2.6 %collective-permute-start.1 = (bf16[128,512]{1,0:T(8,128)(2,1)S(1)}, bf16[128,512]{1,0:T(8,128)(2,1)S(1)}, u32[]{:S(2)}, u32[]{:S(2)}) collective-permute-start(bf16[128,512]{1,0:T(8,128)(2,1)S(1)} %get-tuple-element.95), channel_id=1, source_target_pairs={{0,4},{2,6},{4,0},{6,2},{1,5},{3,7},{5,1},{7,3},{8,12},{10,14},{12... | collective-permute-start | bytes 393224 | tf_op jit(solution)/shard_map/ppermute | solution.py:439
  12.0 3.7 %listed_deltas.1 = (bf16[2,32,1024]{2,1,0:T(8,128)(2,1)S(1)}, bf16[2,32,1024]{2,1,0:T(8,128)(2,1)S(1)}, bf16[2,32,1024]{2,1,0:T(8,128)(2,1)S(1)}, bf16[2,32,1024]{2,1,0:T(8,128)(2,1)S(1)}) custom-call(s32[8]{0:T(128)S(1)} %stack.47.meta_ref, s32[8,4]{1,0:T(8,128)S(1)} %copy.19.list_ref, s32[8]{0:T(128)S(1)} %bitcast.26, f32[8,256,1024]{2,1,0:T(8,128)} %first_ref.4, ...), custom_call_target="tpu_custom_call" | custom-call | flops 1000000 | bytes 3145728 | tf_op jit(solution)/shard_map/listed_deltas/pallas_call | solution.py:194
  15.7 3.5 %fetch_down.2.refs_4_ = bf16[1024,4096]{1,0:T(8,128)(2,1)S(1)} custom-call(bf16[2,1024,4096]{2,1,0:T(8,128)(2,1)} %down_ref.1), custom_call_target="tpu_custom_call" | custom-call | flops 1 | bytes 1 | tf_op jit(solution)/shard_map/fetch_down/pallas_call | solution.py:343
  19.9 1.6 %collective-permute-start.9 = (bf16[3,128,512]{2,1,0:T(8,128)(2,1)S(1)}, bf16[3,128,512]{2,1,0:T(8,128)(2,1)S(1)}, u32[]{:S(2)}, u32[]{:S(2)}) collective-permute-start(bf16[3,128,512]{2,1,0:T(8,128)(2,1)S(1)} %pad_maximum_fusion.refs_0_), channel_id=1, source_target_pairs={{0,16},{8,24},{16,0},{24,8},{1,17},{9,25},{17,1},{25,9},{2,18},{10... | collective-permute-start | bytes 1179656 | tf_op jit(solution)/shard_map/ppermute | solution.py:434
  21.6 1.4 %collective-permute-start.8 = (bf16[3,128,512]{2,1,0:T(8,128)(2,1)S(1)}, bf16[3,128,512]{2,1,0:T(8,128)(2,1)S(1)}, u32[]{:S(2)}, u32[]{:S(2)}) collective-permute-start(bf16[3,128,512]{2,1,0:T(8,128)(2,1)S(1)} %pad_maximum_fusion.refs_0_), channel_id=1, source_target_pairs={{0,8},{8,0},{16,24},{24,16},{1,9},{9,1},{17,25},{25,17},{2,10},{10... | collective-permute-start | bytes 1179656 | tf_op jit(solution)/shard_map/ppermute | solution.py:434
  24.9 2.4 %collective-permute-start.4 = (bf16[2,32,1024]{2,1,0:T(8,128)(2,1)S(1)}, bf16[2,32,1024]{2,1,0:T(8,128)(2,1)S(1)}, u32[]{:S(2)}, u32[]{:S(2)}) collective-permute-start(bf16[2,32,1024]{2,1,0:T(8,128)(2,1)S(1)} %get-tuple-element.105), channel_id=1, source_target_pairs={{0,6},{2,0},{4,2},{6,4},{1,7},{3,1},{5,3},{7,5},{8,14},{10,8},{12,... | collective-permute-start | bytes 393224 | tf_op jit(solution)/shard_map/ppermute | solution.py:439
  27.3 5.3 %gate_up_stage.2.refs_7_ = f32[2,2,256,1024]{3,2,1,0:T(8,128)S(1)} custom-call(s32[8]{0:T(128)S(1)} %stack.47.meta_ref, bf16[128,4096]{1,0:T(8,128)(2,1)S(1)} %own_slots.1.own_ref, bf16[3,128,512]{2,1,0:T(8,128)(2,1)S(1)} %pad_maximum_fusion.refs_0_, bf16[3,128,512]{2,1,0:T(8,128)(2,1)S(1)} %collective-permute-done.5.refs_1_, bf16[2,2,4096,1024]{3,2,1,0:T(8,128)(2,1)} %refs_6_.1), custom_call_target="tpu_custom_call" | custom-call | flops 2147483648 | bytes 8388608 | tf_op jit(solution)/shard_map/gate_up_stage/pallas_call | solution.py:310
  33.7 3.4 %fetch_down.3.refs_5_ = bf16[1024,4096]{1,0:T(8,128)(2,1)S(1)} custom-call(bf16[2,1024,4096]{2,1,0:T(8,128)(2,1)} %down_ref.1), custom_call_target="tpu_custom_call" | custom-call | flops 1 | bytes 1 | tf_op jit(solution)/shard_map/fetch_down/pallas_call | solution.py:343
  37.7 2.7 %adam_moments.3 = (f32[8,256,1024]{2,1,0:T(8,128)}, f32[8,256,1024]{2,1,0:T(8,128)}) custom-call(f32[8,256,1024]{2,1,0:T(8,128)} %first_ref.4, f32[8,256,1024]{2,1,0:T(8,128)} %second_ref.4, bf16[8,256,1024]{2,1,0:T(8,128)(2,1)} %grad_ref.4), custom_call_target="tpu_custom_call" | custom-call | flops 1 | bytes 1 | tf_op jit(solution)/shard_map/adam_moments/pallas_call | solution.py:227
  41.9 1.6 %collective-permute-done.12.refs_5_ = bf16[3,128,512]{2,1,0:T(8,128)(2,1)S(1)} collective-permute-done((bf16[3,128,512]{2,1,0:T(8,128)(2,1)S(1)}, bf16[3,128,512]{2,1,0:T(8,128)(2,1)S(1)}, u32[]{:S(2)}, u32[]{:S(2)}) %collective-permute-start.12) | collective-permute-done | bytes 393248 | tf_op jit(solution)/shard_map/ppermute | solution.py:434
  43.5 11.2 %gate_up_stage.3.hidden_ref = bf16[2,256,1024]{2,1,0:T(8,128)(2,1)S(1)} custom-call(s32[8]{0:T(128)S(1)} %stack.47.meta_ref, bf16[128,4096]{1,0:T(8,128)(2,1)S(1)} %own_slots.1.own_ref, bf16[3,128,512]{2,1,0:T(8,128)(2,1)S(1)} %collective-permute-done.8.refs_0_, bf16[3,128,512]{2,1,0:T(8,128)(2,1)S(1)} %collective-permute-done.10.refs_1_, ...), custom_call_target="tpu_custom_call" | custom-call | flops 6442450944 | bytes 25165824 | tf_op jit(solution)/shard_map/gate_up_stage/pallas_call | solution.py:310
  54.8 1.8 %down_mixed.4 = (bf16[512,512]{1,0:T(8,128)(2,1)S(1)}, bf16[256,512]{1,0:T(8,128)(2,1)S(1)}, bf16[256,512]{1,0:T(8,128)(2,1)S(1)}) custom-call(s32[8]{0:T(128)S(1)} %stack.47.meta_ref, bf16[2,256,1024]{2,1,0:T(8,128)(2,1)S(1)} %gate_up_stage.3.hidden_ref, bf16[1024,4096]{1,0:T(8,128)(2,1)S(1)} %get-tuple-element.132.refs_0_, ...), custom_call_target="tpu_custom_call" | custom-call | flops 1073741824 | bytes 4194304 | tf_op jit(solution)/shard_map/down_mixed/pallas_call | solution.py:413
  58.8 1.6 %collective-permute-start.17 = (bf16[256,512]{1,0:T(8,128)(2,1)S(1)}, bf16[256,512]{1,0:T(8,128)(2,1)S(1)}, u32[]{:S(2)}, u32[]{:S(2)}) collective-permute-start(bf16[256,512]{1,0:T(8,128)(2,1)S(1)} %get-tuple-element.149), channel_id=1, source_target_pairs={{0,8},{8,0},{16,24},{24,16},{1,9},{9,1},{17,25},{25,17},{2,10},{10... | collective-permute-start | bytes 786440 | tf_op jit(solution)/shard_map/ppermute | solution.py:434
  60.3 1.5 %collective-permute-start.18 = (bf16[256,512]{1,0:T(8,128)(2,1)S(1)}, bf16[256,512]{1,0:T(8,128)(2,1)S(1)}, u32[]{:S(2)}, u32[]{:S(2)}) collective-permute-start(bf16[256,512]{1,0:T(8,128)(2,1)S(1)} %get-tuple-element.150), channel_id=1, source_target_pairs={{0,16},{8,24},{16,0},{24,8},{1,17},{9,25},{17,1},{25,9},{2,18},{10... | collective-permute-start | bytes 786440 | tf_op jit(solution)/shard_map/ppermute | solution.py:434
  61.8 1.8 %down_mixed.7 = (bf16[512,512]{1,0:T(8,128)(2,1)S(1)}, bf16[256,512]{1,0:T(8,128)(2,1)S(1)}, bf16[256,512]{1,0:T(8,128)(2,1)S(1)}) custom-call(s32[8]{0:T(128)S(1)} %stack.47.meta_ref, bf16[2,256,1024]{2,1,0:T(8,128)(2,1)S(1)} %gate_up_stage.3.hidden_ref, bf16[1024,4096]{1,0:T(8,128)(2,1)S(1)} %get-tuple-element.132.refs_0_, ...), custom_call_target="tpu_custom_call" | custom-call | flops 1073741824 | bytes 4194304 | tf_op jit(solution)/shard_map/down_mixed/pallas_call | solution.py:413
  64.2 1.8 %down_mixed.6 = (bf16[512,512]{1,0:T(8,128)(2,1)S(1)}, bf16[256,512]{1,0:T(8,128)(2,1)S(1)}, bf16[256,512]{1,0:T(8,128)(2,1)S(1)}) custom-call(s32[8]{0:T(128)S(1)} %stack.47.meta_ref, bf16[2,256,1024]{2,1,0:T(8,128)(2,1)S(1)} %gate_up_stage.3.hidden_ref, bf16[1024,4096]{1,0:T(8,128)(2,1)S(1)} %get-tuple-element.132.refs_0_, ...), custom_call_target="tpu_custom_call" | custom-call | flops 1073741824 | bytes 4194304 | tf_op jit(solution)/shard_map/down_mixed/pallas_call | solution.py:413
  68.9 1.7 %collective-permute-start.24 = (bf16[512,512]{1,0:T(8,128)(2,1)S(1)}, bf16[512,512]{1,0:T(8,128)(2,1)S(1)}, u32[]{:S(2)}, u32[]{:S(2)}) collective-permute-start(bf16[512,512]{1,0:T(8,128)(2,1)S(1)} %add_convert_fusion.1), channel_id=1, source_target_pairs={{0,16},{8,24},{16,0},{24,8},{1,17},{9,25},{17,1},{25,9},{2,18},{10... | collective-permute-start | bytes 1572872 | tf_op jit(solution)/shard_map/ppermute | solution.py:434
  70.7 1.5 %collective-permute-start.23 = (bf16[512,512]{1,0:T(8,128)(2,1)S(1)}, bf16[512,512]{1,0:T(8,128)(2,1)S(1)}, u32[]{:S(2)}, u32[]{:S(2)}) collective-permute-start(bf16[512,512]{1,0:T(8,128)(2,1)S(1)} %add_convert_fusion.2), channel_id=1, source_target_pairs={{0,8},{8,0},{16,24},{24,16},{1,9},{9,1},{17,25},{25,17},{2,10},{10... | collective-permute-start | bytes 1572872 | tf_op jit(solution)/shard_map/ppermute | solution.py:434
  72.2 1.8 %down_mixed.5 = (bf16[512,512]{1,0:T(8,128)(2,1)S(1)}, bf16[256,512]{1,0:T(8,128)(2,1)S(1)}, bf16[256,512]{1,0:T(8,128)(2,1)S(1)}) custom-call(s32[8]{0:T(128)S(1)} %stack.47.meta_ref, bf16[2,256,1024]{2,1,0:T(8,128)(2,1)S(1)} %gate_up_stage.3.hidden_ref, bf16[1024,4096]{1,0:T(8,128)(2,1)S(1)} %get-tuple-element.132.refs_0_, ...), custom_call_target="tpu_custom_call" | custom-call | flops 1073741824 | bytes 4194304 | tf_op jit(solution)/shard_map/down_mixed/pallas_call | solution.py:413
  74.6 9.3 %adam_moments.4 = (f32[8,256,1024]{2,1,0:T(8,128)}, f32[8,256,1024]{2,1,0:T(8,128)}) custom-call(f32[8,256,1024]{2,1,0:T(8,128)} %first_ref.4, f32[8,256,1024]{2,1,0:T(8,128)} %second_ref.4, bf16[8,256,1024]{2,1,0:T(8,128)(2,1)} %grad_ref.4, f32[8,256,1024]{2,1,0:T(8,128)} %get-tuple-element.142.refs_0_, ...), custom_call_target="tpu_custom_call", output_to_operand_aliasing={{0}: (3, {}), {1}: (4, {})} | custom-call | flops 8388608 | bytes 18874368 | tf_op jit(solution)/shard_map/adam_moments/pallas_call | solution.py:227
  87.4 2.3 %collective-permute-start.25 = (bf16[128,512]{1,0:T(8,128)(2,1)S(1)}, bf16[128,512]{1,0:T(8,128)(2,1)S(1)}, u32[]{:S(2)}, u32[]{:S(2)}) collective-permute-start(bf16[128,512]{1,0:T(8,128)(2,1)S(1)} %get-tuple-element.175), channel_id=1, source_target_pairs={{0,6},{2,0},{4,2},{6,4},{1,7},{3,1},{5,3},{7,5},{8,14},{10,8},{12,... | collective-permute-start | bytes 393224 | tf_op jit(solution)/shard_map/ppermute | solution.py:439
  89.7 7.1 %adam_moments.5 = (f32[8,256,1024]{2,1,0:T(8,128)}, f32[8,256,1024]{2,1,0:T(8,128)}) custom-call(f32[8,256,1024]{2,1,0:T(8,128)} %first_ref.4, f32[8,256,1024]{2,1,0:T(8,128)} %second_ref.4, bf16[8,256,1024]{2,1,0:T(8,128)(2,1)} %grad_ref.4, f32[8,256,1024]{2,1,0:T(8,128)} %get-tuple-element.169.refs_0_, ...), custom_call_target="tpu_custom_call", output_to_operand_aliasing={{0}: (3, {}), {1}: (4, {})} | custom-call | flops 6291456 | bytes 14155776 | tf_op jit(solution)/shard_map/adam_moments/pallas_call | solution.py:227
  (65 shorter events, 20.4 us)
Async XLA Ops:
  3.6 16.1 %collective-permute-start = (bf16[128,512]{1,0:T(8,128)(2,1)S(1)}, bf16[128,512]{1,0:T(8,128)(2,1)S(1)}, u32[]{:S(2)}, u32[]{:S(2)}) collective-permute-start(bf16[128,512]{1,0:T(8,128)(2,1)S(1)} %get-tuple-element.94), channel_id=1, source_target_pairs={{0,2},{2,4},{4,6},{6,0},{1,3},{3,5},{5,7},{7,1},{8,10},{10,12},{12... | collective-permute-start | bytes 393224 | tf_op jit(solution)/shard_map/ppermute | solution.py:439
  6.7 13.1 %collective-permute-start.1 = (bf16[128,512]{1,0:T(8,128)(2,1)S(1)}, bf16[128,512]{1,0:T(8,128)(2,1)S(1)}, u32[]{:S(2)}, u32[]{:S(2)}) collective-permute-start(bf16[128,512]{1,0:T(8,128)(2,1)S(1)} %get-tuple-element.95), channel_id=1, source_target_pairs={{0,4},{2,6},{4,0},{6,2},{1,5},{3,7},{5,1},{7,3},{8,12},{10,14},{12... | collective-permute-start | bytes 393224 | tf_op jit(solution)/shard_map/ppermute | solution.py:439
  9.3 10.5 %collective-permute-start.2 = (bf16[128,512]{1,0:T(8,128)(2,1)S(1)}, bf16[128,512]{1,0:T(8,128)(2,1)S(1)}, u32[]{:S(2)}, u32[]{:S(2)}) collective-permute-start(bf16[128,512]{1,0:T(8,128)(2,1)S(1)} %get-tuple-element.96), channel_id=1, source_target_pairs={{0,6},{2,0},{4,2},{6,4},{1,7},{3,1},{5,3},{7,5},{8,14},{10,8},{12,... | collective-permute-start | bytes 393224 | tf_op jit(solution)/shard_map/ppermute | solution.py:439
  19.8 5.0 %collective-permute-start.5 = (bf16[3,128,512]{2,1,0:T(8,128)(2,1)S(1)}, bf16[3,128,512]{2,1,0:T(8,128)(2,1)S(1)}, u32[]{:S(2)}, u32[]{:S(2)}) collective-permute-start(bf16[3,128,512]{2,1,0:T(8,128)(2,1)S(1)} %pad_maximum_fusion.refs_0_), channel_id=1, source_target_pairs={{0,1},{1,0},{2,3},{3,2},{4,5},{5,4},{6,7},{7,6},{8,9},{9,8},{10,11... | collective-permute-start | bytes 1179656 | tf_op jit(solution)/shard_map/ppermute | solution.py:434
  19.9 17.2 %collective-permute-start.9 = (bf16[3,128,512]{2,1,0:T(8,128)(2,1)S(1)}, bf16[3,128,512]{2,1,0:T(8,128)(2,1)S(1)}, u32[]{:S(2)}, u32[]{:S(2)}) collective-permute-start(bf16[3,128,512]{2,1,0:T(8,128)(2,1)S(1)} %pad_maximum_fusion.refs_0_), channel_id=1, source_target_pairs={{0,16},{8,24},{16,0},{24,8},{1,17},{9,25},{17,1},{25,9},{2,18},{10... | collective-permute-start | bytes 1179656 | tf_op jit(solution)/shard_map/ppermute | solution.py:434
  21.6 15.5 %collective-permute-start.8 = (bf16[3,128,512]{2,1,0:T(8,128)(2,1)S(1)}, bf16[3,128,512]{2,1,0:T(8,128)(2,1)S(1)}, u32[]{:S(2)}, u32[]{:S(2)}) collective-permute-start(bf16[3,128,512]{2,1,0:T(8,128)(2,1)S(1)} %pad_maximum_fusion.refs_0_), channel_id=1, source_target_pairs={{0,8},{8,0},{16,24},{24,16},{1,9},{9,1},{17,25},{25,17},{2,10},{10... | collective-permute-start | bytes 1179656 | tf_op jit(solution)/shard_map/ppermute | solution.py:434
  23.0 18.8 %collective-permute-start.6 = (bf16[3,128,512]{2,1,0:T(8,128)(2,1)S(1)}, bf16[3,128,512]{2,1,0:T(8,128)(2,1)S(1)}, u32[]{:S(2)}, u32[]{:S(2)}) collective-permute-start(bf16[3,128,512]{2,1,0:T(8,128)(2,1)S(1)} %pad_maximum_fusion.refs_0_), channel_id=1, source_target_pairs={{0,24},{8,16},{16,8},{24,0},{1,25},{9,17},{17,9},{25,1},{2,26},{10... | collective-permute-start | bytes 1179656 | tf_op jit(solution)/shard_map/ppermute | solution.py:434
  23.5 9.2 %collective-permute-start.3 = (bf16[2,32,1024]{2,1,0:T(8,128)(2,1)S(1)}, bf16[2,32,1024]{2,1,0:T(8,128)(2,1)S(1)}, u32[]{:S(2)}, u32[]{:S(2)}) collective-permute-start(bf16[2,32,1024]{2,1,0:T(8,128)(2,1)S(1)} %get-tuple-element.103), channel_id=1, source_target_pairs={{0,2},{2,4},{4,6},{6,0},{1,3},{3,5},{5,7},{7,1},{8,10},{10,12},{12... | collective-permute-start | bytes 393224 | tf_op jit(solution)/shard_map/ppermute | solution.py:439
  24.9 7.8 %collective-permute-start.4 = (bf16[2,32,1024]{2,1,0:T(8,128)(2,1)S(1)}, bf16[2,32,1024]{2,1,0:T(8,128)(2,1)S(1)}, u32[]{:S(2)}, u32[]{:S(2)}) collective-permute-start(bf16[2,32,1024]{2,1,0:T(8,128)(2,1)S(1)} %get-tuple-element.105), channel_id=1, source_target_pairs={{0,6},{2,0},{4,2},{6,4},{1,7},{3,1},{5,3},{7,5},{8,14},{10,8},{12,... | collective-permute-start | bytes 393224 | tf_op jit(solution)/shard_map/ppermute | solution.py:439
  32.7 7.8 %collective-permute-start.7 = (bf16[2,32,1024]{2,1,0:T(8,128)(2,1)S(1)}, bf16[2,32,1024]{2,1,0:T(8,128)(2,1)S(1)}, u32[]{:S(2)}, u32[]{:S(2)}) collective-permute-start(bf16[2,32,1024]{2,1,0:T(8,128)(2,1)S(1)} %get-tuple-element.115), channel_id=1, source_target_pairs={{0,4},{2,6},{4,0},{6,2},{1,5},{3,7},{5,1},{7,3},{8,12},{10,14},{12... | collective-permute-start | bytes 393224 | tf_op jit(solution)/shard_map/ppermute | solution.py:439
  37.1 4.8 %collective-permute-start.10 = (bf16[3,128,512]{2,1,0:T(8,128)(2,1)S(1)}, bf16[3,128,512]{2,1,0:T(8,128)(2,1)S(1)}, u32[]{:S(2)}, u32[]{:S(2)}) collective-permute-start(bf16[3,128,512]{2,1,0:T(8,128)(2,1)S(1)} %collective-permute-done.8.refs_0_), channel_id=1, source_target_pairs={{0,1},{1,0},{2,3},{3,2},{4,5},{5,4},{6,7},{7,6},{8,9},{9,8},{10,11... | collective-permute-start | bytes 1179656 | tf_op jit(solution)/shard_map/ppermute | solution.py:434
  37.2 4.7 %collective-permute-start.11 = (bf16[3,128,512]{2,1,0:T(8,128)(2,1)S(1)}, bf16[3,128,512]{2,1,0:T(8,128)(2,1)S(1)}, u32[]{:S(2)}, u32[]{:S(2)}) collective-permute-start(bf16[3,128,512]{2,1,0:T(8,128)(2,1)S(1)} %collective-permute-done.9.refs_2_), channel_id=1, source_target_pairs={{0,1},{1,0},{2,3},{3,2},{4,5},{5,4},{6,7},{7,6},{8,9},{9,8},{10,11... | collective-permute-start | bytes 1179656 | tf_op jit(solution)/shard_map/ppermute | solution.py:434
  58.8 8.4 %collective-permute-start.17 = (bf16[256,512]{1,0:T(8,128)(2,1)S(1)}, bf16[256,512]{1,0:T(8,128)(2,1)S(1)}, u32[]{:S(2)}, u32[]{:S(2)}) collective-permute-start(bf16[256,512]{1,0:T(8,128)(2,1)S(1)} %get-tuple-element.149), channel_id=1, source_target_pairs={{0,8},{8,0},{16,24},{24,16},{1,9},{9,1},{17,25},{25,17},{2,10},{10... | collective-permute-start | bytes 786440 | tf_op jit(solution)/shard_map/ppermute | solution.py:434
  60.3 8.1 %collective-permute-start.18 = (bf16[256,512]{1,0:T(8,128)(2,1)S(1)}, bf16[256,512]{1,0:T(8,128)(2,1)S(1)}, u32[]{:S(2)}, u32[]{:S(2)}) collective-permute-start(bf16[256,512]{1,0:T(8,128)(2,1)S(1)} %get-tuple-element.150), channel_id=1, source_target_pairs={{0,16},{8,24},{16,0},{24,8},{1,17},{9,25},{17,1},{25,9},{2,18},{10... | collective-permute-start | bytes 786440 | tf_op jit(solution)/shard_map/ppermute | solution.py:434
  63.6 4.7 %collective-permute-start.21 = (bf16[256,512]{1,0:T(8,128)(2,1)S(1)}, bf16[256,512]{1,0:T(8,128)(2,1)S(1)}, u32[]{:S(2)}, u32[]{:S(2)}) collective-permute-start(bf16[256,512]{1,0:T(8,128)(2,1)S(1)} %get-tuple-element.155), channel_id=1, source_target_pairs={{0,1},{1,0},{2,3},{3,2},{4,5},{5,4},{6,7},{7,6},{8,9},{9,8},{10,11... | collective-permute-start | bytes 786440 | tf_op jit(solution)/shard_map/ppermute | solution.py:434
  63.7 4.7 %collective-permute-start.22 = (bf16[256,512]{1,0:T(8,128)(2,1)S(1)}, bf16[256,512]{1,0:T(8,128)(2,1)S(1)}, u32[]{:S(2)}, u32[]{:S(2)}) collective-permute-start(bf16[256,512]{1,0:T(8,128)(2,1)S(1)} %get-tuple-element.156), channel_id=1, source_target_pairs={{0,1},{1,0},{2,3},{3,2},{4,5},{5,4},{6,7},{7,6},{8,9},{9,8},{10,11... | collective-permute-start | bytes 786440 | tf_op jit(solution)/shard_map/ppermute | solution.py:434
  66.0 2.4 %collective-permute-start.19 = (bf16[256,512]{1,0:T(8,128)(2,1)S(1)}, bf16[256,512]{1,0:T(8,128)(2,1)S(1)}, u32[]{:S(2)}, u32[]{:S(2)}) collective-permute-start(bf16[256,512]{1,0:T(8,128)(2,1)S(1)} %get-tuple-element.152), channel_id=1, source_target_pairs={{0,1},{1,0},{2,3},{3,2},{4,5},{5,4},{6,7},{7,6},{8,9},{9,8},{10,11... | collective-permute-start | bytes 786440 | tf_op jit(solution)/shard_map/ppermute | solution.py:434
  68.9 15.0 %collective-permute-start.24 = (bf16[512,512]{1,0:T(8,128)(2,1)S(1)}, bf16[512,512]{1,0:T(8,128)(2,1)S(1)}, u32[]{:S(2)}, u32[]{:S(2)}) collective-permute-start(bf16[512,512]{1,0:T(8,128)(2,1)S(1)} %add_convert_fusion.1), channel_id=1, source_target_pairs={{0,16},{8,24},{16,0},{24,8},{1,17},{9,25},{17,1},{25,9},{2,18},{10... | collective-permute-start | bytes 1572872 | tf_op jit(solution)/shard_map/ppermute | solution.py:434
  70.7 13.8 %collective-permute-start.23 = (bf16[512,512]{1,0:T(8,128)(2,1)S(1)}, bf16[512,512]{1,0:T(8,128)(2,1)S(1)}, u32[]{:S(2)}, u32[]{:S(2)}) collective-permute-start(bf16[512,512]{1,0:T(8,128)(2,1)S(1)} %add_convert_fusion.2), channel_id=1, source_target_pairs={{0,8},{8,0},{16,24},{24,16},{1,9},{9,1},{17,25},{25,17},{2,10},{10... | collective-permute-start | bytes 1572872 | tf_op jit(solution)/shard_map/ppermute | solution.py:434
  74.0 9.9 %collective-permute-start.15 = (bf16[256,512]{1,0:T(8,128)(2,1)S(1)}, bf16[256,512]{1,0:T(8,128)(2,1)S(1)}, u32[]{:S(2)}, u32[]{:S(2)}) collective-permute-start(bf16[256,512]{1,0:T(8,128)(2,1)S(1)} %get-tuple-element.147), channel_id=1, source_target_pairs={{0,1},{1,0},{2,3},{3,2},{4,5},{5,4},{6,7},{7,6},{8,9},{9,8},{10,11... | collective-permute-start | bytes 786440 | tf_op jit(solution)/shard_map/ppermute | solution.py:434
  74.1 9.8 %collective-permute-start.16 = (bf16[256,512]{1,0:T(8,128)(2,1)S(1)}, bf16[256,512]{1,0:T(8,128)(2,1)S(1)}, u32[]{:S(2)}, u32[]{:S(2)}) collective-permute-start(bf16[256,512]{1,0:T(8,128)(2,1)S(1)} %get-tuple-element.148), channel_id=1, source_target_pairs={{0,1},{1,0},{2,3},{3,2},{4,5},{5,4},{6,7},{7,6},{8,9},{9,8},{10,11... | collective-permute-start | bytes 786440 | tf_op jit(solution)/shard_map/ppermute | solution.py:434
  84.8 12.1 %collective-permute-start.27 = (bf16[128,512]{1,0:T(8,128)(2,1)S(1)}, bf16[128,512]{1,0:T(8,128)(2,1)S(1)}, u32[]{:S(2)}, u32[]{:S(2)}) collective-permute-start(bf16[128,512]{1,0:T(8,128)(2,1)S(1)} %get-tuple-element.173), channel_id=1, source_target_pairs={{0,2},{2,4},{4,6},{6,0},{1,3},{3,5},{5,7},{7,1},{8,10},{10,12},{12... | collective-permute-start | bytes 393224 | tf_op jit(solution)/shard_map/ppermute | solution.py:439
  86.1 11.1 %collective-permute-start.26 = (bf16[128,512]{1,0:T(8,128)(2,1)S(1)}, bf16[128,512]{1,0:T(8,128)(2,1)S(1)}, u32[]{:S(2)}, u32[]{:S(2)}) collective-permute-start(bf16[128,512]{1,0:T(8,128)(2,1)S(1)} %get-tuple-element.174), channel_id=1, source_target_pairs={{0,4},{2,6},{4,0},{6,2},{1,5},{3,7},{5,1},{7,3},{8,12},{10,14},{12... | collective-permute-start | bytes 393224 | tf_op jit(solution)/shard_map/ppermute | solution.py:439
  87.4 9.9 %collective-permute-start.25 = (bf16[128,512]{1,0:T(8,128)(2,1)S(1)}, bf16[128,512]{1,0:T(8,128)(2,1)S(1)}, u32[]{:S(2)}, u32[]{:S(2)}) collective-permute-start(bf16[128,512]{1,0:T(8,128)(2,1)S(1)} %get-tuple-element.175), channel_id=1, source_target_pairs={{0,6},{2,0},{4,2},{6,4},{1,7},{3,1},{5,3},{7,5},{8,14},{10,8},{12,... | collective-permute-start | bytes 393224 | tf_op jit(solution)/shard_map/ppermute | solution.py:439
  (8 other events, 21.5 us)

commit v6 on v5

--- a/solution.py
+++ b/solution.py
@@ -12,7 +12,7 @@
 MAXCH = 4
 CAP = 32
 PIECES = 2
-ADAM_ROWS = 128
+ADAM_ROWS = 256
 RING = 12
 UNIT_TILE = 512
 

time: 99.4 us -> 99.2 us (level)
  waiting for transfers between devices: 6.61 us -> 7.81 us
  Pallas kernels: 58.3 us -> 57.2 us
    pallas_call x3, Pallas kernels: 19.1 us -> 17.6 us  [adam_part(): pl.pallas_call(adam_kernel, grid=(end - begin, rows // lines), in_specs=[...]
    ppermute x19, waiting for transfers between devices: 6.15 us -> 7.55 us  [swap(): lax.ppermute(value, axis, [(i, i ^ distance) for i in range(lax.axis_size...]
  transfers between devices with their start and end apart: 28 -> 28, of which waited for: 8 -> 9; matrix products, arithmetic and copies ran while one was open for 1% -> 1% of each run, Pallas kernels for 43% -> 42%
where the time goes in v6:
time: 99.2 us; the launch traced here: 98.3 us
  Pallas kernels  57.2 us (58%)
  starting transfers between devices  29.2 us (29%)
  waiting for transfers between devices  7.81 us (8%)
  local copies, waits for them, and re-layouts  2.38 us (2%)
    pallas_call x3, Pallas kernels, adam_part(): pl.pallas_call(adam_kernel, grid=(end - begin, rows // lines), in_specs=[...  17.6 us
    ppermute x9, starting transfers between devices, shift(): lax.ppermute(value, axis, [(i, (i + distance) % size) for i in range(size)])  16.8 us
    pallas_call x2, Pallas kernels, gate_up_stage(): pl.pallas_call(functools.partial(gate_up_kernel, begin, shares, across, w...  16.6 us
    ppermute x19, starting transfers between devices, swap(): lax.ppermute(value, axis, [(i, i ^ distance) for i in range(lax.axis_size...  12.4 us
    ppermute x19, waiting for transfers between devices, swap(): lax.ppermute(value, axis, [(i, i ^ distance) for i in range(lax.axis_size...  7.55 us
    pallas_call x4, Pallas kernels, down_pieces(): pl.pallas_call(functools.partial(down_kernel, share, across, within, per_...  7.46 us
    pallas_call x2, Pallas kernels, fetch_down(): pl.pallas_call(functools.partial(fetch_kernel, expert), in_specs=[pl.Bloc...  6.87 us
    pallas_call x1, Pallas kernels, listed_deltas(): pl.pallas_call(functools.partial(delta_kernel, groups), grid_spec=pltpu.P...  3.78 us
  transfers between devices with their start and end apart: 28, of which 9 were waited for; matrix products, arithmetic and copies ran while one was open for 1% of the time, Pallas kernels for 42%

profile of v6, /device:TPU:0, one launch (start us, length us, event | category | flops | bytes accessed | tf_op | source)
XLA Modules:
  0.0 98.3 jit_solution(15403564946841804784)
XLA Ops:
  1.4 2.2 %pack_slots.1 = (bf16[128,512]{1,0:T(8,128)(2,1)S(1)}, bf16[128,512]{1,0:T(8,128)(2,1)S(1)}, bf16[128,512]{1,0:T(8,128)(2,1)S(1)}, bf16[128,128]{1,0:T(8,128)(2,1)S(1)}, bf16[2,128,512]{2,1,0:T(8,128)(2,1)S(1)}) custom-call(s32[8]{0:T(128)S(1)} %stack.47.meta_ref, bf16[2,64,4096]{2,1,0:T(8,128)(2,1)} %tokens_ref.3, s32[2,2,64]{2,1,0:T(2,128)S(1)} %bitcast.24), custom_call_target="tpu_custom_call" | custom-call | flops 10000000 | bytes 262144 | tf_op jit(solution)/shard_map/pack_slots/pallas_call | solution.py:91
  3.6 3.1 %collective-permute-start = (bf16[128,512]{1,0:T(8,128)(2,1)S(1)}, bf16[128,512]{1,0:T(8,128)(2,1)S(1)}, u32[]{:S(2)}, u32[]{:S(2)}) collective-permute-start(bf16[128,512]{1,0:T(8,128)(2,1)S(1)} %get-tuple-element.94), channel_id=1, source_target_pairs={{0,2},{2,4},{4,6},{6,0},{1,3},{3,5},{5,7},{7,1},{8,10},{10,12},{12... | collective-permute-start | bytes 393224 | tf_op jit(solution)/shard_map/ppermute | solution.py:439
  6.7 2.6 %collective-permute-start.1 = (bf16[128,512]{1,0:T(8,128)(2,1)S(1)}, bf16[128,512]{1,0:T(8,128)(2,1)S(1)}, u32[]{:S(2)}, u32[]{:S(2)}) collective-permute-start(bf16[128,512]{1,0:T(8,128)(2,1)S(1)} %get-tuple-element.95), channel_id=1, source_target_pairs={{0,4},{2,6},{4,0},{6,2},{1,5},{3,7},{5,1},{7,3},{8,12},{10,14},{12... | collective-permute-start | bytes 393224 | tf_op jit(solution)/shard_map/ppermute | solution.py:439
  12.0 3.8 %listed_deltas.1 = (bf16[2,32,1024]{2,1,0:T(8,128)(2,1)S(1)}, bf16[2,32,1024]{2,1,0:T(8,128)(2,1)S(1)}, bf16[2,32,1024]{2,1,0:T(8,128)(2,1)S(1)}, bf16[2,32,1024]{2,1,0:T(8,128)(2,1)S(1)}) custom-call(s32[8]{0:T(128)S(1)} %stack.47.meta_ref, s32[8,4]{1,0:T(8,128)S(1)} %copy.19.list_ref, s32[8]{0:T(128)S(1)} %bitcast.26, f32[8,256,1024]{2,1,0:T(8,128)} %first_ref.4, ...), custom_call_target="tpu_custom_call" | custom-call | flops 1000000 | bytes 3145728 | tf_op jit(solution)/shard_map/listed_deltas/pallas_call | solution.py:194
  15.8 3.5 %fetch_down.2.refs_4_ = bf16[1024,4096]{1,0:T(8,128)(2,1)S(1)} custom-call(bf16[2,1024,4096]{2,1,0:T(8,128)(2,1)} %down_ref.1), custom_call_target="tpu_custom_call" | custom-call | flops 1 | bytes 1 | tf_op jit(solution)/shard_map/fetch_down/pallas_call | solution.py:343
  20.0 1.6 %collective-permute-start.9 = (bf16[3,128,512]{2,1,0:T(8,128)(2,1)S(1)}, bf16[3,128,512]{2,1,0:T(8,128)(2,1)S(1)}, u32[]{:S(2)}, u32[]{:S(2)}) collective-permute-start(bf16[3,128,512]{2,1,0:T(8,128)(2,1)S(1)} %pad_maximum_fusion.refs_0_), channel_id=1, source_target_pairs={{0,16},{8,24},{16,0},{24,8},{1,17},{9,25},{17,1},{25,9},{2,18},{10... | collective-permute-start | bytes 1179656 | tf_op jit(solution)/shard_map/ppermute | solution.py:434
  21.6 1.5 %collective-permute-start.8 = (bf16[3,128,512]{2,1,0:T(8,128)(2,1)S(1)}, bf16[3,128,512]{2,1,0:T(8,128)(2,1)S(1)}, u32[]{:S(2)}, u32[]{:S(2)}) collective-permute-start(bf16[3,128,512]{2,1,0:T(8,128)(2,1)S(1)} %pad_maximum_fusion.refs_0_), channel_id=1, source_target_pairs={{0,8},{8,0},{16,24},{24,16},{1,9},{9,1},{17,25},{25,17},{2,10},{10... | collective-permute-start | bytes 1179656 | tf_op jit(solution)/shard_map/ppermute | solution.py:434
  24.9 2.5 %collective-permute-start.4 = (bf16[2,32,1024]{2,1,0:T(8,128)(2,1)S(1)}, bf16[2,32,1024]{2,1,0:T(8,128)(2,1)S(1)}, u32[]{:S(2)}, u32[]{:S(2)}) collective-permute-start(bf16[2,32,1024]{2,1,0:T(8,128)(2,1)S(1)} %get-tuple-element.105), channel_id=1, source_target_pairs={{0,6},{2,0},{4,2},{6,4},{1,7},{3,1},{5,3},{7,5},{8,14},{10,8},{12,... | collective-permute-start | bytes 393224 | tf_op jit(solution)/shard_map/ppermute | solution.py:439
  27.4 5.3 %gate_up_stage.2.refs_7_ = f32[2,2,256,1024]{3,2,1,0:T(8,128)S(1)} custom-call(s32[8]{0:T(128)S(1)} %stack.47.meta_ref, bf16[128,4096]{1,0:T(8,128)(2,1)S(1)} %own_slots.1.own_ref, bf16[3,128,512]{2,1,0:T(8,128)(2,1)S(1)} %pad_maximum_fusion.refs_0_, bf16[3,128,512]{2,1,0:T(8,128)(2,1)S(1)} %collective-permute-done.5.refs_1_, bf16[2,2,4096,1024]{3,2,1,0:T(8,128)(2,1)} %refs_6_.1), custom_call_target="tpu_custom_call" | custom-call | flops 2147483648 | bytes 8388608 | tf_op jit(solution)/shard_map/gate_up_stage/pallas_call | solution.py:310
  33.8 3.4 %fetch_down.3.refs_5_ = bf16[1024,4096]{1,0:T(8,128)(2,1)S(1)} custom-call(bf16[2,1024,4096]{2,1,0:T(8,128)(2,1)} %down_ref.1), custom_call_target="tpu_custom_call" | custom-call | flops 1 | bytes 1 | tf_op jit(solution)/shard_map/fetch_down/pallas_call | solution.py:343
  37.8 3.2 %adam_moments.3 = (f32[8,256,1024]{2,1,0:T(8,128)}, f32[8,256,1024]{2,1,0:T(8,128)}) custom-call(f32[8,256,1024]{2,1,0:T(8,128)} %first_ref.4, f32[8,256,1024]{2,1,0:T(8,128)} %second_ref.4, bf16[8,256,1024]{2,1,0:T(8,128)(2,1)} %grad_ref.4), custom_call_target="tpu_custom_call" | custom-call | flops 1 | bytes 1 | tf_op jit(solution)/shard_map/adam_moments/pallas_call | solution.py:227
  42.5 1.6 %collective-permute-done.12.refs_5_ = bf16[3,128,512]{2,1,0:T(8,128)(2,1)S(1)} collective-permute-done((bf16[3,128,512]{2,1,0:T(8,128)(2,1)S(1)}, bf16[3,128,512]{2,1,0:T(8,128)(2,1)S(1)}, u32[]{:S(2)}, u32[]{:S(2)}) %collective-permute-start.12) | collective-permute-done | bytes 393248 | tf_op jit(solution)/shard_map/ppermute | solution.py:434
  44.2 11.2 %gate_up_stage.3.hidden_ref = bf16[2,256,1024]{2,1,0:T(8,128)(2,1)S(1)} custom-call(s32[8]{0:T(128)S(1)} %stack.47.meta_ref, bf16[128,4096]{1,0:T(8,128)(2,1)S(1)} %own_slots.1.own_ref, bf16[3,128,512]{2,1,0:T(8,128)(2,1)S(1)} %collective-permute-done.8.refs_0_, bf16[3,128,512]{2,1,0:T(8,128)(2,1)S(1)} %collective-permute-done.10.refs_1_, ...), custom_call_target="tpu_custom_call" | custom-call | flops 6442450944 | bytes 25165824 | tf_op jit(solution)/shard_map/gate_up_stage/pallas_call | solution.py:310
  55.4 1.8 %down_mixed.4 = (bf16[512,512]{1,0:T(8,128)(2,1)S(1)}, bf16[256,512]{1,0:T(8,128)(2,1)S(1)}, bf16[256,512]{1,0:T(8,128)(2,1)S(1)}) custom-call(s32[8]{0:T(128)S(1)} %stack.47.meta_ref, bf16[2,256,1024]{2,1,0:T(8,128)(2,1)S(1)} %gate_up_stage.3.hidden_ref, bf16[1024,4096]{1,0:T(8,128)(2,1)S(1)} %get-tuple-element.132.refs_0_, ...), custom_call_target="tpu_custom_call" | custom-call | flops 1073741824 | bytes 4194304 | tf_op jit(solution)/shard_map/down_mixed/pallas_call | solution.py:413
  60.8 1.6 %collective-permute-start.18 = (bf16[256,512]{1,0:T(8,128)(2,1)S(1)}, bf16[256,512]{1,0:T(8,128)(2,1)S(1)}, u32[]{:S(2)}, u32[]{:S(2)}) collective-permute-start(bf16[256,512]{1,0:T(8,128)(2,1)S(1)} %get-tuple-element.150), channel_id=1, source_target_pairs={{0,16},{8,24},{16,0},{24,8},{1,17},{9,25},{17,1},{25,9},{2,18},{10... | collective-permute-start | bytes 786440 | tf_op jit(solution)/shard_map/ppermute | solution.py:434
  62.4 1.8 %down_mixed.7 = (bf16[512,512]{1,0:T(8,128)(2,1)S(1)}, bf16[256,512]{1,0:T(8,128)(2,1)S(1)}, bf16[256,512]{1,0:T(8,128)(2,1)S(1)}) custom-call(s32[8]{0:T(128)S(1)} %stack.47.meta_ref, bf16[2,256,1024]{2,1,0:T(8,128)(2,1)S(1)} %gate_up_stage.3.hidden_ref, bf16[1024,4096]{1,0:T(8,128)(2,1)S(1)} %get-tuple-element.132.refs_0_, ...), custom_call_target="tpu_custom_call" | custom-call | flops 1073741824 | bytes 4194304 | tf_op jit(solution)/shard_map/down_mixed/pallas_call | solution.py:413
  64.8 2.1 %down_mixed.6 = (bf16[512,512]{1,0:T(8,128)(2,1)S(1)}, bf16[256,512]{1,0:T(8,128)(2,1)S(1)}, bf16[256,512]{1,0:T(8,128)(2,1)S(1)}) custom-call(s32[8]{0:T(128)S(1)} %stack.47.meta_ref, bf16[2,256,1024]{2,1,0:T(8,128)(2,1)S(1)} %gate_up_stage.3.hidden_ref, bf16[1024,4096]{1,0:T(8,128)(2,1)S(1)} %get-tuple-element.132.refs_0_, ...), custom_call_target="tpu_custom_call" | custom-call | flops 1073741824 | bytes 4194304 | tf_op jit(solution)/shard_map/down_mixed/pallas_call | solution.py:413
  69.5 1.5 %collective-permute-start.24 = (bf16[512,512]{1,0:T(8,128)(2,1)S(1)}, bf16[512,512]{1,0:T(8,128)(2,1)S(1)}, u32[]{:S(2)}, u32[]{:S(2)}) collective-permute-start(bf16[512,512]{1,0:T(8,128)(2,1)S(1)} %add_convert_fusion.1), channel_id=1, source_target_pairs={{0,16},{8,24},{16,0},{24,8},{1,17},{9,25},{17,1},{25,9},{2,18},{10... | collective-permute-start | bytes 1572872 | tf_op jit(solution)/shard_map/ppermute | solution.py:434
  71.2 1.6 %collective-permute-start.23 = (bf16[512,512]{1,0:T(8,128)(2,1)S(1)}, bf16[512,512]{1,0:T(8,128)(2,1)S(1)}, u32[]{:S(2)}, u32[]{:S(2)}) collective-permute-start(bf16[512,512]{1,0:T(8,128)(2,1)S(1)} %add_convert_fusion.2), channel_id=1, source_target_pairs={{0,8},{8,0},{16,24},{24,16},{1,9},{9,1},{17,25},{25,17},{2,10},{10... | collective-permute-start | bytes 1572872 | tf_op jit(solution)/shard_map/ppermute | solution.py:434
  72.8 1.8 %down_mixed.5 = (bf16[512,512]{1,0:T(8,128)(2,1)S(1)}, bf16[256,512]{1,0:T(8,128)(2,1)S(1)}, bf16[256,512]{1,0:T(8,128)(2,1)S(1)}) custom-call(s32[8]{0:T(128)S(1)} %stack.47.meta_ref, bf16[2,256,1024]{2,1,0:T(8,128)(2,1)S(1)} %gate_up_stage.3.hidden_ref, bf16[1024,4096]{1,0:T(8,128)(2,1)S(1)} %get-tuple-element.132.refs_0_, ...), custom_call_target="tpu_custom_call" | custom-call | flops 1073741824 | bytes 4194304 | tf_op jit(solution)/shard_map/down_mixed/pallas_call | solution.py:413
  75.2 7.5 %adam_moments.4 = (f32[8,256,1024]{2,1,0:T(8,128)}, f32[8,256,1024]{2,1,0:T(8,128)}) custom-call(f32[8,256,1024]{2,1,0:T(8,128)} %first_ref.4, f32[8,256,1024]{2,1,0:T(8,128)} %second_ref.4, bf16[8,256,1024]{2,1,0:T(8,128)(2,1)} %grad_ref.4, f32[8,256,1024]{2,1,0:T(8,128)} %get-tuple-element.142.refs_0_, ...), custom_call_target="tpu_custom_call", output_to_operand_aliasing={{0}: (3, {}), {1}: (4, {})} | custom-call | flops 8388608 | bytes 18874368 | tf_op jit(solution)/shard_map/adam_moments/pallas_call | solution.py:227
  83.5 1.4 %collective-permute-done.23 = bf16[512,512]{1,0:T(8,128)(2,1)S(1)} collective-permute-done((bf16[512,512]{1,0:T(8,128)(2,1)S(1)}, bf16[512,512]{1,0:T(8,128)(2,1)S(1)}, u32[]{:S(2)}, u32[]{:S(2)}) %collective-permute-start.23) | collective-permute-done | bytes 524320 | tf_op jit(solution)/shard_map/ppermute | solution.py:434
  87.5 2.8 %collective-permute-start.25 = (bf16[128,512]{1,0:T(8,128)(2,1)S(1)}, bf16[128,512]{1,0:T(8,128)(2,1)S(1)}, u32[]{:S(2)}, u32[]{:S(2)}) collective-permute-start(bf16[128,512]{1,0:T(8,128)(2,1)S(1)} %get-tuple-element.175), channel_id=1, source_target_pairs={{0,6},{2,0},{4,2},{6,4},{1,7},{3,1},{5,3},{7,5},{8,14},{10,8},{12,... | collective-permute-start | bytes 393224 | tf_op jit(solution)/shard_map/ppermute | solution.py:439
  90.3 6.8 %adam_moments.5 = (f32[8,256,1024]{2,1,0:T(8,128)}, f32[8,256,1024]{2,1,0:T(8,128)}) custom-call(f32[8,256,1024]{2,1,0:T(8,128)} %first_ref.4, f32[8,256,1024]{2,1,0:T(8,128)} %second_ref.4, bf16[8,256,1024]{2,1,0:T(8,128)(2,1)} %grad_ref.4, f32[8,256,1024]{2,1,0:T(8,128)} %get-tuple-element.169.refs_0_, ...), custom_call_target="tpu_custom_call", output_to_operand_aliasing={{0}: (3, {}), {1}: (4, {})} | custom-call | flops 6291456 | bytes 14155776 | tf_op jit(solution)/shard_map/adam_moments/pallas_call | solution.py:227
  (65 shorter events, 21.0 us)
Async XLA Ops:
  3.6 16.3 %collective-permute-start = (bf16[128,512]{1,0:T(8,128)(2,1)S(1)}, bf16[128,512]{1,0:T(8,128)(2,1)S(1)}, u32[]{:S(2)}, u32[]{:S(2)}) collective-permute-start(bf16[128,512]{1,0:T(8,128)(2,1)S(1)} %get-tuple-element.94), channel_id=1, source_target_pairs={{0,2},{2,4},{4,6},{6,0},{1,3},{3,5},{5,7},{7,1},{8,10},{10,12},{12... | collective-permute-start | bytes 393224 | tf_op jit(solution)/shard_map/ppermute | solution.py:439
  6.7 13.2 %collective-permute-start.1 = (bf16[128,512]{1,0:T(8,128)(2,1)S(1)}, bf16[128,512]{1,0:T(8,128)(2,1)S(1)}, u32[]{:S(2)}, u32[]{:S(2)}) collective-permute-start(bf16[128,512]{1,0:T(8,128)(2,1)S(1)} %get-tuple-element.95), channel_id=1, source_target_pairs={{0,4},{2,6},{4,0},{6,2},{1,5},{3,7},{5,1},{7,3},{8,12},{10,14},{12... | collective-permute-start | bytes 393224 | tf_op jit(solution)/shard_map/ppermute | solution.py:439
  9.3 10.6 %collective-permute-start.2 = (bf16[128,512]{1,0:T(8,128)(2,1)S(1)}, bf16[128,512]{1,0:T(8,128)(2,1)S(1)}, u32[]{:S(2)}, u32[]{:S(2)}) collective-permute-start(bf16[128,512]{1,0:T(8,128)(2,1)S(1)} %get-tuple-element.96), channel_id=1, source_target_pairs={{0,6},{2,0},{4,2},{6,4},{1,7},{3,1},{5,3},{7,5},{8,14},{10,8},{12,... | collective-permute-start | bytes 393224 | tf_op jit(solution)/shard_map/ppermute | solution.py:439
  19.9 4.9 %collective-permute-start.5 = (bf16[3,128,512]{2,1,0:T(8,128)(2,1)S(1)}, bf16[3,128,512]{2,1,0:T(8,128)(2,1)S(1)}, u32[]{:S(2)}, u32[]{:S(2)}) collective-permute-start(bf16[3,128,512]{2,1,0:T(8,128)(2,1)S(1)} %pad_maximum_fusion.refs_0_), channel_id=1, source_target_pairs={{0,1},{1,0},{2,3},{3,2},{4,5},{5,4},{6,7},{7,6},{8,9},{9,8},{10,11... | collective-permute-start | bytes 1179656 | tf_op jit(solution)/shard_map/ppermute | solution.py:434
  20.0 17.2 %collective-permute-start.9 = (bf16[3,128,512]{2,1,0:T(8,128)(2,1)S(1)}, bf16[3,128,512]{2,1,0:T(8,128)(2,1)S(1)}, u32[]{:S(2)}, u32[]{:S(2)}) collective-permute-start(bf16[3,128,512]{2,1,0:T(8,128)(2,1)S(1)} %pad_maximum_fusion.refs_0_), channel_id=1, source_target_pairs={{0,16},{8,24},{16,0},{24,8},{1,17},{9,25},{17,1},{25,9},{2,18},{10... | collective-permute-start | bytes 1179656 | tf_op jit(solution)/shard_map/ppermute | solution.py:434
  21.6 15.6 %collective-permute-start.8 = (bf16[3,128,512]{2,1,0:T(8,128)(2,1)S(1)}, bf16[3,128,512]{2,1,0:T(8,128)(2,1)S(1)}, u32[]{:S(2)}, u32[]{:S(2)}) collective-permute-start(bf16[3,128,512]{2,1,0:T(8,128)(2,1)S(1)} %pad_maximum_fusion.refs_0_), channel_id=1, source_target_pairs={{0,8},{8,0},{16,24},{24,16},{1,9},{9,1},{17,25},{25,17},{2,10},{10... | collective-permute-start | bytes 1179656 | tf_op jit(solution)/shard_map/ppermute | solution.py:434
  23.1 19.3 %collective-permute-start.6 = (bf16[3,128,512]{2,1,0:T(8,128)(2,1)S(1)}, bf16[3,128,512]{2,1,0:T(8,128)(2,1)S(1)}, u32[]{:S(2)}, u32[]{:S(2)}) collective-permute-start(bf16[3,128,512]{2,1,0:T(8,128)(2,1)S(1)} %pad_maximum_fusion.refs_0_), channel_id=1, source_target_pairs={{0,24},{8,16},{16,8},{24,0},{1,25},{9,17},{17,9},{25,1},{2,26},{10... | collective-permute-start | bytes 1179656 | tf_op jit(solution)/shard_map/ppermute | solution.py:434
  23.6 9.2 %collective-permute-start.3 = (bf16[2,32,1024]{2,1,0:T(8,128)(2,1)S(1)}, bf16[2,32,1024]{2,1,0:T(8,128)(2,1)S(1)}, u32[]{:S(2)}, u32[]{:S(2)}) collective-permute-start(bf16[2,32,1024]{2,1,0:T(8,128)(2,1)S(1)} %get-tuple-element.103), channel_id=1, source_target_pairs={{0,2},{2,4},{4,6},{6,0},{1,3},{3,5},{5,7},{7,1},{8,10},{10,12},{12... | collective-permute-start | bytes 393224 | tf_op jit(solution)/shard_map/ppermute | solution.py:439
  24.9 7.9 %collective-permute-start.4 = (bf16[2,32,1024]{2,1,0:T(8,128)(2,1)S(1)}, bf16[2,32,1024]{2,1,0:T(8,128)(2,1)S(1)}, u32[]{:S(2)}, u32[]{:S(2)}) collective-permute-start(bf16[2,32,1024]{2,1,0:T(8,128)(2,1)S(1)} %get-tuple-element.105), channel_id=1, source_target_pairs={{0,6},{2,0},{4,2},{6,4},{1,7},{3,1},{5,3},{7,5},{8,14},{10,8},{12,... | collective-permute-start | bytes 393224 | tf_op jit(solution)/shard_map/ppermute | solution.py:439
  32.8 8.3 %collective-permute-start.7 = (bf16[2,32,1024]{2,1,0:T(8,128)(2,1)S(1)}, bf16[2,32,1024]{2,1,0:T(8,128)(2,1)S(1)}, u32[]{:S(2)}, u32[]{:S(2)}) collective-permute-start(bf16[2,32,1024]{2,1,0:T(8,128)(2,1)S(1)} %get-tuple-element.115), channel_id=1, source_target_pairs={{0,4},{2,6},{4,0},{6,2},{1,5},{3,7},{5,1},{7,3},{8,12},{10,14},{12... | collective-permute-start | bytes 393224 | tf_op jit(solution)/shard_map/ppermute | solution.py:439
  37.2 5.3 %collective-permute-start.10 = (bf16[3,128,512]{2,1,0:T(8,128)(2,1)S(1)}, bf16[3,128,512]{2,1,0:T(8,128)(2,1)S(1)}, u32[]{:S(2)}, u32[]{:S(2)}) collective-permute-start(bf16[3,128,512]{2,1,0:T(8,128)(2,1)S(1)} %collective-permute-done.8.refs_0_), channel_id=1, source_target_pairs={{0,1},{1,0},{2,3},{3,2},{4,5},{5,4},{6,7},{7,6},{8,9},{9,8},{10,11... | collective-permute-start | bytes 1179656 | tf_op jit(solution)/shard_map/ppermute | solution.py:434
  37.3 5.2 %collective-permute-start.11 = (bf16[3,128,512]{2,1,0:T(8,128)(2,1)S(1)}, bf16[3,128,512]{2,1,0:T(8,128)(2,1)S(1)}, u32[]{:S(2)}, u32[]{:S(2)}) collective-permute-start(bf16[3,128,512]{2,1,0:T(8,128)(2,1)S(1)} %collective-permute-done.9.refs_2_), channel_id=1, source_target_pairs={{0,1},{1,0},{2,3},{3,2},{4,5},{5,4},{6,7},{7,6},{8,9},{9,8},{10,11... | collective-permute-start | bytes 1179656 | tf_op jit(solution)/shard_map/ppermute | solution.py:434
  59.4 8.4 %collective-permute-start.17 = (bf16[256,512]{1,0:T(8,128)(2,1)S(1)}, bf16[256,512]{1,0:T(8,128)(2,1)S(1)}, u32[]{:S(2)}, u32[]{:S(2)}) collective-permute-start(bf16[256,512]{1,0:T(8,128)(2,1)S(1)} %get-tuple-element.149), channel_id=1, source_target_pairs={{0,8},{8,0},{16,24},{24,16},{1,9},{9,1},{17,25},{25,17},{2,10},{10... | collective-permute-start | bytes 786440 | tf_op jit(solution)/shard_map/ppermute | solution.py:434
  60.8 8.1 %collective-permute-start.18 = (bf16[256,512]{1,0:T(8,128)(2,1)S(1)}, bf16[256,512]{1,0:T(8,128)(2,1)S(1)}, u32[]{:S(2)}, u32[]{:S(2)}) collective-permute-start(bf16[256,512]{1,0:T(8,128)(2,1)S(1)} %get-tuple-element.150), channel_id=1, source_target_pairs={{0,16},{8,24},{16,0},{24,8},{1,17},{9,25},{17,1},{25,9},{2,18},{10... | collective-permute-start | bytes 786440 | tf_op jit(solution)/shard_map/ppermute | solution.py:434
  64.3 4.6 %collective-permute-start.21 = (bf16[256,512]{1,0:T(8,128)(2,1)S(1)}, bf16[256,512]{1,0:T(8,128)(2,1)S(1)}, u32[]{:S(2)}, u32[]{:S(2)}) collective-permute-start(bf16[256,512]{1,0:T(8,128)(2,1)S(1)} %get-tuple-element.155), channel_id=1, source_target_pairs={{0,1},{1,0},{2,3},{3,2},{4,5},{5,4},{6,7},{7,6},{8,9},{9,8},{10,11... | collective-permute-start | bytes 786440 | tf_op jit(solution)/shard_map/ppermute | solution.py:434
  64.3 4.6 %collective-permute-start.22 = (bf16[256,512]{1,0:T(8,128)(2,1)S(1)}, bf16[256,512]{1,0:T(8,128)(2,1)S(1)}, u32[]{:S(2)}, u32[]{:S(2)}) collective-permute-start(bf16[256,512]{1,0:T(8,128)(2,1)S(1)} %get-tuple-element.156), channel_id=1, source_target_pairs={{0,1},{1,0},{2,3},{3,2},{4,5},{5,4},{6,7},{7,6},{8,9},{9,8},{10,11... | collective-permute-start | bytes 786440 | tf_op jit(solution)/shard_map/ppermute | solution.py:434
  66.9 2.0 %collective-permute-start.19 = (bf16[256,512]{1,0:T(8,128)(2,1)S(1)}, bf16[256,512]{1,0:T(8,128)(2,1)S(1)}, u32[]{:S(2)}, u32[]{:S(2)}) collective-permute-start(bf16[256,512]{1,0:T(8,128)(2,1)S(1)} %get-tuple-element.152), channel_id=1, source_target_pairs={{0,1},{1,0},{2,3},{3,2},{4,5},{5,4},{6,7},{7,6},{8,9},{9,8},{10,11... | collective-permute-start | bytes 786440 | tf_op jit(solution)/shard_map/ppermute | solution.py:434
  69.5 14.0 %collective-permute-start.24 = (bf16[512,512]{1,0:T(8,128)(2,1)S(1)}, bf16[512,512]{1,0:T(8,128)(2,1)S(1)}, u32[]{:S(2)}, u32[]{:S(2)}) collective-permute-start(bf16[512,512]{1,0:T(8,128)(2,1)S(1)} %add_convert_fusion.1), channel_id=1, source_target_pairs={{0,16},{8,24},{16,0},{24,8},{1,17},{9,25},{17,1},{25,9},{2,18},{10... | collective-permute-start | bytes 1572872 | tf_op jit(solution)/shard_map/ppermute | solution.py:434
  71.2 13.8 %collective-permute-start.23 = (bf16[512,512]{1,0:T(8,128)(2,1)S(1)}, bf16[512,512]{1,0:T(8,128)(2,1)S(1)}, u32[]{:S(2)}, u32[]{:S(2)}) collective-permute-start(bf16[512,512]{1,0:T(8,128)(2,1)S(1)} %add_convert_fusion.2), channel_id=1, source_target_pairs={{0,8},{8,0},{16,24},{24,16},{1,9},{9,1},{17,25},{25,17},{2,10},{10... | collective-permute-start | bytes 1572872 | tf_op jit(solution)/shard_map/ppermute | solution.py:434
  74.6 8.1 %collective-permute-start.15 = (bf16[256,512]{1,0:T(8,128)(2,1)S(1)}, bf16[256,512]{1,0:T(8,128)(2,1)S(1)}, u32[]{:S(2)}, u32[]{:S(2)}) collective-permute-start(bf16[256,512]{1,0:T(8,128)(2,1)S(1)} %get-tuple-element.147), channel_id=1, source_target_pairs={{0,1},{1,0},{2,3},{3,2},{4,5},{5,4},{6,7},{7,6},{8,9},{9,8},{10,11... | collective-permute-start | bytes 786440 | tf_op jit(solution)/shard_map/ppermute | solution.py:434
  74.7 8.0 %collective-permute-start.16 = (bf16[256,512]{1,0:T(8,128)(2,1)S(1)}, bf16[256,512]{1,0:T(8,128)(2,1)S(1)}, u32[]{:S(2)}, u32[]{:S(2)}) collective-permute-start(bf16[256,512]{1,0:T(8,128)(2,1)S(1)} %get-tuple-element.148), channel_id=1, source_target_pairs={{0,1},{1,0},{2,3},{3,2},{4,5},{5,4},{6,7},{7,6},{8,9},{9,8},{10,11... | collective-permute-start | bytes 786440 | tf_op jit(solution)/shard_map/ppermute | solution.py:434
  85.3 11.8 %collective-permute-start.27 = (bf16[128,512]{1,0:T(8,128)(2,1)S(1)}, bf16[128,512]{1,0:T(8,128)(2,1)S(1)}, u32[]{:S(2)}, u32[]{:S(2)}) collective-permute-start(bf16[128,512]{1,0:T(8,128)(2,1)S(1)} %get-tuple-element.173), channel_id=1, source_target_pairs={{0,2},{2,4},{4,6},{6,0},{1,3},{3,5},{5,7},{7,1},{8,10},{10,12},{12... | collective-permute-start | bytes 393224 | tf_op jit(solution)/shard_map/ppermute | solution.py:439
  86.6 10.7 %collective-permute-start.26 = (bf16[128,512]{1,0:T(8,128)(2,1)S(1)}, bf16[128,512]{1,0:T(8,128)(2,1)S(1)}, u32[]{:S(2)}, u32[]{:S(2)}) collective-permute-start(bf16[128,512]{1,0:T(8,128)(2,1)S(1)} %get-tuple-element.174), channel_id=1, source_target_pairs={{0,4},{2,6},{4,0},{6,2},{1,5},{3,7},{5,1},{7,3},{8,12},{10,14},{12... | collective-permute-start | bytes 393224 | tf_op jit(solution)/shard_map/ppermute | solution.py:439
  87.5 9.8 %collective-permute-start.25 = (bf16[128,512]{1,0:T(8,128)(2,1)S(1)}, bf16[128,512]{1,0:T(8,128)(2,1)S(1)}, u32[]{:S(2)}, u32[]{:S(2)}) collective-permute-start(bf16[128,512]{1,0:T(8,128)(2,1)S(1)} %get-tuple-element.175), channel_id=1, source_target_pairs={{0,6},{2,0},{4,2},{6,4},{1,7},{3,1},{5,3},{7,5},{8,14},{10,8},{12,... | collective-permute-start | bytes 393224 | tf_op jit(solution)/shard_map/ppermute | solution.py:439
  (8 other events, 21.5 us)
